TPU v7x, 32 devices: a whole 2x2x4 slice. The times are simulated.
32 devices in a mesh: section: 2 (over core), vocab: 16 (over z, y, x).
Axes of the slice: x: 2, y: 2, z: 4, core: 2. Of those that a mesh axis runs over, the one named last changes fastest.
Arguments:
- hidden: bfloat16 [2, 512, 8192], P('section', None, 'vocab'), may hold values from -160 to 160
- final_hidden: bfloat16 [512, 8192], P('section', 'vocab'), may hold values from -160 to 160
- row_pick: int32 [2, 128], P('section'), may hold values from 0 to 511
- trans_weight: bfloat16 [2, 8192, 8192], P('section', None, 'vocab'), may hold values from -0.0625 to 0.0625
- trans_bias: bfloat16 [2, 8192], P('section', 'vocab'), may hold values from -6 to 6
- norm_gain: bfloat16 [8192], P('vocab'), may hold values from 0.5 to 1.5
- unembed: bfloat16 [8192, 8192], P('section', 'vocab'), may hold values from -100 to 100
Outputs:
- grad_weight: bfloat16 [2, 8192, 8192], P('section', None, 'vocab')
- grad_bias: float32 [2, 8192], P('section', 'vocab')
- kl_mean: float32 [2], P('section')
All inputs are finite; a program needn't handle non-finite values.
Results may differ from a plain program's by a relative error of at most 0.024.
Values may be sent and summed in bfloat16 or wider, within the bound.
No kernel may reach another device: no remote copies, remote signals or barrier semaphores. Data moves between devices by JAX's collectives and lax.ppermute only.
A program may use at most 64 MiB of HBM per device.

v0:
```python
import jax
import jax.numpy as jnp
from jax import lax
from jax.sharding import PartitionSpec as P

epsilon = 1e-05


def combined_all(value, axis, join):
    pieces = jax.tree.map(lambda part: lax.all_gather(part, axis), value)
    head = jax.tree.map(lambda part: part[0], pieces)
    tail = jax.tree.map(lambda part: part[1:], pieces)
    so_far, _ = lax.scan(lambda so_far, section: (join(so_far, section), None), head, tail)
    return so_far


def combine_totals(first, second):
    trans_max = jnp.maximum(first[0], second[0])
    trans_sum = first[1] * jnp.exp(first[0] - trans_max) + second[1] * jnp.exp(
        second[0] - trans_max
    )
    target_max = jnp.maximum(first[2], second[2])
    target_sum = first[3] * jnp.exp(first[2] - target_max) + second[3] * jnp.exp(
        second[2] - target_max
    )
    return (trans_max, trans_sum, target_max, target_sum)


def local_totals(logits):
    highest = jnp.max(logits, axis=-1)
    return (highest, jnp.sum(jnp.exp(logits - highest[:, None]), axis=-1))


def per_device(hidden, final_hidden, row_pick, trans_weight, trans_bias, norm_gain, unembed):
    gain_cols = norm_gain.astype(jnp.float32)
    width = trans_weight.shape[1]
    row_count = row_pick.shape[1]
    unembed_full = lax.all_gather(unembed, "section", axis=0, tiled=True)
    final_cols = lax.all_gather(final_hidden, "section", axis=0, tiled=True)
    picked = row_pick[0]
    input_cols = hidden[0][picked]
    inputs = lax.all_gather(input_cols, "vocab", axis=1, tiled=True)
    trans = (
        input_cols.astype(jnp.float32)
        + jnp.dot(inputs, trans_weight[0], preferred_element_type=jnp.float32)
        + trans_bias[0].astype(jnp.float32)
    )
    finals = final_cols[picked].astype(jnp.float32)
    trans_total, final_total = lax.psum(
        (jnp.sum(trans * trans, axis=-1), jnp.sum(finals * finals, axis=-1)), "vocab"
    )
    trans_scale = lax.rsqrt(trans_total / width + epsilon)
    final_scale = lax.rsqrt(final_total / width + epsilon)
    normed = (trans * trans_scale[:, None] * gain_cols).astype(jnp.bfloat16)
    target = (finals * final_scale[:, None] * gain_cols).astype(jnp.bfloat16)
    slab_rows = unembed_full
    logits = jnp.dot(
        lax.all_gather(normed, "vocab", axis=1, tiled=True),
        slab_rows,
        preferred_element_type=jnp.float32,
    )
    target_logits = jnp.dot(
        lax.all_gather(target, "vocab", axis=1, tiled=True),
        slab_rows,
        preferred_element_type=jnp.float32,
    )
    trans_max, trans_sum = local_totals(logits)
    target_max, target_sum = local_totals(target_logits)
    totals = combined_all((trans_max, trans_sum, target_max, target_sum), "vocab", combine_totals)
    log_trans = logits - (totals[0] + jnp.log(totals[1]))[:, None]
    log_target = target_logits - (totals[2] + jnp.log(totals[3]))[:, None]
    probs = jnp.exp(log_target)
    kl_part = jnp.sum(probs * (log_target - log_trans), axis=-1)
    dlogits = (jnp.exp(log_trans) - probs).astype(jnp.bfloat16)
    kl_rows, logit_dots = lax.psum(
        (kl_part, jnp.sum(dlogits.astype(jnp.float32) * logits, axis=-1)), "vocab"
    )
    slab_rows = unembed_full
    dnormed_cols = lax.psum_scatter(
        lax.dot_general(
            slab_rows, dlogits, (((1,), (1,)), ((), ())), preferred_element_type=jnp.float32
        ).astype(jnp.bfloat16),
        "vocab",
        scatter_dimension=0,
        tiled=True,
    ).astype(jnp.float32)
    trans_cols = trans.T
    scaled_cols = dnormed_cols * gain_cols[:, None]
    product = logit_dots / (width * trans_scale)
    dtrans_cols = trans_scale[None, :] * (
        scaled_cols - trans_cols * (trans_scale * trans_scale * product)[None, :]
    )
    grad_weights = [
        lax.dot_general(
            inputs,
            dtrans_cols.astype(jnp.bfloat16),
            (((0,), (1,)), ((), ())),
            preferred_element_type=jnp.float32,
        ).astype(jnp.bfloat16)
    ]
    grad_biases = [jnp.sum(dtrans_cols, axis=1)]
    kl_values = [jnp.sum(kl_rows) / row_count]
    return (jnp.stack(grad_weights), jnp.stack(grad_biases), jnp.stack(kl_values))


def solution(mesh):
    placed = (
        P("section", None, "vocab"),
        P("section", "vocab"),
        P("section", None),
        P("section", None, "vocab"),
        P("section", "vocab"),
        P("vocab"),
        P("section", "vocab"),
    )
    return jax.shard_map(
        per_device,
        mesh=mesh,
        in_specs=placed,
        out_specs=(P("section", None, "vocab"), P("section", "vocab"), P("section")),
        check_vma=False,
    )
```

profile of v0, /device:TPU:0, one launch (start us, length us, event | category | flops | bytes accessed | tf_op | source)
XLA Modules:
  0.0 460.6 jit_solution(4328733027532448367)
XLA Ops:
  7.2 0.7 fusion.30
  7.9 0.3 copy-done
  8.2 1.5 gather_fusion
  9.8 0.7 add.72
  10.5 0.7 convert_element_type.41
  11.2 2.5 all_gather.46
  13.6 0.8 gather_fusion.1
  14.5 0.1 fusion.20
  14.6 61.2 %all-gather.20.cloned.1.call-done = bf16[128,8192]{1,0:T(8,128)(2,1)} async-done(((bf16[128,512]{1,0:T(8,128)(2,1)}), bf16[128,8192]{1,0:T(8,128)(2,1)}) %all-gather.20.cloned.1.call-update) | async-done | bytes 2097168 | tf_op jit(solution)/shard_map/all_gather | solution.py:42
  75.8 5.3 %multiply_reduce_fusion.2 = (f32[128]{0:T(128)S(1)}, f32[128,512]{1,0:T(8,128)S(1)}) fusion(f32[512]{0:T(512)S(1)} %bitcast.94, bf16[128,8192]{1,0:T(8,128)(2,1)} %all-gather.20.cloned.1.call-done, bf16[1,8192,512]{2,1,0:T(8,128)(2,1)} %param.12, bf16[128,512]{1,0:T(8,128)(2,1)} %gather_fusion), kind=kOutput, calls=%fused_computation.37 | convolution fusion | flops 1074069376 | bytes 10881536 | tf_op jit(solution)/shard_map/dot_general | solution.py:45
  81.1 38.9 %all-reduce.1 = (f32[128]{0:T(128)S(1)}, f32[128]{0:T(128)S(1)}) all-reduce(f32[128]{0:T(128)S(1)} %fusion.20, f32[128]{0:T(128)S(1)} %get-tuple-element.89), channel_id=1, replica_groups=mesh['section'=2,'vocab'=16] {'vocab'}, use_global_device_ids=true, to_apply=%region_5.0 | all-reduce | flops 256 | bytes 2048 | tf_op jit(solution)/shard_map/psum | solution.py:49
  120.1 0.8 multiply_convert_fusion
  121.0 0.7 all-gather.16.cloned.1.call-update
  121.7 0.5 all-gather.18.cloned.1.call-update
  122.3 56.4 %all-gather.14.cloned.1.call-done = bf16[128,8192]{1,0:T(8,128)(2,1)} async-done(((bf16[128,512]{1,0:T(8,128)(2,1)}), bf16[128,8192]{1,0:T(8,128)(2,1)}) %all-gather.14.cloned.1.call-update) | async-done | bytes 2097168 | tf_op jit(solution)/shard_map/all_gather | solution.py:58
  178.7 19.6 %all-gather.16.cloned.1.call-done = bf16[8192,512]{1,0:T(8,128)(2,1)} async-done(((bf16[4096,512]{1,0:T(8,128)(2,1)}), bf16[8192,512]{1,0:T(8,128)(2,1)}) %all-gather.16.cloned.1.call-update) | async-done | bytes 8388624 | tf_op jit(solution)/shard_map/all_gather | solution.py:38
  198.3 5.4 %fusion.33 = (f32[128]{0:T(128)S(1)}, f32[128,512]{1,0:T(8,128)S(1)}) fusion(bf16[128,8192]{1,0:T(8,128)(2,1)} %all-gather.14.cloned.1.call-done, bf16[8192,512]{1,0:T(8,128)(2,1)} %all-gather.16.cloned.1.call-done), kind=kOutput, calls=%fused_computation.59 | convolution fusion | flops 1073807232 | bytes 10748416 | tf_op jit(solution)/shard_map/dot_general | solution.py:57
  203.7 40.8 %all-gather.5 = f32[16,1,128]{2,1,0:T(1,128)S(1)} all-gather(f32[1,1,128]{2,1,0:T(1,128)S(1)} %bitcast.96), channel_id=3, replica_groups=mesh['section'=2,'vocab'=16] {'vocab'}, dimensions={0}, use_global_device_ids=true | all-gather | bytes 8704 | tf_op jit(solution)/shard_map/all_gather | solution.py:10
  244.4 0.2 exponential_reduce_fusion.1
  244.6 35.4 %all-gather.6 = f32[16,1,128]{2,1,0:T(1,128)S(1)} all-gather(f32[1,1,128]{2,1,0:T(1,128)S(1)} %bitcast.98), channel_id=4, replica_groups=mesh['section'=2,'vocab'=16] {'vocab'}, dimensions={0}, use_global_device_ids=true | all-gather | bytes 8704 | tf_op jit(solution)/shard_map/all_gather | solution.py:10
  280.0 5.4 %fusion.34 = (f32[128]{0:T(128)S(1)}, f32[128,512]{1,0:T(8,128)S(1)}) fusion(bf16[128,8192]{1,0:T(8,128)(2,1)} %all-gather.18.cloned.1.call-done, bf16[8192,512]{1,0:T(8,128)(2,1)} %all-gather.16.cloned.1.call-done), kind=kOutput, calls=%fused_computation.60 | convolution fusion | flops 1073807232 | bytes 10748416 | tf_op jit(solution)/shard_map/dot_general | solution.py:62
  285.4 37.3 %all-gather.7 = f32[16,1,128]{2,1,0:T(1,128)S(1)} all-gather(f32[1,1,128]{2,1,0:T(1,128)S(1)} %bitcast.95), channel_id=5, replica_groups=mesh['section'=2,'vocab'=16] {'vocab'}, dimensions={0}, use_global_device_ids=true | all-gather | bytes 8704 | tf_op jit(solution)/shard_map/all_gather | solution.py:10
  322.7 0.2 exponential_reduce_fusion
  322.9 35.3 %all-gather.8 = f32[16,1,128]{2,1,0:T(1,128)S(1)} all-gather(f32[1,1,128]{2,1,0:T(1,128)S(1)} %bitcast.99), channel_id=6, replica_groups=mesh['section'=2,'vocab'=16] {'vocab'}, dimensions={0}, use_global_device_ids=true | all-gather | bytes 8704 | tf_op jit(solution)/shard_map/all_gather | solution.py:10
  358.2 0.7 while.16
  359.0 7.5 %fusion.11 = bf16[8192,128]{0,1:T(8,128)(2,1)} fusion(bf16[8192,512]{1,0:T(8,128)(2,1)} %all-gather.16.cloned.1.call-done, f32[128,512]{1,0:T(8,128)S(1)} %get-tuple-element.94, f32[128,512]{1,0:T(8,128)S(1)} %get-tuple-element.92, f32[128]{0:T(128)S(1)} %get-tuple-element.95, f32[128]{0:T(128)S(1)} %get-tuple-element.96), kind=kOutput, calls=%fused_computation.19 | convolution fusion | flops 1075052544 | bytes 11011072 | tf_op jit(solution)/shard_map/dot_general | solution.py:80
  366.5 0.3 multiply_reduce_fusion
  366.8 38.9 %all-reduce = (f32[128]{0:T(128)S(1)}, f32[128]{0:T(128)S(1)}) all-reduce(f32[128]{0:T(128)S(1)} %get-tuple-element.58, f32[128]{0:T(128)S(1)} %get-tuple-element.57), channel_id=1, replica_groups=mesh['section'=2,'vocab'=16] {'vocab'}, use_global_device_ids=true, to_apply=%region_12.13 | all-reduce | flops 256 | bytes 2048 | tf_op jit(solution)/shard_map/psum | solution.py:75
  405.7 0.6 reduce_sum.79
  407.0 38.5 %reduce-scatter.2.cloned.1.call-done = bf16[512,128]{0,1:T(8,128)(2,1)} async-done(((bf16[8192,128]{0,1:T(8,128)(2,1)}), bf16[512,128]{0,1:T(8,128)(2,1)}) %reduce-scatter.2.cloned.1.call-update) | async-done | bytes 131088 | tf_op jit(solution)/shard_map/reduce_scatter | solution.py:79
  445.5 6.8 %fusion.10 = bf16[1,8192,512]{2,1,0:T(8,128)(2,1)} fusion(bf16[128,8192]{1,0:T(8,128)(2,1)S(1)} %copy-done.1, f32[128,512]{1,0:T(8,128)S(1)} %get-tuple-element.90, bf16[512,128]{0,1:T(8,128)(2,1)} %reduce-scatter.2.cloned.1.call-done, f32[128]{0:T(128)S(1)} %divide_multiply_fusion, f32[512]{0:T(512)S(1)} %convert_element_type.41, f32[128]{0:T(128)S(1)} %add_rsqrt_fusion.1), kind=kOutput, calls=%fused_computation.17 | convolution fusion | flops 1078329344 | bytes 10882048 | tf_op jit(solution)/shard_map/dot_general | solution.py:94
  452.3 0.7 fusion.24
  (46 shorter events, 0.8 us)
Async XLA Ops:
  7.2 1.1 copy-start
  7.2 68.6 %all-gather.20.cloned.1.call-start = ((), (), s32[]{:S(2)}) async-start(), calls=%async_computation.5 | async-start | bytes 2228224 | tf_op jit(solution)/shard_map/all_gather | solution.py:42
  9.8 168.9 %all-gather.14.cloned.1.call-start = ((), (), s32[]{:S(2)}) async-start(), calls=%async_computation.1 | async-start | bytes 2228224 | tf_op jit(solution)/shard_map/all_gather | solution.py:58
  120.9 77.4 %all-gather.16.cloned.1.call-start = ((), (), s32[]{:S(2)}) async-start(), calls=%async_computation.2 | async-start | bytes 12582912 | tf_op jit(solution)/shard_map/all_gather | solution.py:38
  121.7 158.4 %all-gather.18.cloned.1.call-start = ((), (), s32[]{:S(2)}) async-start(), calls=%async_computation.3 | async-start | bytes 2228224 | tf_op jit(solution)/shard_map/all_gather | solution.py:63
  122.2 323.2 %reduce-scatter.2.cloned.1.call-start = ((), (), s32[]{:S(2)}) async-start(), calls=%async_computation.4 | async-start | bytes 2228224 | tf_op jit(solution)/shard_map/reduce_scatter | solution.py:79
  366.5 79.0 %copy-start.1 = (bf16[128,8192]{1,0:T(8,128)(2,1)S(1)}, bf16[128,8192]{1,0:T(8,128)(2,1)}, u32[]{:S(2)}) copy-start(bf16[128,8192]{1,0:T(8,128)(2,1)} %all-gather.20.cloned.1.call-done) | copy-start | bytes 6291460
  445.5 6.8 %copy-start.2 = (bf16[512,128]{0,1:T(8,128)(2,1)S(1)}, bf16[512,128]{0,1:T(8,128)(2,1)}, u32[]{:S(2)}) copy-start(bf16[512,128]{0,1:T(8,128)(2,1)} %reduce-scatter.2.cloned.1.call-done) | copy-start | bytes 393220
Sparse Core Ops, SparseCore 0:
  11.3 64.4 all-gather.19
  121.0 57.6 all-gather.13
  180.2 18.0 all-gather.15
  200.9 62.9 all-gather.17
  366.7 78.7 reduce-scatter.1
where the time goes:
time: 461 us
  blocking collectives  229 us (50%)
  waiting for transfers between devices  177 us (38%)
  matrix products  30.4 us (7%)
  between operations  15.6 us (3%)
  other arithmetic  5.48 us (1%)
    all_gather x4, blocking collectives, combined_all(): pieces = jax.tree.map(lambda part: lax.all_gather(part, axis), value)  149 us
    all_gather x1, waiting for transfers between devices, per_device(): inputs = lax.all_gather(input_cols, 'vocab', axis=1, tiled=True)  61.2 us
    all_gather x1, waiting for transfers between devices, per_device(): lax.all_gather(normed, 'vocab', axis=1, tiled=True)  56.4 us
    psum x1, blocking collectives, per_device(): lax.psum((jnp.sum(trans * trans, axis=-1), jnp.sum(finals * finals, axis=...  38.9 us
    psum x1, blocking collectives, per_device(): lax.psum((kl_part, jnp.sum(dlogits.astype(jnp.float32) * logits, axis=-1)...  38.9 us
    reduce_scatter x1, waiting for transfers between devices, per_device(): lax.psum_scatter(lax.dot_general(slab_rows, dlogits, (((1,), (1,)), ((),...  38.5 us
    all_gather x1, waiting for transfers between devices, per_device(): unembed_full = lax.all_gather(unembed, 'section', axis=0, tiled=True)  19.6 us
  transfers between devices with their start and end apart: 5, of which 4 were waited for; matrix products, arithmetic and copies ran while one was open for 2% of the time, Pallas kernels for 0%

commit v1 on v0

v1 whole, which is shorter than its diff:
```python
import jax
import jax.numpy as jnp
from jax import lax
from jax.sharding import PartitionSpec as P

epsilon = 1e-05
f32 = jnp.float32
bf16 = jnp.bfloat16


def swap(value, offset, count):
    return lax.ppermute(value, "vocab", [(i, i ^ offset) for i in range(count)])


def gather_pieces(own, count):
    pieces = {0: own}
    outer = range(4, count, 4)
    for k in outer:
        pieces[k] = swap(own, k, count)
    for number, base in enumerate(range(0, count, 4)):
        pieces[base + 1] = swap(pieces[base], 1, count)
        pieces[base + 2] = swap(pieces[base], 2, count)
        if number % 2:
            pieces[base + 3] = swap(pieces[base + 2], 1, count)
        else:
            pieces[base + 3] = swap(pieces[base + 1], 2, count)
    return pieces


def arrival_order(count):
    order = [0, 4, 1, 2, 5, 6, 3, 7] if count > 4 else [0, 1, 2, 3]
    for base in range(8, count, 8):
        order += [base, base + 4, base + 1, base + 2, base + 5, base + 6, base + 3, base + 7]
    return order


def total(*parts):
    result = parts[0].astype(f32)
    for part in parts[1:]:
        result = result + part.astype(f32)
    return result


def scatter_sum(block_of, count):
    bases = list(range(0, count, 4))[::-1]
    blocks = {}
    for base in bases:
        far = block_of(base + 3)
        if (base // 4) % 2:
            blocks[base + 1] = block_of(base + 1)
            blocks[base + 2] = total(block_of(base + 2), swap(far, 1, count)).astype(bf16)
        else:
            blocks[base + 2] = block_of(base + 2)
            blocks[base + 1] = total(block_of(base + 1), swap(far, 2, count)).astype(bf16)
    result = None
    for base in bases:
        near = total(block_of(base), swap(blocks[base + 1], 1, count), swap(blocks[base + 2], 2, count))
        if base:
            near = swap(near.astype(bf16), base, count)
        result = near if result is None else total(result, near)
    return result


def split_words(value):
    high = lax.reduce_precision(value, 8, 7)
    rest = value - high
    middle = lax.reduce_precision(rest, 8, 7)
    return jnp.stack([high, middle, rest - middle]).astype(bf16)


def with_squares(rows, squares):
    words = split_words(squares)
    extra = jnp.zeros((8, rows.shape[1]), bf16).at[:3, : squares.shape[0]].set(words)
    return jnp.concatenate([rows, extra], axis=0)


def squares_of(pieces, row_count):
    return sum(jnp.sum(piece[row_count : row_count + 3, :row_count].astype(f32), axis=0) for piece in pieces)


def gather_stats(stats, count):
    parts = jnp.stack([stats] + [swap(stats, k, count) for k in range(4, count, 4)])
    return jnp.concatenate([parts] + [swap(parts, k, count) for k in (1, 2, 3)])


def per_device(hidden, final_hidden, row_pick, trans_weight, trans_bias, norm_gain, unembed):
    count = lax.axis_size("vocab")
    sections = lax.axis_size("section")
    me = lax.axis_index("vocab")
    section = lax.axis_index("section")
    gain = norm_gain.astype(f32)
    width = trans_weight.shape[1]
    cols = trans_weight.shape[2]
    row_count = row_pick.shape[1]
    picked = row_pick[0]

    own_inputs = hidden[0][picked]
    inputs = gather_pieces(own_inputs, count)

    unembed_all = jnp.concatenate(
        [unembed]
        + [
            lax.ppermute(unembed, "section", [((i + k) % sections, i) for i in range(sections)])
            for k in range(1, sections)
        ],
        axis=0,
    )

    def unembed_block(index):
        start = lax.rem(index * cols + width - section * unembed.shape[0], width)
        return lax.dynamic_slice_in_dim(unembed_all, start, cols, axis=0)

    final_all = lax.all_gather(final_hidden, "section", axis=0, tiled=True)
    finals = final_all[picked].astype(f32)
    target_own = with_squares((finals * gain).astype(bf16), jnp.sum(finals * finals, axis=-1))
    targets = lax.all_gather(target_own, "vocab", axis=0)

    trans = own_inputs.astype(f32) + trans_bias[0].astype(f32)
    for k in arrival_order(count):
        weight = lax.dynamic_slice_in_dim(trans_weight[0], (me ^ k) * cols, cols, axis=0)
        trans = trans + jnp.dot(inputs[k], weight, preferred_element_type=f32)
    trans_own = with_squares((trans * gain).astype(bf16), jnp.sum(trans * trans, axis=-1))
    normed = gather_pieces(trans_own, count)

    target_logits = 0.0
    for k in range(count):
        target_logits = target_logits + jnp.dot(targets[k], unembed_block(k), preferred_element_type=f32)
    final_squares = squares_of([targets[k] for k in range(count)], row_count)
    final_scale = lax.rsqrt(final_squares / width + epsilon)
    target_logits = target_logits[:row_count] * final_scale[:, None]

    logits = 0.0
    for k in arrival_order(count):
        logits = logits + jnp.dot(normed[k], unembed_block(me ^ k), preferred_element_type=f32)
    trans_squares = squares_of([normed[k] for k in range(count)], row_count)
    trans_scale = lax.rsqrt(trans_squares / width + epsilon)
    logits = logits[:row_count] * trans_scale[:, None]

    trans_max = jnp.max(logits, axis=-1)
    target_max = jnp.max(target_logits, axis=-1)
    shifted = logits - trans_max[:, None]
    trans_exp = jnp.exp(shifted)
    target_exp = jnp.exp(target_logits - target_max[:, None])
    stats = jnp.stack(
        [
            trans_max,
            jnp.sum(trans_exp, axis=-1),
            jnp.sum(trans_exp * shifted, axis=-1),
            target_max,
            jnp.sum(target_exp, axis=-1),
            jnp.sum(target_exp * (target_logits - logits), axis=-1),
            jnp.sum(target_exp * shifted, axis=-1),
            jnp.zeros_like(trans_max),
        ]
    )
    every = gather_stats(stats, count)
    top = jnp.max(every[:, 0], axis=0)
    target_top = jnp.max(every[:, 3], axis=0)
    drop = every[:, 0] - top
    factor = jnp.exp(drop)
    target_factor = jnp.exp(every[:, 3] - target_top)
    trans_sum = jnp.sum(factor * every[:, 1], axis=0)
    target_sum = jnp.sum(target_factor * every[:, 4], axis=0)
    log_sum = top + jnp.log(trans_sum)
    target_log_sum = target_top + jnp.log(target_sum)
    kl_rows = jnp.sum(target_factor * every[:, 5], axis=0) / target_sum - (target_log_sum - log_sum)
    logit_dots = (
        jnp.sum(factor * (every[:, 2] + every[:, 1] * drop), axis=0) / trans_sum
        - jnp.sum(target_factor * (every[:, 6] + every[:, 4] * drop), axis=0) / target_sum
    )

    dlogits = (
        jnp.exp(logits - log_sum[:, None]) - jnp.exp(target_logits - target_log_sum[:, None])
    ).astype(bf16)

    def dnormed_block(k):
        return lax.dot_general(
            dlogits, unembed_block(me ^ k), (((1,), (1,)), ((), ())), preferred_element_type=f32
        ).astype(bf16)

    dnormed = scatter_sum(dnormed_block, count)
    product = logit_dots / (width * trans_scale)
    dtrans = trans_scale[:, None] * (
        dnormed * gain - trans * (trans_scale * trans_scale * product)[:, None]
    )

    inputs_all = jnp.zeros((row_count, width), bf16)
    for k in arrival_order(count):
        inputs_all = lax.dynamic_update_slice_in_dim(inputs_all, inputs[k], (me ^ k) * cols, axis=1)
    grad_weight = lax.dot_general(
        inputs_all, dtrans.astype(bf16), (((0,), (0,)), ((), ())), preferred_element_type=f32
    ).astype(bf16)
    grad_bias = jnp.sum(dtrans, axis=0)
    kl_mean = jnp.sum(kl_rows) / row_count
    return grad_weight[None], grad_bias[None], kl_mean[None]


def solution(mesh):
    placed = (
        P("section", None, "vocab"),
        P("section", "vocab"),
        P("section", None),
        P("section", None, "vocab"),
        P("section", "vocab"),
        P("vocab"),
        P("section", "vocab"),
    )
    return jax.shard_map(
        per_device,
        mesh=mesh,
        in_specs=placed,
        out_specs=(P("section", None, "vocab"), P("section", "vocab"), P("section")),
        check_vma=False,
    )
```

time: 461 us -> 244 us (0.53)
  blocking collectives: 229 us -> 2.38 us
  waiting for transfers between devices: 177 us -> 34.9 us
  starting transfers between devices: 0.2 us -> 66 us
  matrix products: 30.4 us -> 93.3 us
  local copies, waits for them, and re-layouts: 2.67 us -> 19.6 us
    all_gather x5 -> x1, blocking collectives: 151 us -> 2.38 us  [per_device(): final_all = lax.all_gather(final_hidden, 'section', axis=0, tiled=True)]
    all_gather x4 -> x1, waiting for transfers between devices: 137 us -> 8.94 us  [per_device(): targets = lax.all_gather(target_own, 'vocab', axis=0)]
    psum x2 -> x0, blocking collectives: 77.8 us -> none  [the longest x1 38.9 us: per_device(): lax.psum((jnp.sum(trans * trans, axis=-1), jnp.sum(finals * finals, axis=...]
    ppermute x0 -> x52, starting transfers between devices: none -> 65.9 us  [the longest x51 65.7 us: swap(): return lax.ppermute(value, 'vocab', [(i, i ^ offset) for i in range(count)])]
    dot_general x5 -> x65, matrix products: 30.4 us -> 93.3 us  [the longest x16 24.3 us: dnormed_block(): lax.dot_general(dlogits, unembed_block(me ^ k), (((1,), (1,)), ((), ())),...]
    reduce_scatter x1 -> x0, waiting for transfers between devices: 38.5 us -> none  [per_device(): lax.psum_scatter(lax.dot_general(slab_rows, dlogits, (((1,), (1,)), ((),...]
    ppermute x0 -> x52, waiting for transfers between devices: none -> 25.9 us  [the longest x51 25.9 us: swap(): return lax.ppermute(value, 'vocab', [(i, i ^ offset) for i in range(count)])]
    dynamic_update_slice x0 -> x16, local copies, waits for them, and re-layouts: none -> 8.39 us  [per_device(): lax.dynamic_update_slice_in_dim(inputs_all, inputs[k], (me ^ k) * cols, a...]
  transfers between devices with their start and end apart: 5 -> 53, of which waited for: 4 -> 19; matrix products, arithmetic and copies ran while one was open for 2% -> 32% of each run, Pallas kernels for 0% -> 0%
where the time goes in v1:
time: 244 us; the launch traced here: 241 us
  matrix products  93.3 us (38%)
  starting transfers between devices  66 us (27%)
  waiting for transfers between devices  34.9 us (14%)
  local copies, waits for them, and re-layouts  19.6 us (8%)
  between operations  17.2 us (7%)
  other arithmetic  8.11 us (3%)
    ppermute x51, starting transfers between devices, swap(): return lax.ppermute(value, 'vocab', [(i, i ^ offset) for i in range(count)])  65.7 us
    ppermute x51, waiting for transfers between devices, swap(): return lax.ppermute(value, 'vocab', [(i, i ^ offset) for i in range(count)])  25.9 us
    dot_general x16, matrix products, dnormed_block(): lax.dot_general(dlogits, unembed_block(me ^ k), (((1,), (1,)), ((), ())),...  24.3 us
    dot_general x16, matrix products, per_device(): jnp.dot(targets[k], unembed_block(k), preferred_element_type=f32)  21.7 us
    dot_general x16, matrix products, per_device(): trans = trans + jnp.dot(inputs[k], weight, preferred_element_type=f32)  20.8 us
    dot_general x16, matrix products, per_device(): jnp.dot(normed[k], unembed_block(me ^ k), preferred_element_type=f32)  20.7 us
    all_gather x1, waiting for transfers between devices, per_device(): targets = lax.all_gather(target_own, 'vocab', axis=0)  8.94 us
    dynamic_update_slice x16, local copies, waits for them, and re-layouts, per_device(): lax.dynamic_update_slice_in_dim(inputs_all, inputs[k], (me ^ k) * cols, a...  8.39 us
  transfers between devices with their start and end apart: 53, of which 19 were waited for; matrix products, arithmetic and copies ran while one was open for 32% of the time, Pallas kernels for 0%

profile of v1, /device:TPU:0, one launch (start us, length us, event | category | flops | bytes accessed | tf_op | source)
XLA Modules:
  0.0 241.4 jit_solution(14335708066127468895)
XLA Ops:
  9.1 3.1 %collective-permute-start = (bf16[128,512]{1,0:T(8,128)(2,1)S(1)}, bf16[128,512]{1,0:T(8,128)(2,1)S(1)}, u32[]{:S(2)}, u32[]{:S(2)}) collective-permute-start(bf16[128,512]{1,0:T(8,128)(2,1)S(1)} %gather_fusion), channel_id=1, source_target_pairs={{0,4},{1,5},{2,6},{3,7},{4,0},{5,1},{6,2},{7,3},{8,12},{9,13},{10,... | collective-permute-start | bytes 393224 | tf_op jit(solution)/shard_map/ppermute | solution.py:12
  15.2 2.6 %collective-permute-start.7 = (bf16[128,512]{1,0:T(8,128)(2,1)S(1)}, bf16[128,512]{1,0:T(8,128)(2,1)S(1)}, u32[]{:S(2)}, u32[]{:S(2)}) collective-permute-start(bf16[128,512]{1,0:T(8,128)(2,1)S(1)} %gather_fusion), channel_id=1, source_target_pairs={{0,8},{1,9},{2,10},{3,11},{4,12},{5,13},{6,14},{7,15},{8,0},{9,1},... | collective-permute-start | bytes 393224 | tf_op jit(solution)/shard_map/ppermute | solution.py:12
  18.0 2.4 all_gather.9
  21.1 4.5 %constant_dynamic-update-slice_fusion.1 = bf16[8192,512]{1,0:T(8,128)(2,1)} fusion(bf16[4096,512]{1,0:T(8,128)(2,1)} %param.17), kind=kLoop, calls=%fused_computation.250 | loop fusion | bytes 8388608
  32.2 1.8 collective-permute-start.5
  44.4 2.2 collective-permute-done.11
  51.3 3.1 %collective-permute-done.10 = bf16[128,512]{1,0:T(8,128)(2,1)S(1)} collective-permute-done((bf16[128,512]{1,0:T(8,128)(2,1)S(1)}, bf16[128,512]{1,0:T(8,128)(2,1)S(1)}, u32[]{:S(2)}, u32[]{:S(2)}) %collective-permute-start.10) | collective-permute-done | bytes 131104 | tf_op jit(solution)/shard_map/ppermute | solution.py:12
  67.2 3.6 %collective-permute-start.26 = (bf16[136,512]{1,0:T(8,128)(2,1)}, bf16[136,512]{1,0:T(8,128)(2,1)}, u32[]{:S(2)}, u32[]{:S(2)}) collective-permute-start(bf16[136,512]{1,0:T(8,128)(2,1)} %fusion.177), channel_id=1, source_target_pairs={{0,12},{1,13},{2,14},{3,15},{4,8},{5,9},{6,10},{7,11},{8,4},{9,5},... | collective-permute-start | bytes 417800 | tf_op jit(solution)/shard_map/ppermute | solution.py:12
  84.7 2.4 %collective-permute-start.24 = (bf16[136,512]{1,0:T(8,128)(2,1)}, bf16[136,512]{1,0:T(8,128)(2,1)S(1)}, u32[]{:S(2)}, u32[]{:S(2)}) collective-permute-start(bf16[136,512]{1,0:T(8,128)(2,1)} %collective-permute-done.22), channel_id=1, source_target_pairs={{0,2},{1,3},{2,0},{3,1},{4,6},{5,7},{6,4},{7,5},{8,10},{9,11},{10,... | collective-permute-start | bytes 417800 | tf_op jit(solution)/shard_map/ppermute | solution.py:12
  88.5 2.6 %collective-permute-start.19 = (bf16[136,512]{1,0:T(8,128)(2,1)}, bf16[136,512]{1,0:T(8,128)(2,1)S(1)}, u32[]{:S(2)}, u32[]{:S(2)}) collective-permute-start(bf16[136,512]{1,0:T(8,128)(2,1)} %collective-permute-done.18), channel_id=1, source_target_pairs={{0,1},{1,0},{2,3},{3,2},{4,5},{5,4},{6,7},{7,6},{8,9},{9,8},{10,11... | collective-permute-start | bytes 417800 | tf_op jit(solution)/shard_map/ppermute | solution.py:12
  91.3 2.4 collective-permute-start.17
  94.6 2.0 collective-permute-start.25
  99.7 2.1 collective-permute-done.21
  101.9 4.5 %constant_dynamic-update-slice_fusion = bf16[8192,512]{1,0:T(8,128)(2,1)} fusion(bf16[8192,512]{1,0:T(8,128)(2,1)} %constant_dynamic-update-slice_fusion.1, bf16[4096,512]{1,0:T(8,128)(2,1)} %collective-permute-done.30), kind=kLoop, calls=%fused_computation.249 | loop fusion | bytes 8388608 | tf_op jit(solution)/shard_map/concatenate | solution.py:100
  127.4 8.9 %all-gather.3.cloned.1.call-done = bf16[2176,512]{1,0:T(8,128)(2,1)} async-done(((bf16[136,512]{1,0:T(8,128)(2,1)}), bf16[2176,512]{1,0:T(8,128)(2,1)}) %all-gather.3.cloned.1.call-update) | async-done | bytes 2228240 | tf_op jit(solution)/shard_map/all_gather | solution.py:116
  161.8 2.2 collective-permute-start.33
  165.6 1.7 collective-permute-done.33
  167.2 1.6 collective-permute-start.34
  174.8 2.0 convolution_convert_fusion.1
  184.9 1.6 collective-permute-start.51
  198.6 2.2 collective-permute-start.37
  203.7 1.9 collective-permute-start.50
  205.6 1.7 collective-permute-done.47
  209.1 1.6 collective-permute-start.39
  210.7 1.6 collective-permute-done.42
  212.4 2.0 fusion.50
  214.4 2.2 collective-permute-start.44
  216.6 2.0 fusion.49
  218.6 2.1 collective-permute-start.40
  223.3 2.3 collective-permute-done.40
  225.6 2.1 fusion.279
  227.7 5.8 %fusion = bf16[1,8192,512]{2,1,0:T(8,128)(2,1)} fusion(bf16[128,8192]{1,0:T(8,128)(2,1)S(1)} %constant_dynamic-update-slice_fusion.9, bf16[128,512]{1,0:T(8,128)(2,1)S(1)} %get-tuple-element.86), kind=kOutput, calls=%fused_computation.3 | convolution fusion | flops 1077936128 | bytes 10616832 | tf_op jit(solution)/shard_map/dot_general | solution.py:190
  (227 shorter events, 139.3 us)
Async XLA Ops:
  7.2 129.1 %all-gather.3.cloned.1.call-start = ((), (), s32[]{:S(2)}) async-start(), calls=%async_computation | async-start | bytes 2367488 | tf_op jit(solution)/shard_map/all_gather | solution.py:116
  9.1 19.3 %collective-permute-start = (bf16[128,512]{1,0:T(8,128)(2,1)S(1)}, bf16[128,512]{1,0:T(8,128)(2,1)S(1)}, u32[]{:S(2)}, u32[]{:S(2)}) collective-permute-start(bf16[128,512]{1,0:T(8,128)(2,1)S(1)} %gather_fusion), channel_id=1, source_target_pairs={{0,4},{1,5},{2,6},{3,7},{4,0},{5,1},{6,2},{7,3},{8,12},{9,13},{10,... | collective-permute-start | bytes 393224 | tf_op jit(solution)/shard_map/ppermute | solution.py:12
  12.2 18.3 %collective-permute-start.1 = (bf16[128,512]{1,0:T(8,128)(2,1)S(1)}, bf16[128,512]{1,0:T(8,128)(2,1)}, u32[]{:S(2)}, u32[]{:S(2)}) collective-permute-start(bf16[128,512]{1,0:T(8,128)(2,1)S(1)} %gather_fusion), channel_id=1, source_target_pairs={{0,1},{1,0},{2,3},{3,2},{4,5},{5,4},{6,7},{7,6},{8,9},{9,8},{10,11... | collective-permute-start | bytes 393224 | tf_op jit(solution)/shard_map/ppermute | solution.py:12
  13.7 21.6 %collective-permute-start.2 = (bf16[128,512]{1,0:T(8,128)(2,1)S(1)}, bf16[128,512]{1,0:T(8,128)(2,1)}, u32[]{:S(2)}, u32[]{:S(2)}) collective-permute-start(bf16[128,512]{1,0:T(8,128)(2,1)S(1)} %gather_fusion), channel_id=1, source_target_pairs={{0,2},{1,3},{2,0},{3,1},{4,6},{5,7},{6,4},{7,5},{8,10},{9,11},{10,... | collective-permute-start | bytes 393224 | tf_op jit(solution)/shard_map/ppermute | solution.py:12
  15.2 17.0 %collective-permute-start.7 = (bf16[128,512]{1,0:T(8,128)(2,1)S(1)}, bf16[128,512]{1,0:T(8,128)(2,1)S(1)}, u32[]{:S(2)}, u32[]{:S(2)}) collective-permute-start(bf16[128,512]{1,0:T(8,128)(2,1)S(1)} %gather_fusion), channel_id=1, source_target_pairs={{0,8},{1,9},{2,10},{3,11},{4,12},{5,13},{6,14},{7,15},{8,0},{9,1},... | collective-permute-start | bytes 393224 | tf_op jit(solution)/shard_map/ppermute | solution.py:12
  17.8 10.9 %collective-permute-start.8 = (bf16[128,512]{1,0:T(8,128)(2,1)S(1)}, bf16[128,512]{1,0:T(8,128)(2,1)S(1)}, u32[]{:S(2)}, u32[]{:S(2)}) collective-permute-start(bf16[128,512]{1,0:T(8,128)(2,1)S(1)} %gather_fusion), channel_id=1, source_target_pairs={{0,12},{1,13},{2,14},{3,15},{4,8},{5,9},{6,10},{7,11},{8,4},{9,5},... | collective-permute-start | bytes 393224 | tf_op jit(solution)/shard_map/ppermute | solution.py:12
  28.4 73.4 %collective-permute-start.30 = (bf16[4096,512]{1,0:T(8,128)(2,1)}, bf16[4096,512]{1,0:T(8,128)(2,1)}, u32[]{:S(2)}, u32[]{:S(2)}) collective-permute-start(bf16[4096,512]{1,0:T(8,128)(2,1)} %param.17), channel_id=1, source_target_pairs={{16,0},{0,16},{17,1},{1,17},{18,2},{2,18},{19,3},{3,19},{20,4},{4,... | collective-permute-start | bytes 12582920 | tf_op jit(solution)/shard_map/ppermute | solution.py:103
  28.6 31.0 %collective-permute-start.3 = (bf16[128,512]{1,0:T(8,128)(2,1)S(1)}, bf16[128,512]{1,0:T(8,128)(2,1)S(1)}, u32[]{:S(2)}, u32[]{:S(2)}) collective-permute-start(bf16[128,512]{1,0:T(8,128)(2,1)S(1)} %collective-permute-done), channel_id=1, source_target_pairs={{0,1},{1,0},{2,3},{3,2},{4,5},{5,4},{6,7},{7,6},{8,9},{9,8},{10,11... | collective-permute-start | bytes 393224 | tf_op jit(solution)/shard_map/ppermute | solution.py:12
  30.5 18.9 %collective-permute-start.4 = (bf16[128,512]{1,0:T(8,128)(2,1)S(1)}, bf16[128,512]{1,0:T(8,128)(2,1)S(1)}, u32[]{:S(2)}, u32[]{:S(2)}) collective-permute-start(bf16[128,512]{1,0:T(8,128)(2,1)S(1)} %collective-permute-done), channel_id=1, source_target_pairs={{0,2},{1,3},{2,0},{3,1},{4,6},{5,7},{6,4},{7,5},{8,10},{9,11},{10,... | collective-permute-start | bytes 393224 | tf_op jit(solution)/shard_map/ppermute | solution.py:12
  32.2 24.1 %collective-permute-start.5 = (bf16[128,512]{1,0:T(8,128)(2,1)}, bf16[128,512]{1,0:T(8,128)(2,1)S(1)}, u32[]{:S(2)}, u32[]{:S(2)}) collective-permute-start(bf16[128,512]{1,0:T(8,128)(2,1)} %collective-permute-done.1), channel_id=1, source_target_pairs={{0,2},{1,3},{2,0},{3,1},{4,6},{5,7},{6,4},{7,5},{8,10},{9,11},{10,... | collective-permute-start | bytes 393224 | tf_op jit(solution)/shard_map/ppermute | solution.py:12
  46.6 11.2 %collective-permute-start.9 = (bf16[128,512]{1,0:T(8,128)(2,1)S(1)}, bf16[128,512]{1,0:T(8,128)(2,1)S(1)}, u32[]{:S(2)}, u32[]{:S(2)}) collective-permute-start(bf16[128,512]{1,0:T(8,128)(2,1)S(1)} %collective-permute-done.7), channel_id=1, source_target_pairs={{0,1},{1,0},{2,3},{3,2},{4,5},{5,4},{6,7},{7,6},{8,9},{9,8},{10,11... | collective-permute-start | bytes 393224 | tf_op jit(solution)/shard_map/ppermute | solution.py:12
  56.2 7.4 %collective-permute-start.14 = (bf16[128,512]{1,0:T(8,128)(2,1)S(1)}, bf16[128,512]{1,0:T(8,128)(2,1)S(1)}, u32[]{:S(2)}, u32[]{:S(2)}) collective-permute-start(bf16[128,512]{1,0:T(8,128)(2,1)S(1)} %collective-permute-done.12), channel_id=1, source_target_pairs={{0,1},{1,0},{2,3},{3,2},{4,5},{5,4},{6,7},{7,6},{8,9},{9,8},{10,11... | collective-permute-start | bytes 393224 | tf_op jit(solution)/shard_map/ppermute | solution.py:12
  57.8 7.2 %collective-permute-start.13 = (bf16[128,512]{1,0:T(8,128)(2,1)S(1)}, bf16[128,512]{1,0:T(8,128)(2,1)S(1)}, u32[]{:S(2)}, u32[]{:S(2)}) collective-permute-start(bf16[128,512]{1,0:T(8,128)(2,1)S(1)} %collective-permute-done.9), channel_id=1, source_target_pairs={{0,2},{1,3},{2,0},{3,1},{4,6},{5,7},{6,4},{7,5},{8,10},{9,11},{10,... | collective-permute-start | bytes 393224 | tf_op jit(solution)/shard_map/ppermute | solution.py:12
  67.2 10.3 %collective-permute-start.26 = (bf16[136,512]{1,0:T(8,128)(2,1)}, bf16[136,512]{1,0:T(8,128)(2,1)}, u32[]{:S(2)}, u32[]{:S(2)}) collective-permute-start(bf16[136,512]{1,0:T(8,128)(2,1)} %fusion.177), channel_id=1, source_target_pairs={{0,12},{1,13},{2,14},{3,15},{4,8},{5,9},{6,10},{7,11},{8,4},{9,5},... | collective-permute-start | bytes 417800 | tf_op jit(solution)/shard_map/ppermute | solution.py:12
  70.8 8.9 %collective-permute-start.22 = (bf16[136,512]{1,0:T(8,128)(2,1)}, bf16[136,512]{1,0:T(8,128)(2,1)}, u32[]{:S(2)}, u32[]{:S(2)}) collective-permute-start(bf16[136,512]{1,0:T(8,128)(2,1)} %fusion.177), channel_id=1, source_target_pairs={{0,8},{1,9},{2,10},{3,11},{4,12},{5,13},{6,14},{7,15},{8,0},{9,1},... | collective-permute-start | bytes 417800 | tf_op jit(solution)/shard_map/ppermute | solution.py:12
  70.8 10.2 %collective-permute-start.18 = (bf16[136,512]{1,0:T(8,128)(2,1)}, bf16[136,512]{1,0:T(8,128)(2,1)}, u32[]{:S(2)}, u32[]{:S(2)}) collective-permute-start(bf16[136,512]{1,0:T(8,128)(2,1)} %fusion.177), channel_id=1, source_target_pairs={{0,4},{1,5},{2,6},{3,7},{4,0},{5,1},{6,2},{7,3},{8,12},{9,13},{10,... | collective-permute-start | bytes 417800 | tf_op jit(solution)/shard_map/ppermute | solution.py:12
  71.6 13.1 %collective-permute-start.15 = (bf16[136,512]{1,0:T(8,128)(2,1)}, bf16[136,512]{1,0:T(8,128)(2,1)}, u32[]{:S(2)}, u32[]{:S(2)}) collective-permute-start(bf16[136,512]{1,0:T(8,128)(2,1)} %fusion.177), channel_id=1, source_target_pairs={{0,1},{1,0},{2,3},{3,2},{4,5},{5,4},{6,7},{7,6},{8,9},{9,8},{10,11... | collective-permute-start | bytes 417800 | tf_op jit(solution)/shard_map/ppermute | solution.py:12
  79.7 8.1 %collective-permute-start.28 = (bf16[136,512]{1,0:T(8,128)(2,1)}, bf16[136,512]{1,0:T(8,128)(2,1)S(1)}, u32[]{:S(2)}, u32[]{:S(2)}) collective-permute-start(bf16[136,512]{1,0:T(8,128)(2,1)} %collective-permute-done.26), channel_id=1, source_target_pairs={{0,2},{1,3},{2,0},{3,1},{4,6},{5,7},{6,4},{7,5},{8,10},{9,11},{10,... | collective-permute-start | bytes 417800 | tf_op jit(solution)/shard_map/ppermute | solution.py:12
  81.1 7.5 %collective-permute-start.27 = (bf16[136,512]{1,0:T(8,128)(2,1)}, bf16[136,512]{1,0:T(8,128)(2,1)S(1)}, u32[]{:S(2)}, u32[]{:S(2)}) collective-permute-start(bf16[136,512]{1,0:T(8,128)(2,1)} %collective-permute-done.26), channel_id=1, source_target_pairs={{0,1},{1,0},{2,3},{3,2},{4,5},{5,4},{6,7},{7,6},{8,9},{9,8},{10,11... | collective-permute-start | bytes 417800 | tf_op jit(solution)/shard_map/ppermute | solution.py:12
  83.3 10.4 %collective-permute-start.23 = (bf16[136,512]{1,0:T(8,128)(2,1)}, bf16[136,512]{1,0:T(8,128)(2,1)S(1)}, u32[]{:S(2)}, u32[]{:S(2)}) collective-permute-start(bf16[136,512]{1,0:T(8,128)(2,1)} %collective-permute-done.22), channel_id=1, source_target_pairs={{0,1},{1,0},{2,3},{3,2},{4,5},{5,4},{6,7},{7,6},{8,9},{9,8},{10,11... | collective-permute-start | bytes 417800 | tf_op jit(solution)/shard_map/ppermute | solution.py:12
  87.8 6.8 %collective-permute-start.20 = (bf16[136,512]{1,0:T(8,128)(2,1)}, bf16[136,512]{1,0:T(8,128)(2,1)S(1)}, u32[]{:S(2)}, u32[]{:S(2)}) collective-permute-start(bf16[136,512]{1,0:T(8,128)(2,1)} %collective-permute-done.18), channel_id=1, source_target_pairs={{0,2},{1,3},{2,0},{3,1},{4,6},{5,7},{6,4},{7,5},{8,10},{9,11},{10,... | collective-permute-start | bytes 417800 | tf_op jit(solution)/shard_map/ppermute | solution.py:12
  88.5 8.2 %collective-permute-start.19 = (bf16[136,512]{1,0:T(8,128)(2,1)}, bf16[136,512]{1,0:T(8,128)(2,1)S(1)}, u32[]{:S(2)}, u32[]{:S(2)}) collective-permute-start(bf16[136,512]{1,0:T(8,128)(2,1)} %collective-permute-done.18), channel_id=1, source_target_pairs={{0,1},{1,0},{2,3},{3,2},{4,5},{5,4},{6,7},{7,6},{8,9},{9,8},{10,11... | collective-permute-start | bytes 417800 | tf_op jit(solution)/shard_map/ppermute | solution.py:12
  184.9 38.3 %collective-permute-start.51 = (bf16[128,512]{1,0:T(8,128)(2,1)}, bf16[128,512]{1,0:T(8,128)(2,1)}, u32[]{:S(2)}, u32[]{:S(2)}) collective-permute-start(bf16[128,512]{1,0:T(8,128)(2,1)} %convolution_convert_fusion.1), channel_id=1, source_target_pairs={{0,2},{1,3},{2,0},{3,1},{4,6},{5,7},{6,4},{7,5},{8,10},{9,11},{10,... | collective-permute-start | bytes 393224 | tf_op jit(solution)/shard_map/ppermute | solution.py:12
  187.0 8.9 %collective-permute-start.46 = (bf16[128,512]{1,0:T(8,128)(2,1)S(1)}, bf16[128,512]{1,0:T(8,128)(2,1)S(1)}, u32[]{:S(2)}, u32[]{:S(2)}) collective-permute-start(bf16[128,512]{1,0:T(8,128)(2,1)S(1)} %convolution_convert_fusion.5), channel_id=1, source_target_pairs={{0,1},{1,0},{2,3},{3,2},{4,5},{5,4},{6,7},{7,6},{8,9},{9,8},{10,11... | collective-permute-start | bytes 393224 | tf_op jit(solution)/shard_map/ppermute | solution.py:12
  188.5 15.2 %collective-permute-start.45 = (bf16[128,512]{1,0:T(8,128)(2,1)S(1)}, bf16[128,512]{1,0:T(8,128)(2,1)S(1)}, u32[]{:S(2)}, u32[]{:S(2)}) collective-permute-start(bf16[128,512]{1,0:T(8,128)(2,1)S(1)} %convolution_convert_fusion.7), channel_id=1, source_target_pairs={{0,1},{1,0},{2,3},{3,2},{4,5},{5,4},{6,7},{7,6},{8,9},{9,8},{10,11... | collective-permute-start | bytes 393224 | tf_op jit(solution)/shard_map/ppermute | solution.py:12
  189.1 20.1 %collective-permute-start.43 = (bf16[128,512]{1,0:T(8,128)(2,1)S(1)}, bf16[128,512]{1,0:T(8,128)(2,1)S(1)}, u32[]{:S(2)}, u32[]{:S(2)}) collective-permute-start(bf16[128,512]{1,0:T(8,128)(2,1)S(1)} %convolution_convert_fusion.9), channel_id=1, source_target_pairs={{0,2},{1,3},{2,0},{3,1},{4,6},{5,7},{6,4},{7,5},{8,10},{9,11},{10,... | collective-permute-start | bytes 393224 | tf_op jit(solution)/shard_map/ppermute | solution.py:12
  198.6 15.8 %collective-permute-start.37 = (bf16[128,512]{1,0:T(8,128)(2,1)S(1)}, bf16[128,512]{1,0:T(8,128)(2,1)S(1)}, u32[]{:S(2)}, u32[]{:S(2)}) collective-permute-start(bf16[128,512]{1,0:T(8,128)(2,1)S(1)} %convolution_convert_fusion.15), channel_id=1, source_target_pairs={{0,1},{1,0},{2,3},{3,2},{4,5},{5,4},{6,7},{7,6},{8,9},{9,8},{10,11... | collective-permute-start | bytes 393224 | tf_op jit(solution)/shard_map/ppermute | solution.py:12
  203.7 19.5 %collective-permute-start.50 = (bf16[128,512]{1,0:T(8,128)(2,1)S(1)}, bf16[128,512]{1,0:T(8,128)(2,1)}, u32[]{:S(2)}, u32[]{:S(2)}) collective-permute-start(bf16[128,512]{1,0:T(8,128)(2,1)S(1)} %fusion.27), channel_id=1, source_target_pairs={{0,1},{1,0},{2,3},{3,2},{4,5},{5,4},{6,7},{7,6},{8,9},{9,8},{10,11... | collective-permute-start | bytes 393224 | tf_op jit(solution)/shard_map/ppermute | solution.py:12
  209.1 7.5 %collective-permute-start.39 = (bf16[128,512]{1,0:T(8,128)(2,1)S(1)}, bf16[128,512]{1,0:T(8,128)(2,1)S(1)}, u32[]{:S(2)}, u32[]{:S(2)}) collective-permute-start(bf16[128,512]{1,0:T(8,128)(2,1)S(1)} %fusion.45), channel_id=1, source_target_pairs={{0,2},{1,3},{2,0},{3,1},{4,6},{5,7},{6,4},{7,5},{8,10},{9,11},{10,... | collective-permute-start | bytes 393224 | tf_op jit(solution)/shard_map/ppermute | solution.py:12
  212.3 10.9 %collective-permute-start.48 = (bf16[128,512]{1,0:T(8,128)(2,1)S(1)}, bf16[128,512]{1,0:T(8,128)(2,1)S(1)}, u32[]{:S(2)}, u32[]{:S(2)}) collective-permute-start(bf16[128,512]{1,0:T(8,128)(2,1)S(1)} %fusion.51), channel_id=1, source_target_pairs={{0,4},{1,5},{2,6},{3,7},{4,0},{5,1},{6,2},{7,3},{8,12},{9,13},{10,... | collective-permute-start | bytes 393224 | tf_op jit(solution)/shard_map/ppermute | solution.py:12
  214.4 8.9 %collective-permute-start.44 = (bf16[128,512]{1,0:T(8,128)(2,1)}, bf16[128,512]{1,0:T(8,128)(2,1)}, u32[]{:S(2)}, u32[]{:S(2)}) collective-permute-start(bf16[128,512]{1,0:T(8,128)(2,1)} %fusion.50), channel_id=1, source_target_pairs={{0,8},{1,9},{2,10},{3,11},{4,12},{5,13},{6,14},{7,15},{8,0},{9,1},... | collective-permute-start | bytes 393224 | tf_op jit(solution)/shard_map/ppermute | solution.py:12
  218.6 7.0 %collective-permute-start.40 = (bf16[128,512]{1,0:T(8,128)(2,1)}, bf16[128,512]{1,0:T(8,128)(2,1)S(1)}, u32[]{:S(2)}, u32[]{:S(2)}) collective-permute-start(bf16[128,512]{1,0:T(8,128)(2,1)} %fusion.49), channel_id=1, source_target_pairs={{0,12},{1,13},{2,14},{3,15},{4,8},{5,9},{6,10},{7,11},{8,4},{9,5},... | collective-permute-start | bytes 393224 | tf_op jit(solution)/shard_map/ppermute | solution.py:12
  (30 other events, 257.6 us)
Sparse Core Ops, SparseCore 0:
  73.0 63.2 all-gather.2

commit v2 on v0

v2 whole, which is shorter than its diff:
```python
import functools

import jax
import jax.numpy as jnp
from jax import lax
from jax.experimental import pallas as pl
from jax.experimental.pallas import tpu as pltpu
from jax.sharding import PartitionSpec as P

epsilon = 1e-05
f32 = jnp.float32
bf16 = jnp.bfloat16
words_height = 16
vmem = pl.BlockSpec(memory_space=pltpu.VMEM)
smem = pl.BlockSpec(memory_space=pltpu.SMEM)
anywhere = pl.BlockSpec(memory_space=pl.ANY)


def kernel_call(body, name, in_specs, out_shapes, out_specs, scratch, flops, moved):
    return pl.pallas_call(
        body,
        name=name,
        in_specs=in_specs,
        out_shape=out_shapes,
        out_specs=out_specs,
        scratch_shapes=scratch,
        cost_estimate=pl.CostEstimate(flops=flops, bytes_accessed=moved, transcendentals=0),
        compiler_params=pltpu.CompilerParams(vmem_limit_bytes=32 * 1024 * 1024),
    )


def swap(value, offset, count):
    return lax.ppermute(value, "vocab", [(i, i ^ offset) for i in range(count)])


def gather_pieces(own, count):
    pieces = {0: own}
    for k in range(4, count, 4):
        pieces[k] = swap(own, k, count)
    for number, base in enumerate(range(0, count, 4)):
        pieces[base + 1] = swap(pieces[base], 1, count)
        pieces[base + 2] = swap(pieces[base], 2, count)
        if number % 2:
            pieces[base + 3] = swap(pieces[base + 2], 1, count)
        else:
            pieces[base + 3] = swap(pieces[base + 1], 2, count)
    return pieces


def total(*parts):
    result = parts[0].astype(f32)
    for part in parts[1:]:
        result = result + part.astype(f32)
    return result


def scatter_sums(blocks, count):
    bases = list(range(0, count, 4))[::-1]
    second = {}
    for base in bases:
        if (base // 4) % 2:
            second[base + 1] = blocks[base + 1]
            second[base + 2] = total(blocks[base + 2], swap(blocks[base + 3], 1, count)).astype(bf16)
        else:
            second[base + 2] = blocks[base + 2]
            second[base + 1] = total(blocks[base + 1], swap(blocks[base + 3], 2, count)).astype(bf16)
    terms = []
    for base in bases:
        near = swap(second[base + 1], 1, count), swap(second[base + 2], 2, count)
        if base:
            terms.append(swap(total(blocks[base], *near).astype(bf16), base, count))
        else:
            terms.extend((blocks[0], *near))
    return terms


def pull(place, k, tables, buffer, sem):
    height = buffer.shape[0]
    index = place[0] ^ k
    if len(tables) == 1:
        rows = pl.ds(pl.multiple_of(index * height, height), height)
        pltpu.make_async_copy(tables[0].at[rows], buffer, sem).start()
        return
    per_table = tables[0].shape[0] // height
    rows = pl.ds(pl.multiple_of(lax.rem(index, per_table) * height, height), height)
    turn = lax.rem(lax.div(index, per_table) - place[1] + len(tables), len(tables))
    for number, table in enumerate(tables):

        @pl.when(turn == number)
        def _():
            pltpu.make_async_copy(table.at[rows], buffer, sem).start()


def arrived(tables, buffer, sem):
    pltpu.make_async_copy(tables[0].at[pl.ds(0, buffer.shape[0])], buffer, sem).wait()


def as_row(column):
    size = column.shape[0]
    return jnp.transpose(jnp.broadcast_to(column, (size, size)))[:1]


def as_column(row):
    size = row.shape[1]
    return jnp.transpose(jnp.broadcast_to(row, (size, size)))[:, :1]


def words_of(row, first):
    high = row.astype(bf16).astype(f32)
    middle = (row - high).astype(bf16).astype(f32)
    low = row - high - middle
    line = lax.broadcasted_iota(jnp.int32, (words_height, row.shape[1]), 0)
    block = jnp.where(line == first, high, 0.0)
    block = jnp.where(line == first + 1, middle, block)
    return jnp.where(line == first + 2, low, block)


def head_kernel(inputs, finals, gain, first, tail):
    rows = inputs.shape[0]
    half = rows // 2
    value = finals[...].astype(f32)
    target = (value * gain[...]).astype(bf16)
    first[:rows] = inputs[...]
    first[rows:] = target[:half]
    tail[:half] = target[half:]
    tail[half:] = jnp.zeros((words_height, value.shape[1]), bf16)
    squares = as_row(jnp.sum(value * value, axis=1, keepdims=True))
    tail[half:, :rows] = words_of(squares, 3).astype(bf16)


def contract_kernel(order, lines, table_count, words, place, *refs):
    pieces, refs = refs[: len(order)], refs[len(order) :]
    tables, refs = refs[:table_count], refs[table_count:]
    result, refs = refs[0], refs[1:]
    if words:
        word_sum, refs = refs[0], refs[1:]
    buffer, sems = refs
    for slot, k in enumerate(order):
        pull(place, k, tables, buffer.at[slot], sems.at[slot])
    for slot in range(len(order)):
        arrived(tables, buffer.at[slot], sems.at[slot])
        part = jnp.dot(pieces[slot][lines[0] : lines[1]], buffer[slot], preferred_element_type=f32)
        if slot:
            result[...] += part
        else:
            result[...] = part
    if words:
        word_sum[...] = sum(piece[-words_height:].astype(f32) for piece in pieces)


def trans_kernel(order, place, *refs):
    pieces, refs = refs[: len(order)], refs[len(order) :]
    weight, so_far, own, bias, gain, tail, trans, payload, buffer, sems = refs
    rows = so_far.shape[0]
    for slot, k in enumerate(order):
        pull(place, k, [weight], buffer.at[slot], sems.at[slot])
    trans[...] = so_far[...] + own[:rows].astype(f32) + bias[...]
    for slot in range(len(order)):
        arrived([weight], buffer.at[slot], sems.at[slot])
        trans[...] += jnp.dot(pieces[slot][:rows], buffer[slot], preferred_element_type=f32)
    value = trans[...]
    payload[:rows] = (value * gain[...]).astype(bf16)
    payload[rows:] = tail[...]
    squares = as_row(jnp.sum(value * value, axis=1, keepdims=True))
    start = payload.shape[0] - words_height
    payload[start:, :rows] = (
        words_of(squares, 0) + tail[-words_height:, :rows].astype(f32)
    ).astype(bf16)


def logits_kernel(order, table_count, width, place, *refs):
    pieces, refs = refs[: len(order)], refs[len(order) :]
    tables, refs = refs[:table_count], refs[table_count:]
    so_far, early_words, target_half, logits, target_logits, stats, scale, buffer, sems, acc = refs
    rows = logits.shape[0]
    half = target_half.shape[0]
    for slot, k in enumerate(order):
        pull(place, k, tables, buffer.at[slot], sems.at[slot])
    acc[...] = so_far[...]
    words = early_words[...] + sum(piece[-words_height:].astype(f32) for piece in pieces)
    words = words[:, :rows]
    trans_scale = lax.rsqrt((words[0:1] + words[1:2] + words[2:3]) / width + epsilon)
    final_scale = lax.rsqrt((words[3:4] + words[4:5] + words[5:6]) / width + epsilon)
    scale[...] = jnp.broadcast_to(trans_scale, scale.shape)
    trans_column, final_column = as_column(trans_scale), as_column(final_scale)
    for slot in range(len(order)):
        arrived(tables, buffer.at[slot], sems.at[slot])
        acc[...] += jnp.dot(pieces[slot][...], buffer[slot], preferred_element_type=f32)
    trans_logits = acc[:rows] * trans_column
    logits[...] = trans_logits
    target_logits[:half] = target_half[...] * final_column[:half]
    target_logits[half:] = acc[rows : rows + rows - half] * final_column[half:]
    target = target_logits[...]
    trans_max = jnp.max(trans_logits, axis=1, keepdims=True)
    target_max = jnp.max(target, axis=1, keepdims=True)
    shifted = trans_logits - trans_max
    trans_exp = jnp.exp(shifted)
    target_exp = jnp.exp(target - target_max)
    columns = (
        trans_max,
        jnp.sum(trans_exp, axis=1, keepdims=True),
        jnp.sum(trans_exp * shifted, axis=1, keepdims=True),
        target_max,
        jnp.sum(target_exp, axis=1, keepdims=True),
        jnp.sum(target_exp * (target - trans_logits), axis=1, keepdims=True),
        jnp.sum(target_exp * shifted, axis=1, keepdims=True),
    )
    lane = lax.broadcasted_iota(jnp.int32, (rows, rows), 1)
    packed = jnp.zeros((rows, rows), f32)
    for number, column in enumerate(columns):
        packed = jnp.where(lane == number, column, packed)
    stats[...] = jnp.transpose(packed)[: stats.shape[0]]


def backward_blocks(order, place, tables, dlogits, outs, buffer, sems):
    for slot in range(len(order)):
        arrived(tables, buffer.at[slot], sems.at[slot])
        outs[slot][...] = lax.dot_general(
            dlogits, buffer[slot], (((1,), (1,)), ((), ())), preferred_element_type=f32
        ).astype(bf16)


def first_backward_kernel(order, table_count, place, *refs):
    tables, refs = refs[:table_count], refs[table_count:]
    logits, target_logits, *stats = refs[:6]
    refs = refs[6:]
    dlogits, info, *outs = refs[:-2]
    buffer, sems = refs[-2:]
    for slot, k in enumerate(order):
        pull(place, k, tables, buffer.at[slot], sems.at[slot])
    every = [part[i] for part in stats for i in range(part.shape[0])]
    top = functools.reduce(jnp.maximum, [s[0:1] for s in every])
    target_top = functools.reduce(jnp.maximum, [s[3:4] for s in every])
    trans_sum = target_sum = kl_sum = trans_dot = target_dot = 0.0
    for s in every:
        drop = s[0:1] - top
        factor = jnp.exp(drop)
        target_factor = jnp.exp(s[3:4] - target_top)
        trans_sum += factor * s[1:2]
        target_sum += target_factor * s[4:5]
        kl_sum += target_factor * s[5:6]
        trans_dot += factor * (s[2:3] + s[1:2] * drop)
        target_dot += target_factor * (s[6:7] + s[4:5] * drop)
    log_sum = top + jnp.log(trans_sum)
    target_log_sum = target_top + jnp.log(target_sum)
    value = (
        jnp.exp(logits[...] - as_column(log_sum))
        - jnp.exp(target_logits[...] - as_column(target_log_sum))
    ).astype(bf16)
    dlogits[...] = value
    line = lax.broadcasted_iota(jnp.int32, info.shape, 0)
    kl_rows = kl_sum / target_sum - (target_log_sum - log_sum)
    info[...] = jnp.where(line == 0, kl_rows, trans_dot / trans_sum - target_dot / target_sum)
    backward_blocks(order, place, tables, value, outs, buffer, sems)


def later_backward_kernel(order, table_count, place, *refs):
    tables, refs = refs[:table_count], refs[table_count:]
    dlogits, *outs = refs[:-2]
    buffer, sems = refs[-2:]
    for slot, k in enumerate(order):
        pull(place, k, tables, buffer.at[slot], sems.at[slot])
    backward_blocks(order, place, tables, dlogits[...], outs, buffer, sems)


def weight_kernel(count, term_count, width, place, *refs):
    pieces, refs = refs[:count], refs[count:]
    terms, refs = refs[:term_count], refs[term_count:]
    trans, gain, scale, info, grad_weight, grad_bias, kl, buffer, sems = refs
    rows = trans.shape[0]
    height = buffer.shape[1]
    dnormed = functools.reduce(lambda a, b: a + b, [term[...].astype(f32) for term in terms])
    scale_row = scale[0:1]
    weight_row = scale_row * scale_row * info[1:2] / (width * scale_row)
    dtrans = as_column(scale_row) * (dnormed * gain[...] - trans[...] * as_column(weight_row))
    grad_bias[...] = jnp.sum(dtrans, axis=0, keepdims=True)
    kl[...] = jnp.broadcast_to(jnp.sum(info[0:1], axis=1, keepdims=True) / rows, kl.shape)
    rounded = dtrans.astype(bf16)
    copies = []
    for k in range(count):
        buffer[k] = lax.dot_general(
            pieces[k][:rows], rounded, (((0,), (0,)), ((), ())), preferred_element_type=f32
        ).astype(bf16)
        start = pl.multiple_of((place[0] ^ k) * height, height)
        copies.append(pltpu.make_async_copy(buffer.at[k], grad_weight.at[0, pl.ds(start, height)], sems.at[k]))
        copies[-1].start()
    for copy in copies:
        copy.wait()


def per_device(hidden, final_hidden, row_pick, trans_weight, trans_bias, norm_gain, unembed):
    count = lax.axis_size("vocab")
    sections = lax.axis_size("section")
    me = lax.axis_index("vocab")
    section = lax.axis_index("section")
    place = jnp.stack([me, section]).astype(jnp.int32)
    width, cols = trans_weight.shape[1:]
    rows = row_pick.shape[1]
    half = rows // 2
    picked = row_pick[0]
    weight = trans_weight[0]
    gain = norm_gain.astype(f32)[None]
    bias = trans_bias.astype(f32)
    shape = jax.ShapeDtypeStruct
    entries = unembed.shape[1]
    weight_block = 2 * cols * cols
    table_block = 2 * cols * entries

    def table_scratch(number, columns):
        return [pltpu.VMEM((number, cols, columns), bf16), pltpu.SemaphoreType.DMA((number,))]

    final_all = lax.all_gather(final_hidden, "section", axis=0, tiled=True)
    first_own, tail = kernel_call(
        head_kernel,
        "head",
        [vmem] * 3,
        (shape((rows + half, cols), bf16), shape((rows - half + words_height, cols), bf16)),
        (vmem, vmem),
        [],
        0,
        6 * rows * cols,
    )(hidden[0][picked], final_all[picked], gain)
    first = gather_pieces(first_own, count)

    tables = [unembed] + [
        lax.ppermute(unembed, "section", [((i + k) % sections, i) for i in range(sections)])
        for k in range(1, sections)
    ]

    early = list(range(count // 2))
    late = list(range(count // 2, count))
    side = len(early)
    so_far = kernel_call(
        functools.partial(contract_kernel, early, (0, rows), 1, False),
        "trans_early",
        [smem] + [vmem] * side + [anywhere],
        shape((rows, cols), f32),
        vmem,
        table_scratch(side, cols),
        side * rows * weight_block,
        side * weight_block,
    )(place, *[first[k] for k in early], weight)
    payload_shape = shape((first_own.shape[0] + words_height, cols), bf16)
    trans, second_own = kernel_call(
        functools.partial(trans_kernel, late),
        "trans_late",
        [smem] + [vmem] * side + [anywhere] + [vmem] * 5,
        (shape((rows, cols), f32), payload_shape),
        (vmem, vmem),
        table_scratch(side, cols),
        side * rows * weight_block,
        side * weight_block,
    )(place, *[first[k] for k in late], weight, so_far, first_own, bias, gain, tail)
    second = gather_pieces(second_own, count)

    every = early + late
    target_half = kernel_call(
        functools.partial(contract_kernel, every, (rows, rows + half), sections, False),
        "target_half",
        [smem] + [vmem] * count + [anywhere] * sections,
        shape((half, entries), f32),
        vmem,
        table_scratch(count, entries),
        count * half * table_block,
        count * table_block,
    )(place, *[first[k] for k in every], *tables)
    height = payload_shape.shape[0]
    so_far, words = kernel_call(
        functools.partial(contract_kernel, early, (0, height), sections, True),
        "logits_early",
        [smem] + [vmem] * side + [anywhere] * sections,
        (shape((height, entries), f32), shape((words_height, cols), f32)),
        (vmem, vmem),
        table_scratch(side, entries),
        side * height * table_block,
        side * table_block,
    )(place, *[second[k] for k in early], *tables)
    logits, target_logits, stats, scale = kernel_call(
        functools.partial(logits_kernel, late, sections, width),
        "logits_late",
        [smem] + [vmem] * side + [anywhere] * sections + [vmem] * 3,
        (shape((rows, entries), f32), shape((rows, entries), f32), shape((8, rows), f32), shape((8, rows), f32)),
        (vmem,) * 4,
        table_scratch(side, entries) + [pltpu.VMEM((height, entries), f32)],
        side * height * table_block,
        side * table_block,
    )(place, *[second[k] for k in late], *tables, so_far, words, target_half)

    line_stats = jnp.stack([stats] + [swap(stats, k, count) for k in range(4, count, 4)])
    all_stats = [line_stats] + [swap(line_stats, k, count) for k in (1, 2, 3)]

    blocks = {}
    far = [base + 3 for base in range(0, count, 4)][::-1]
    piece = shape((rows, cols), bf16)
    dlogits, info, *made = kernel_call(
        functools.partial(first_backward_kernel, far, sections),
        "backward_far",
        [smem] + [anywhere] * sections + [vmem] * 6,
        (shape((rows, entries), bf16), shape((8, rows), f32), *[piece] * len(far)),
        (vmem,) * (2 + len(far)),
        table_scratch(len(far), entries),
        len(far) * rows * table_block,
        len(far) * table_block,
    )(place, *tables, logits, target_logits, *all_stats)
    blocks.update(zip(far, made))
    rest = [base + k for k in (1, 2, 0) for base in range(0, count, 4)[::-1]]
    made = kernel_call(
        functools.partial(later_backward_kernel, rest, sections),
        "backward_rest",
        [smem] + [anywhere] * sections + [vmem],
        tuple([piece] * len(rest)),
        (vmem,) * len(rest),
        table_scratch(len(rest), entries),
        len(rest) * rows * table_block,
        len(rest) * table_block,
    )(place, *tables, dlogits)
    blocks.update(zip(rest, made))
    terms = scatter_sums(blocks, count)

    grad_weight, grad_bias, kl = kernel_call(
        functools.partial(weight_kernel, count, len(terms), width),
        "grad_weight",
        [smem] + [vmem] * (count + len(terms) + 4),
        (shape((1, width, cols), bf16), shape((1, cols), f32), shape((1, rows), f32)),
        (anywhere, vmem, vmem),
        table_scratch(count, cols),
        count * rows * weight_block,
        count * weight_block,
    )(place, *[first[k] for k in range(count)], *terms, trans, gain, scale, info)
    return grad_weight, grad_bias, kl[0, :1]


def solution(mesh):
    placed = (
        P("section", None, "vocab"),
        P("section", "vocab"),
        P("section", None),
        P("section", None, "vocab"),
        P("section", "vocab"),
        P("vocab"),
        P("section", "vocab"),
    )
    return jax.shard_map(
        per_device,
        mesh=mesh,
        in_specs=placed,
        out_specs=(P("section", None, "vocab"), P("section", "vocab"), P("section")),
        check_vma=False,
    )
```

time: 461 us -> 171 us (0.37)
  blocking collectives: 229 us -> 5.17 us
  waiting for transfers between devices: 177 us -> 57 us
  starting transfers between devices: 0.2 us -> 67.8 us
  matrix products: 30.4 us -> 0 us
  Pallas kernels: 0 us -> 29 us
  between operations: 15.6 us -> 1.05 us
  local copies, waits for them, and re-layouts: 2.67 us -> 8.47 us
    all_gather x5 -> x1, blocking collectives: 151 us -> 5.17 us  [per_device(): final_all = lax.all_gather(final_hidden, 'section', axis=0, tiled=True)]
    all_gather x4 -> x0, waiting for transfers between devices: 137 us -> none  [the longest x1 61.2 us: per_device(): inputs = lax.all_gather(input_cols, 'vocab', axis=1, tiled=True)]
    psum x2 -> x0, blocking collectives: 77.8 us -> none  [the longest x1 38.9 us: per_device(): lax.psum((jnp.sum(trans * trans, axis=-1), jnp.sum(finals * finals, axis=...]
    ppermute x0 -> x52, starting transfers between devices: none -> 67.8 us  [the longest x51 67.3 us: swap(): return lax.ppermute(value, 'vocab', [(i, i ^ offset) for i in range(count)])]
    ppermute x0 -> x52, waiting for transfers between devices: none -> 57 us  [the longest x51 57 us: swap(): return lax.ppermute(value, 'vocab', [(i, i ^ offset) for i in range(count)])]
    reduce_scatter x1 -> x0, waiting for transfers between devices: 38.5 us -> none  [per_device(): lax.psum_scatter(lax.dot_general(slab_rows, dlogits, (((1,), (1,)), ((),...]
    dot_general x5 -> x0, matrix products: 30.4 us -> none  [the longest x1 7.54 us: per_device(): lax.dot_general(slab_rows, dlogits, (((1,), (1,)), ((), ())), preferred_e...]
    pallas_call x0 -> x9, Pallas kernels: none -> 29 us  [the longest x1 5.44 us: per_device(): kernel_call(functools.partial(later_backward_kernel, rest, sections), 'ba...]
  transfers between devices with their start and end apart: 5 -> 52, of which waited for: 4 -> 22; matrix products, arithmetic and copies ran while one was open for 2% -> 2% of each run, Pallas kernels for 0% -> 10%
where the time goes in v2:
time: 171 us
  starting transfers between devices  67.8 us (40%)
  waiting for transfers between devices  57 us (33%)
  Pallas kernels  29 us (17%)
  local copies, waits for them, and re-layouts  8.47 us (5%)
  blocking collectives  5.17 us (3%)
  other arithmetic  2.43 us (1%)
    ppermute x51, starting transfers between devices, swap(): return lax.ppermute(value, 'vocab', [(i, i ^ offset) for i in range(count)])  67.3 us
    ppermute x51, waiting for transfers between devices, swap(): return lax.ppermute(value, 'vocab', [(i, i ^ offset) for i in range(count)])  57 us
    unnamed x12, local copies, waits for them, and re-layouts  6.78 us
    pallas_call x1, Pallas kernels, per_device(): kernel_call(functools.partial(later_backward_kernel, rest, sections), 'ba...  5.44 us
    pallas_call x1, Pallas kernels, per_device(): kernel_call(functools.partial(weight_kernel, count, len(terms), width), '...  5.42 us
    all_gather x1, blocking collectives, per_device(): final_all = lax.all_gather(final_hidden, 'section', axis=0, tiled=True)  5.17 us
    pallas_call x1, Pallas kernels, per_device(): kernel_call(functools.partial(logits_kernel, late, sections, width), 'log...  4.14 us
    pallas_call x1, Pallas kernels, per_device(): kernel_call(functools.partial(contract_kernel, every, (rows, rows + half)...  3.88 us
  transfers between devices with their start and end apart: 52, of which 22 were waited for; matrix products, arithmetic and copies ran while one was open for 2% of the time, Pallas kernels for 10%

profile of v2, /device:TPU:0, one launch (start us, length us, event | category | flops | bytes accessed | tf_op | source)
XLA Modules:
  0.0 170.9 jit_solution(12791262365886316780)
XLA Ops:
  3.4 5.2 %all_gather.3 = bf16[512,512]{1,0:T(8,128)(2,1)S(1)} all-gather(bf16[256,512]{1,0:T(8,128)(2,1)} %param.8), channel_id=1, replica_groups=mesh['section'=2,'vocab'=16] {'section'}, dimensions={0}, use_global_device_ids=true | all-gather | bytes 786432 | tf_op jit(solution)/shard_map/all_gather | solution.py:312
  9.6 5.0 %collective-permute-start.11 = (bf16[192,512]{1,0:T(8,128)(2,1)S(1)}, bf16[192,512]{1,0:T(8,128)(2,1)S(1)}, u32[]{:S(2)}, u32[]{:S(2)}) collective-permute-start(bf16[192,512]{1,0:T(8,128)(2,1)S(1)} %get-tuple-element.34.refs_0_.refs_10_), channel_id=1, source_target_pairs={{0,12},{1,13},{2,14},{3,15},{4,8},{5,9},{6,10},{7,11},{8,4},{9,5},... | collective-permute-start | bytes 589832 | tf_op jit(solution)/shard_map/ppermute | solution.py:33
  16.9 3.5 %collective-permute-done.11.refs_4_.refs_12_ = bf16[192,512]{1,0:T(8,128)(2,1)S(1)} collective-permute-done((bf16[192,512]{1,0:T(8,128)(2,1)S(1)}, bf16[192,512]{1,0:T(8,128)(2,1)S(1)}, u32[]{:S(2)}, u32[]{:S(2)}) %collective-permute-start.11) | collective-permute-done | bytes 196640 | tf_op jit(solution)/shard_map/ppermute | solution.py:33
  22.1 9.4 %collective-permute-done.7.refs_0_.refs_8_ = bf16[192,512]{1,0:T(8,128)(2,1)S(1)} collective-permute-done((bf16[192,512]{1,0:T(8,128)(2,1)S(1)}, bf16[192,512]{1,0:T(8,128)(2,1)S(1)}, u32[]{:S(2)}, u32[]{:S(2)}) %collective-permute-start.7) | collective-permute-done | bytes 196640 | tf_op jit(solution)/shard_map/ppermute | solution.py:33
  35.6 3.8 %collective-permute-done.13.refs_6_.refs_14_ = bf16[192,512]{1,0:T(8,128)(2,1)S(1)} collective-permute-done((bf16[192,512]{1,0:T(8,128)(2,1)S(1)}, bf16[192,512]{1,0:T(8,128)(2,1)S(1)}, u32[]{:S(2)}, u32[]{:S(2)}) %collective-permute-start.13) | collective-permute-done | bytes 196640 | tf_op jit(solution)/shard_map/ppermute | solution.py:33
  40.9 2.7 %collective-permute-done.5.refs_6_ = bf16[192,512]{1,0:T(8,128)(2,1)S(1)} collective-permute-done((bf16[192,512]{1,0:T(8,128)(2,1)S(1)}, bf16[192,512]{1,0:T(8,128)(2,1)S(1)}, u32[]{:S(2)}, u32[]{:S(2)}) %collective-permute-start.5) | collective-permute-done | bytes 196640 | tf_op jit(solution)/shard_map/ppermute | solution.py:33
  49.3 2.1 %collective-permute-done.6.refs_7_ = bf16[192,512]{1,0:T(8,128)(2,1)S(1)} collective-permute-done((bf16[192,512]{1,0:T(8,128)(2,1)S(1)}, bf16[192,512]{1,0:T(8,128)(2,1)S(1)}, u32[]{:S(2)}, u32[]{:S(2)}) %collective-permute-start.6) | collective-permute-done | bytes 196640 | tf_op jit(solution)/shard_map/ppermute | solution.py:33
  53.8 3.4 %copy-done.2 = bf16[1,8192,512]{2,1,0:T(8,128)(2,1)S(1)} copy-done((bf16[1,8192,512]{2,1,0:T(8,128)(2,1)S(1)}, bf16[1,8192,512]{2,1,0:T(8,128)(2,1)}, u32[]{:S(2)}) %copy-start.2) | copy-done | bytes 8388632
  57.1 2.0 %trans_early.1.refs_9_ = f32[128,512]{1,0:T(8,128)S(1)} custom-call(s32[2]{0:T(128)S(1)} %pad_add_fusion.place, bf16[192,512]{1,0:T(8,128)(2,1)S(1)} %get-tuple-element.34.refs_0_.refs_10_, bf16[192,512]{1,0:T(8,128)(2,1)S(1)} %collective-permute-done.refs_1_, bf16[192,512]{1,0:T(8,128)(2,1)S(1)} %collective-permute-done.1.refs_2_, ...), custom_call_target="tpu_custom_call" | custom-call | flops 536870912 | bytes 4194304 | tf_op jit(solution)/shard_map/trans_early/pallas_call | solution.py:333
  59.2 3.4 %copy-done.3 = bf16[1,8192,512]{2,1,0:T(8,128)(2,1)S(1)} copy-done((bf16[1,8192,512]{2,1,0:T(8,128)(2,1)S(1)}, bf16[1,8192,512]{2,1,0:T(8,128)(2,1)}, u32[]{:S(2)}) %copy-start.3) | copy-done | bytes 8388632
  62.6 2.6 %trans_late.1 = (f32[128,512]{1,0:T(8,128)S(1)}, bf16[208,512]{1,0:T(8,128)(2,1)S(1)}) custom-call(s32[2]{0:T(128)S(1)} %pad_add_fusion.place, bf16[192,512]{1,0:T(8,128)(2,1)S(1)} %collective-permute-done.7.refs_0_.refs_8_, bf16[192,512]{1,0:T(8,128)(2,1)S(1)} %collective-permute-done.8.refs_1_.refs_9_, ...), custom_call_target="tpu_custom_call" | custom-call | flops 536870912 | bytes 4194304 | tf_op jit(solution)/shard_map/trans_late/pallas_call | solution.py:344
  67.3 2.5 %collective-permute-start.20 = (bf16[208,512]{1,0:T(8,128)(2,1)S(1)}, bf16[208,512]{1,0:T(8,128)(2,1)S(1)}, u32[]{:S(2)}, u32[]{:S(2)}) collective-permute-start(bf16[208,512]{1,0:T(8,128)(2,1)S(1)} %get-tuple-element.36.refs_0_), channel_id=1, source_target_pairs={{0,12},{1,13},{2,14},{3,15},{4,8},{5,9},{6,10},{7,11},{8,4},{9,5},... | collective-permute-start | bytes 638984 | tf_op jit(solution)/shard_map/ppermute | solution.py:33
  74.0 3.0 %collective-permute-start.28 = (bf16[208,512]{1,0:T(8,128)(2,1)S(1)}, bf16[208,512]{1,0:T(8,128)(2,1)S(1)}, u32[]{:S(2)}, u32[]{:S(2)}) collective-permute-start(bf16[208,512]{1,0:T(8,128)(2,1)S(1)} %collective-permute-done.27.refs_4_), channel_id=1, source_target_pairs={{0,1},{1,0},{2,3},{3,2},{4,5},{5,4},{6,7},{7,6},{8,9},{9,8},{10,11... | collective-permute-start | bytes 638984 | tf_op jit(solution)/shard_map/ppermute | solution.py:33
  78.9 3.8 %collective-permute-done.16.refs_0_ = bf16[208,512]{1,0:T(8,128)(2,1)S(1)} collective-permute-done((bf16[208,512]{1,0:T(8,128)(2,1)S(1)}, bf16[208,512]{1,0:T(8,128)(2,1)S(1)}, u32[]{:S(2)}, u32[]{:S(2)}) %collective-permute-start.16) | collective-permute-done | bytes 213024 | tf_op jit(solution)/shard_map/ppermute | solution.py:33
  87.3 2.1 %collective-permute-done.22.refs_6_ = bf16[208,512]{1,0:T(8,128)(2,1)S(1)} collective-permute-done((bf16[208,512]{1,0:T(8,128)(2,1)S(1)}, bf16[208,512]{1,0:T(8,128)(2,1)S(1)}, u32[]{:S(2)}, u32[]{:S(2)}) %collective-permute-start.22) | collective-permute-done | bytes 213024 | tf_op jit(solution)/shard_map/ppermute | solution.py:33
  90.3 2.0 %collective-permute-done.17.refs_1_ = bf16[208,512]{1,0:T(8,128)(2,1)S(1)} collective-permute-done((bf16[208,512]{1,0:T(8,128)(2,1)S(1)}, bf16[208,512]{1,0:T(8,128)(2,1)S(1)}, u32[]{:S(2)}, u32[]{:S(2)}) %collective-permute-start.17) | collective-permute-done | bytes 213024 | tf_op jit(solution)/shard_map/ppermute | solution.py:33
  93.3 2.0 %collective-permute-start.19 = (bf16[208,512]{1,0:T(8,128)(2,1)S(1)}, bf16[208,512]{1,0:T(8,128)(2,1)S(1)}, u32[]{:S(2)}, u32[]{:S(2)}) collective-permute-start(bf16[208,512]{1,0:T(8,128)(2,1)S(1)} %collective-permute-done.17.refs_1_), channel_id=1, source_target_pairs={{0,2},{1,3},{2,0},{3,1},{4,6},{5,7},{6,4},{7,5},{8,10},{9,11},{10,... | collective-permute-start | bytes 638984 | tf_op jit(solution)/shard_map/ppermute | solution.py:33
  95.3 3.9 %target_half.1.refs_12_ = f32[64,512]{1,0:T(8,128)S(1)} custom-call(s32[2]{0:T(128)S(1)} %pad_add_fusion.place, bf16[192,512]{1,0:T(8,128)(2,1)S(1)} %get-tuple-element.34.refs_0_.refs_10_, bf16[192,512]{1,0:T(8,128)(2,1)S(1)} %collective-permute-done.refs_1_, bf16[192,512]{1,0:T(8,128)(2,1)S(1)} %collective-permute-done.1.refs_2_, ...), custom_call_target="tpu_custom_call" | custom-call | flops 536870912 | bytes 8388608 | tf_op jit(solution)/shard_map/target_half/pallas_call | solution.py:357
  99.2 2.5 %logits_early.1 = (f32[208,512]{1,0:T(8,128)S(1)}, f32[16,512]{1,0:T(8,128)S(1)}) custom-call(s32[2]{0:T(128)S(1)} %pad_add_fusion.place, bf16[208,512]{1,0:T(8,128)(2,1)S(1)} %get-tuple-element.36.refs_0_, bf16[208,512]{1,0:T(8,128)(2,1)S(1)} %collective-permute-done.24.refs_1_, bf16[208,512]{1,0:T(8,128)(2,1)S(1)} %collective-permute-done.25.refs_2_, ...), custom_call_target="tpu_custom_call" | custom-call | flops 872415232 | bytes 4194304 | tf_op jit(solution)/shard_map/logits_early/pallas_call | solution.py:368
  101.7 4.1 %logits_late.1 = (f32[128,512]{1,0:T(8,128)S(1)}, f32[128,512]{1,0:T(8,128)S(1)}, f32[8,128]{1,0:T(8,128)S(1)}, f32[8,128]{1,0:T(8,128)S(1)}) custom-call(s32[2]{0:T(128)S(1)} %pad_add_fusion.place, bf16[208,512]{1,0:T(8,128)(2,1)S(1)} %collective-permute-done.16.refs_0_, bf16[208,512]{1,0:T(8,128)(2,1)S(1)} %collective-permute-done.17.refs_1_, ...), custom_call_target="tpu_custom_call" | custom-call | flops 872415232 | bytes 4194304 | tf_op jit(solution)/shard_map/logits_late/pallas_call | solution.py:378
  105.8 2.4 %collective-permute-start.33 = (f32[8,128]{1,0:T(8,128)S(1)}, f32[8,128]{1,0:T(8,128)S(1)}, u32[]{:S(2)}, u32[]{:S(2)}) collective-permute-start(f32[8,128]{1,0:T(8,128)S(1)} %get-tuple-element.41), channel_id=1, source_target_pairs={{0,12},{1,13},{2,14},{3,15},{4,8},{5,9},{6,10},{7,11},{8,4},{9,5},... | collective-permute-start | bytes 12296 | tf_op jit(solution)/shard_map/ppermute | solution.py:33
  108.2 2.1 %collective-permute-start.31 = (f32[8,128]{1,0:T(8,128)S(1)}, f32[8,128]{1,0:T(8,128)S(1)}, u32[]{:S(2)}, u32[]{:S(2)}) collective-permute-start(f32[8,128]{1,0:T(8,128)S(1)} %get-tuple-element.41), channel_id=1, source_target_pairs={{0,4},{1,5},{2,6},{3,7},{4,0},{5,1},{6,2},{7,3},{8,12},{9,13},{10,... | collective-permute-start | bytes 12296 | tf_op jit(solution)/shard_map/ppermute | solution.py:33
  118.4 2.9 %backward_far.1 = (bf16[128,512]{1,0:T(8,128)(2,1)S(1)}, f32[8,128]{1,0:T(8,128)S(1)}, bf16[128,512]{1,0:T(8,128)(2,1)S(1)}, bf16[128,512]{1,0:T(8,128)(2,1)S(1)...) custom-call(s32[2]{0:T(128)S(1)} %pad_add_fusion.place, bf16[4096,512]{1,0:T(8,128)(2,1)S(1)} %copy-done.1, ...), custom_call_target="tpu_custom_call" | custom-call | flops 268435456 | bytes 2097152 | tf_op jit(solution)/shard_map/backward_far/pallas_call | solution.py:395
  122.9 5.4 %backward_rest.1 = (bf16[128,512]{1,0:T(8,128)(2,1)S(1)}, bf16[128,512]{1,0:T(8,128)(2,1)S(1)}, bf16[128,512]{1,0:T(8,128)(2,1)S(1)}, bf16[128,512]{1,0:T(8,128)...) custom-call(s32[2]{0:T(128)S(1)} %pad_add_fusion.place, ...), custom_call_target="tpu_custom_call" | custom-call | flops 805306368 | bytes 6291456 | tf_op jit(solution)/shard_map/backward_rest/pallas_call | solution.py:407
  132.9 5.1 %collective-permute-done.41 = bf16[128,512]{1,0:T(8,128)(2,1)S(1)} collective-permute-done((bf16[128,512]{1,0:T(8,128)(2,1)S(1)}, bf16[128,512]{1,0:T(8,128)(2,1)S(1)}, u32[]{:S(2)}, u32[]{:S(2)}) %collective-permute-start.41) | collective-permute-done | bytes 131104 | tf_op jit(solution)/shard_map/ppermute | solution.py:33
  139.7 3.3 %collective-permute-done.46 = bf16[128,512]{1,0:T(8,128)(2,1)S(1)} collective-permute-done((bf16[128,512]{1,0:T(8,128)(2,1)S(1)}, bf16[128,512]{1,0:T(8,128)(2,1)S(1)}, u32[]{:S(2)}, u32[]{:S(2)}) %collective-permute-start.46) | collective-permute-done | bytes 131104 | tf_op jit(solution)/shard_map/ppermute | solution.py:33
  144.4 3.5 %collective-permute-done.49 = bf16[128,512]{1,0:T(8,128)(2,1)S(1)} collective-permute-done((bf16[128,512]{1,0:T(8,128)(2,1)S(1)}, bf16[128,512]{1,0:T(8,128)(2,1)S(1)}, u32[]{:S(2)}, u32[]{:S(2)}) %collective-permute-start.49) | collective-permute-done | bytes 131104 | tf_op jit(solution)/shard_map/ppermute | solution.py:33
  150.2 2.7 %collective-permute-done.39 = bf16[128,512]{1,0:T(8,128)(2,1)S(1)} collective-permute-done((bf16[128,512]{1,0:T(8,128)(2,1)S(1)}, bf16[128,512]{1,0:T(8,128)(2,1)S(1)}, u32[]{:S(2)}, u32[]{:S(2)}) %collective-permute-start.39) | collective-permute-done | bytes 131104 | tf_op jit(solution)/shard_map/ppermute | solution.py:33
  155.2 2.1 %collective-permute-start.40 = (bf16[128,512]{1,0:T(8,128)(2,1)S(1)}, bf16[128,512]{1,0:T(8,128)(2,1)S(1)}, u32[]{:S(2)}, u32[]{:S(2)}) collective-permute-start(bf16[128,512]{1,0:T(8,128)(2,1)S(1)} %add_convert_fusion.5), channel_id=1, source_target_pairs={{0,12},{1,13},{2,14},{3,15},{4,8},{5,9},{6,10},{7,11},{8,4},{9,5},... | collective-permute-start | bytes 393224 | tf_op jit(solution)/shard_map/ppermute | solution.py:33
  159.9 2.2 %collective-permute-done.40.refs_16_ = bf16[128,512]{1,0:T(8,128)(2,1)S(1)} collective-permute-done((bf16[128,512]{1,0:T(8,128)(2,1)S(1)}, bf16[128,512]{1,0:T(8,128)(2,1)S(1)}, u32[]{:S(2)}, u32[]{:S(2)}) %collective-permute-start.40) | collective-permute-done | bytes 131104 | tf_op jit(solution)/shard_map/ppermute | solution.py:33
  162.1 3.2 %collective-permute-done.44.refs_17_ = bf16[128,512]{1,0:T(8,128)(2,1)S(1)} collective-permute-done((bf16[128,512]{1,0:T(8,128)(2,1)S(1)}, bf16[128,512]{1,0:T(8,128)(2,1)S(1)}, u32[]{:S(2)}, u32[]{:S(2)}) %collective-permute-start.44) | collective-permute-done | bytes 131104 | tf_op jit(solution)/shard_map/ppermute | solution.py:33
  165.3 5.4 %grad_weight.1 = (bf16[1,8192,512]{2,1,0:T(8,128)(2,1)}, f32[1,512]{1,0:T(1,128)}, f32[1,128]{1,0:T(1,128)}) custom-call(s32[2]{0:T(128)S(1)} %pad_add_fusion.place, bf16[192,512]{1,0:T(8,128)(2,1)S(1)} %get-tuple-element.34.refs_0_.refs_10_, bf16[192,512]{1,0:T(8,128)(2,1)S(1)} %collective-permute-done.refs_1_, ...), custom_call_target="tpu_custom_call" | custom-call | flops 1073741824 | bytes 8388608 | tf_op jit(solution)/shard_map/grad_weight/pallas_call | solution.py:420
  (109 shorter events, 60.5 us)
Async XLA Ops:
  0.6 92.6 %collective-permute-start.15 = (bf16[4096,512]{1,0:T(8,128)(2,1)}, bf16[4096,512]{1,0:T(8,128)(2,1)}, u32[]{:S(2)}, u32[]{:S(2)}) collective-permute-start(bf16[4096,512]{1,0:T(8,128)(2,1)} %refs_0_.3), channel_id=1, source_target_pairs={{16,0},{0,16},{17,1},{1,17},{18,2},{2,18},{19,3},{3,19},{20,4},{4,... | collective-permute-start | bytes 12582920 | tf_op jit(solution)/shard_map/ppermute | solution.py:326
  9.6 10.8 %collective-permute-start.11 = (bf16[192,512]{1,0:T(8,128)(2,1)S(1)}, bf16[192,512]{1,0:T(8,128)(2,1)S(1)}, u32[]{:S(2)}, u32[]{:S(2)}) collective-permute-start(bf16[192,512]{1,0:T(8,128)(2,1)S(1)} %get-tuple-element.34.refs_0_.refs_10_), channel_id=1, source_target_pairs={{0,12},{1,13},{2,14},{3,15},{4,8},{5,9},{6,10},{7,11},{8,4},{9,5},... | collective-permute-start | bytes 589832 | tf_op jit(solution)/shard_map/ppermute | solution.py:33
  14.6 17.0 %collective-permute-start.7 = (bf16[192,512]{1,0:T(8,128)(2,1)S(1)}, bf16[192,512]{1,0:T(8,128)(2,1)S(1)}, u32[]{:S(2)}, u32[]{:S(2)}) collective-permute-start(bf16[192,512]{1,0:T(8,128)(2,1)S(1)} %get-tuple-element.34.refs_0_.refs_10_), channel_id=1, source_target_pairs={{0,8},{1,9},{2,10},{3,11},{4,12},{5,13},{6,14},{7,15},{8,0},{9,1},... | collective-permute-start | bytes 589832 | tf_op jit(solution)/shard_map/ppermute | solution.py:33
  14.6 18.5 %collective-permute-start.3 = (bf16[192,512]{1,0:T(8,128)(2,1)S(1)}, bf16[192,512]{1,0:T(8,128)(2,1)S(1)}, u32[]{:S(2)}, u32[]{:S(2)}) collective-permute-start(bf16[192,512]{1,0:T(8,128)(2,1)S(1)} %get-tuple-element.34.refs_0_.refs_10_), channel_id=1, source_target_pairs={{0,4},{1,5},{2,6},{3,7},{4,0},{5,1},{6,2},{7,3},{8,12},{9,13},{10,... | collective-permute-start | bytes 589832 | tf_op jit(solution)/shard_map/ppermute | solution.py:33
  15.2 18.4 %collective-permute-start.1 = (bf16[192,512]{1,0:T(8,128)(2,1)S(1)}, bf16[192,512]{1,0:T(8,128)(2,1)S(1)}, u32[]{:S(2)}, u32[]{:S(2)}) collective-permute-start(bf16[192,512]{1,0:T(8,128)(2,1)S(1)} %get-tuple-element.34.refs_0_.refs_10_), channel_id=1, source_target_pairs={{0,2},{1,3},{2,0},{3,1},{4,6},{5,7},{6,4},{7,5},{8,10},{9,11},{10,... | collective-permute-start | bytes 589832 | tf_op jit(solution)/shard_map/ppermute | solution.py:33
  20.4 14.7 %collective-permute-start = (bf16[192,512]{1,0:T(8,128)(2,1)S(1)}, bf16[192,512]{1,0:T(8,128)(2,1)S(1)}, u32[]{:S(2)}, u32[]{:S(2)}) collective-permute-start(bf16[192,512]{1,0:T(8,128)(2,1)S(1)} %get-tuple-element.34.refs_0_.refs_10_), channel_id=1, source_target_pairs={{0,1},{1,0},{2,3},{3,2},{4,5},{5,4},{6,7},{7,6},{8,9},{9,8},{10,11... | collective-permute-start | bytes 589832 | tf_op jit(solution)/shard_map/ppermute | solution.py:33
  33.1 10.5 %collective-permute-start.5 = (bf16[192,512]{1,0:T(8,128)(2,1)S(1)}, bf16[192,512]{1,0:T(8,128)(2,1)S(1)}, u32[]{:S(2)}, u32[]{:S(2)}) collective-permute-start(bf16[192,512]{1,0:T(8,128)(2,1)S(1)} %collective-permute-done.3.refs_4_), channel_id=1, source_target_pairs={{0,2},{1,3},{2,0},{3,1},{4,6},{5,7},{6,4},{7,5},{8,10},{9,11},{10,... | collective-permute-start | bytes 589832 | tf_op jit(solution)/shard_map/ppermute | solution.py:33
  33.6 11.5 %collective-permute-start.8 = (bf16[192,512]{1,0:T(8,128)(2,1)S(1)}, bf16[192,512]{1,0:T(8,128)(2,1)S(1)}, u32[]{:S(2)}, u32[]{:S(2)}) collective-permute-start(bf16[192,512]{1,0:T(8,128)(2,1)S(1)} %collective-permute-done.7.refs_0_.refs_8_), channel_id=1, source_target_pairs={{0,1},{1,0},{2,3},{3,2},{4,5},{5,4},{6,7},{7,6},{8,9},{9,8},{10,11... | collective-permute-start | bytes 589832 | tf_op jit(solution)/shard_map/ppermute | solution.py:33
  35.1 10.6 %collective-permute-start.4 = (bf16[192,512]{1,0:T(8,128)(2,1)S(1)}, bf16[192,512]{1,0:T(8,128)(2,1)S(1)}, u32[]{:S(2)}, u32[]{:S(2)}) collective-permute-start(bf16[192,512]{1,0:T(8,128)(2,1)S(1)} %collective-permute-done.3.refs_4_), channel_id=1, source_target_pairs={{0,1},{1,0},{2,3},{3,2},{4,5},{5,4},{6,7},{7,6},{8,9},{9,8},{10,11... | collective-permute-start | bytes 589832 | tf_op jit(solution)/shard_map/ppermute | solution.py:33
  39.4 8.4 %collective-permute-start.2 = (bf16[192,512]{1,0:T(8,128)(2,1)S(1)}, bf16[192,512]{1,0:T(8,128)(2,1)S(1)}, u32[]{:S(2)}, u32[]{:S(2)}) collective-permute-start(bf16[192,512]{1,0:T(8,128)(2,1)S(1)} %collective-permute-done.refs_1_), channel_id=1, source_target_pairs={{0,2},{1,3},{2,0},{3,1},{4,6},{5,7},{6,4},{7,5},{8,10},{9,11},{10,... | collective-permute-start | bytes 589832 | tf_op jit(solution)/shard_map/ppermute | solution.py:33
  45.1 14.0 %collective-permute-start.12 = (bf16[192,512]{1,0:T(8,128)(2,1)S(1)}, bf16[192,512]{1,0:T(8,128)(2,1)S(1)}, u32[]{:S(2)}, u32[]{:S(2)}) collective-permute-start(bf16[192,512]{1,0:T(8,128)(2,1)S(1)} %collective-permute-done.11.refs_4_.refs_12_), channel_id=1, source_target_pairs={{0,1},{1,0},{2,3},{3,2},{4,5},{5,4},{6,7},{7,6},{8,9},{9,8},{10,11... | collective-permute-start | bytes 589832 | tf_op jit(solution)/shard_map/ppermute | solution.py:33
  45.6 13.5 %collective-permute-start.9 = (bf16[192,512]{1,0:T(8,128)(2,1)S(1)}, bf16[192,512]{1,0:T(8,128)(2,1)S(1)}, u32[]{:S(2)}, u32[]{:S(2)}) collective-permute-start(bf16[192,512]{1,0:T(8,128)(2,1)S(1)} %collective-permute-done.7.refs_0_.refs_8_), channel_id=1, source_target_pairs={{0,2},{1,3},{2,0},{3,1},{4,6},{5,7},{6,4},{7,5},{8,10},{9,11},{10,... | collective-permute-start | bytes 589832 | tf_op jit(solution)/shard_map/ppermute | solution.py:33
  47.8 11.3 %collective-permute-start.14 = (bf16[192,512]{1,0:T(8,128)(2,1)S(1)}, bf16[192,512]{1,0:T(8,128)(2,1)S(1)}, u32[]{:S(2)}, u32[]{:S(2)}) collective-permute-start(bf16[192,512]{1,0:T(8,128)(2,1)S(1)} %collective-permute-done.13.refs_6_.refs_14_), channel_id=1, source_target_pairs={{0,1},{1,0},{2,3},{3,2},{4,5},{5,4},{6,7},{7,6},{8,9},{9,8},{10,11... | collective-permute-start | bytes 589832 | tf_op jit(solution)/shard_map/ppermute | solution.py:33
  65.3 8.2 %collective-permute-start.25 = (bf16[208,512]{1,0:T(8,128)(2,1)S(1)}, bf16[208,512]{1,0:T(8,128)(2,1)S(1)}, u32[]{:S(2)}, u32[]{:S(2)}) collective-permute-start(bf16[208,512]{1,0:T(8,128)(2,1)S(1)} %get-tuple-element.36.refs_0_), channel_id=1, source_target_pairs={{0,2},{1,3},{2,0},{3,1},{4,6},{5,7},{6,4},{7,5},{8,10},{9,11},{10,... | collective-permute-start | bytes 638984 | tf_op jit(solution)/shard_map/ppermute | solution.py:33
  65.8 8.2 %collective-permute-start.24 = (bf16[208,512]{1,0:T(8,128)(2,1)S(1)}, bf16[208,512]{1,0:T(8,128)(2,1)S(1)}, u32[]{:S(2)}, u32[]{:S(2)}) collective-permute-start(bf16[208,512]{1,0:T(8,128)(2,1)S(1)} %get-tuple-element.36.refs_0_), channel_id=1, source_target_pairs={{0,1},{1,0},{2,3},{3,2},{4,5},{5,4},{6,7},{7,6},{8,9},{9,8},{10,11... | collective-permute-start | bytes 638984 | tf_op jit(solution)/shard_map/ppermute | solution.py:33
  67.3 9.7 %collective-permute-start.20 = (bf16[208,512]{1,0:T(8,128)(2,1)S(1)}, bf16[208,512]{1,0:T(8,128)(2,1)S(1)}, u32[]{:S(2)}, u32[]{:S(2)}) collective-permute-start(bf16[208,512]{1,0:T(8,128)(2,1)S(1)} %get-tuple-element.36.refs_0_), channel_id=1, source_target_pairs={{0,12},{1,13},{2,14},{3,15},{4,8},{5,9},{6,10},{7,11},{8,4},{9,5},... | collective-permute-start | bytes 638984 | tf_op jit(solution)/shard_map/ppermute | solution.py:33
  71.1 11.7 %collective-permute-start.16 = (bf16[208,512]{1,0:T(8,128)(2,1)S(1)}, bf16[208,512]{1,0:T(8,128)(2,1)S(1)}, u32[]{:S(2)}, u32[]{:S(2)}) collective-permute-start(bf16[208,512]{1,0:T(8,128)(2,1)S(1)} %get-tuple-element.36.refs_0_), channel_id=1, source_target_pairs={{0,8},{1,9},{2,10},{3,11},{4,12},{5,13},{6,14},{7,15},{8,0},{9,1},... | collective-permute-start | bytes 638984 | tf_op jit(solution)/shard_map/ppermute | solution.py:33
  73.5 10.6 %collective-permute-start.29 = (bf16[208,512]{1,0:T(8,128)(2,1)S(1)}, bf16[208,512]{1,0:T(8,128)(2,1)S(1)}, u32[]{:S(2)}, u32[]{:S(2)}) collective-permute-start(bf16[208,512]{1,0:T(8,128)(2,1)S(1)} %collective-permute-done.27.refs_4_), channel_id=1, source_target_pairs={{0,2},{1,3},{2,0},{3,1},{4,6},{5,7},{6,4},{7,5},{8,10},{9,11},{10,... | collective-permute-start | bytes 638984 | tf_op jit(solution)/shard_map/ppermute | solution.py:33
  74.0 11.1 %collective-permute-start.28 = (bf16[208,512]{1,0:T(8,128)(2,1)S(1)}, bf16[208,512]{1,0:T(8,128)(2,1)S(1)}, u32[]{:S(2)}, u32[]{:S(2)}) collective-permute-start(bf16[208,512]{1,0:T(8,128)(2,1)S(1)} %collective-permute-done.27.refs_4_), channel_id=1, source_target_pairs={{0,1},{1,0},{2,3},{3,2},{4,5},{5,4},{6,7},{7,6},{8,9},{9,8},{10,11... | collective-permute-start | bytes 638984 | tf_op jit(solution)/shard_map/ppermute | solution.py:33
  77.0 9.1 %collective-permute-start.26 = (bf16[208,512]{1,0:T(8,128)(2,1)S(1)}, bf16[208,512]{1,0:T(8,128)(2,1)S(1)}, u32[]{:S(2)}, u32[]{:S(2)}) collective-permute-start(bf16[208,512]{1,0:T(8,128)(2,1)S(1)} %collective-permute-done.24.refs_1_), channel_id=1, source_target_pairs={{0,2},{1,3},{2,0},{3,1},{4,6},{5,7},{6,4},{7,5},{8,10},{9,11},{10,... | collective-permute-start | bytes 638984 | tf_op jit(solution)/shard_map/ppermute | solution.py:33
  84.1 8.2 %collective-permute-start.17 = (bf16[208,512]{1,0:T(8,128)(2,1)S(1)}, bf16[208,512]{1,0:T(8,128)(2,1)S(1)}, u32[]{:S(2)}, u32[]{:S(2)}) collective-permute-start(bf16[208,512]{1,0:T(8,128)(2,1)S(1)} %collective-permute-done.16.refs_0_), channel_id=1, source_target_pairs={{0,1},{1,0},{2,3},{3,2},{4,5},{5,4},{6,7},{7,6},{8,9},{9,8},{10,11... | collective-permute-start | bytes 638984 | tf_op jit(solution)/shard_map/ppermute | solution.py:33
  85.1 14.1 %collective-permute-start.30 = (bf16[208,512]{1,0:T(8,128)(2,1)S(1)}, bf16[208,512]{1,0:T(8,128)(2,1)S(1)}, u32[]{:S(2)}, u32[]{:S(2)}) collective-permute-start(bf16[208,512]{1,0:T(8,128)(2,1)S(1)} %collective-permute-done.29.refs_6_), channel_id=1, source_target_pairs={{0,1},{1,0},{2,3},{3,2},{4,5},{5,4},{6,7},{7,6},{8,9},{9,8},{10,11... | collective-permute-start | bytes 638984 | tf_op jit(solution)/shard_map/ppermute | solution.py:33
  86.1 15.5 %collective-permute-start.21 = (bf16[208,512]{1,0:T(8,128)(2,1)S(1)}, bf16[208,512]{1,0:T(8,128)(2,1)S(1)}, u32[]{:S(2)}, u32[]{:S(2)}) collective-permute-start(bf16[208,512]{1,0:T(8,128)(2,1)S(1)} %collective-permute-done.20.refs_4_), channel_id=1, source_target_pairs={{0,1},{1,0},{2,3},{3,2},{4,5},{5,4},{6,7},{7,6},{8,9},{9,8},{10,11... | collective-permute-start | bytes 638984 | tf_op jit(solution)/shard_map/ppermute | solution.py:33
  89.4 12.2 %collective-permute-start.18 = (bf16[208,512]{1,0:T(8,128)(2,1)S(1)}, bf16[208,512]{1,0:T(8,128)(2,1)S(1)}, u32[]{:S(2)}, u32[]{:S(2)}) collective-permute-start(bf16[208,512]{1,0:T(8,128)(2,1)S(1)} %collective-permute-done.16.refs_0_), channel_id=1, source_target_pairs={{0,2},{1,3},{2,0},{3,1},{4,6},{5,7},{6,4},{7,5},{8,10},{9,11},{10,... | collective-permute-start | bytes 638984 | tf_op jit(solution)/shard_map/ppermute | solution.py:33
  92.3 9.4 %collective-permute-start.23 = (bf16[208,512]{1,0:T(8,128)(2,1)S(1)}, bf16[208,512]{1,0:T(8,128)(2,1)S(1)}, u32[]{:S(2)}, u32[]{:S(2)}) collective-permute-start(bf16[208,512]{1,0:T(8,128)(2,1)S(1)} %collective-permute-done.22.refs_6_), channel_id=1, source_target_pairs={{0,1},{1,0},{2,3},{3,2},{4,5},{5,4},{6,7},{7,6},{8,9},{9,8},{10,11... | collective-permute-start | bytes 638984 | tf_op jit(solution)/shard_map/ppermute | solution.py:33
  93.3 8.4 %collective-permute-start.19 = (bf16[208,512]{1,0:T(8,128)(2,1)S(1)}, bf16[208,512]{1,0:T(8,128)(2,1)S(1)}, u32[]{:S(2)}, u32[]{:S(2)}) collective-permute-start(bf16[208,512]{1,0:T(8,128)(2,1)S(1)} %collective-permute-done.17.refs_1_), channel_id=1, source_target_pairs={{0,2},{1,3},{2,0},{3,1},{4,6},{5,7},{6,4},{7,5},{8,10},{9,11},{10,... | collective-permute-start | bytes 638984 | tf_op jit(solution)/shard_map/ppermute | solution.py:33
  121.3 11.2 %collective-permute-start.38 = (bf16[128,512]{1,0:T(8,128)(2,1)S(1)}, bf16[128,512]{1,0:T(8,128)(2,1)S(1)}, u32[]{:S(2)}, u32[]{:S(2)}) collective-permute-start(bf16[128,512]{1,0:T(8,128)(2,1)S(1)} %get-tuple-element.46), channel_id=1, source_target_pairs={{0,1},{1,0},{2,3},{3,2},{4,5},{5,4},{6,7},{7,6},{8,9},{9,8},{10,11... | collective-permute-start | bytes 393224 | tf_op jit(solution)/shard_map/ppermute | solution.py:33
  128.4 21.1 %collective-permute-start.37 = (bf16[128,512]{1,0:T(8,128)(2,1)S(1)}, bf16[128,512]{1,0:T(8,128)(2,1)S(1)}, u32[]{:S(2)}, u32[]{:S(2)}) collective-permute-start(bf16[128,512]{1,0:T(8,128)(2,1)S(1)} %get-tuple-element.44), channel_id=1, source_target_pairs={{0,1},{1,0},{2,3},{3,2},{4,5},{5,4},{6,7},{7,6},{8,9},{9,8},{10,11... | collective-permute-start | bytes 393224 | tf_op jit(solution)/shard_map/ppermute | solution.py:33
  128.9 25.5 %collective-permute-start.43 = (bf16[128,512]{1,0:T(8,128)(2,1)S(1)}, bf16[128,512]{1,0:T(8,128)(2,1)S(1)}, u32[]{:S(2)}, u32[]{:S(2)}) collective-permute-start(bf16[128,512]{1,0:T(8,128)(2,1)S(1)} %get-tuple-element.50), channel_id=1, source_target_pairs={{0,2},{1,3},{2,0},{3,1},{4,6},{5,7},{6,4},{7,5},{8,10},{9,11},{10,... | collective-permute-start | bytes 393224 | tf_op jit(solution)/shard_map/ppermute | solution.py:33
  130.2 27.2 %collective-permute-start.45 = (bf16[128,512]{1,0:T(8,128)(2,1)S(1)}, bf16[128,512]{1,0:T(8,128)(2,1)S(1)}, u32[]{:S(2)}, u32[]{:S(2)}) collective-permute-start(bf16[128,512]{1,0:T(8,128)(2,1)S(1)} %get-tuple-element.52), channel_id=1, source_target_pairs={{0,1},{1,0},{2,3},{3,2},{4,5},{5,4},{6,7},{7,6},{8,9},{9,8},{10,11... | collective-permute-start | bytes 393224 | tf_op jit(solution)/shard_map/ppermute | solution.py:33
  130.9 29.0 %collective-permute-start.51 = (bf16[128,512]{1,0:T(8,128)(2,1)S(1)}, bf16[128,512]{1,0:T(8,128)(2,1)S(1)}, u32[]{:S(2)}, u32[]{:S(2)}) collective-permute-start(bf16[128,512]{1,0:T(8,128)(2,1)S(1)} %get-tuple-element.58), channel_id=1, source_target_pairs={{0,2},{1,3},{2,0},{3,1},{4,6},{5,7},{6,4},{7,5},{8,10},{9,11},{10,... | collective-permute-start | bytes 393224 | tf_op jit(solution)/shard_map/ppermute | solution.py:33
  157.4 7.9 %collective-permute-start.44 = (bf16[128,512]{1,0:T(8,128)(2,1)S(1)}, bf16[128,512]{1,0:T(8,128)(2,1)S(1)}, u32[]{:S(2)}, u32[]{:S(2)}) collective-permute-start(bf16[128,512]{1,0:T(8,128)(2,1)S(1)} %add_convert_fusion.3), channel_id=1, source_target_pairs={{0,8},{1,9},{2,10},{3,11},{4,12},{5,13},{6,14},{7,15},{8,0},{9,1},... | collective-permute-start | bytes 393224 | tf_op jit(solution)/shard_map/ppermute | solution.py:33
  (26 other events, 174.5 us)

commit v3 on v2

v3 whole, which is shorter than its diff:
```python
import functools

import jax
import jax.numpy as jnp
from jax import lax
from jax.experimental import pallas as pl
from jax.experimental.pallas import tpu as pltpu
from jax.sharding import PartitionSpec as P

epsilon = 1e-05
f32 = jnp.float32
bf16 = jnp.bfloat16
words_height = 16
vmem = pl.BlockSpec(memory_space=pltpu.VMEM)
smem = pl.BlockSpec(memory_space=pltpu.SMEM)
main_memory = pl.BlockSpec(memory_space=pltpu.HBM)


def kernel_call(body, name, in_specs, out_shapes, out_specs, scratch, flops, moved):
    return pl.pallas_call(
        body,
        name=name,
        in_specs=in_specs,
        out_shape=out_shapes,
        out_specs=out_specs,
        scratch_shapes=scratch,
        cost_estimate=pl.CostEstimate(flops=flops, bytes_accessed=moved, transcendentals=0),
        compiler_params=pltpu.CompilerParams(vmem_limit_bytes=32 * 1024 * 1024),
    )


def in_main_memory(value):
    return pltpu.with_memory_space_constraint(value, pltpu.HBM)


def swap(value, offset, count):
    return lax.ppermute(value, "vocab", [(i, i ^ offset) for i in range(count)])


def after(value, *earlier):
    return lax.optimization_barrier((value, *earlier))[0]


def gather_pieces(own, count, also=()):
    pieces = {0: own}
    for k in range(4, count, 4):
        pieces[k] = swap(own, k, count)
    for number, base in enumerate(range(0, count, 4)):
        source = after(pieces[base], *also) if base else pieces[base]
        pieces[base + 1] = swap(source, 1, count)
        pieces[base + 2] = swap(source, 2, count)
        if number % 2:
            pieces[base + 3] = swap(pieces[base + 2], 1, count)
        else:
            pieces[base + 3] = swap(pieces[base + 1], 2, count)
    return pieces


def total(*parts):
    result = parts[0].astype(f32)
    for part in parts[1:]:
        result = result + part.astype(f32)
    return result


def scatter_sums(blocks, count):
    bases = list(range(0, count, 4))[::-1]
    far = {base: swap(blocks[base + 3], 1 if (base // 4) % 2 else 2, count) for base in bases}
    terms, near = [], {}
    for base in bases:
        x_part, y_part = blocks[base + 1], blocks[base + 2]
        if (base // 4) % 2:
            y_part = total(y_part, far[base]).astype(bf16)
        else:
            x_part = total(x_part, far[base]).astype(bf16)
        earlier = [far[base]] + near.get(base + 8, [])
        near[base] = [
            swap(after(x_part, *earlier), 1, count),
            swap(after(y_part, *earlier), 2, count),
        ]
        if base:
            terms.append(swap(total(blocks[base], *near[base]).astype(bf16), base, count))
        else:
            terms.extend((blocks[0], *near[base]))
    return terms


def pull(place, k, tables, buffer, sem):
    height = buffer.shape[0]
    index = place[0] ^ k
    if len(tables) == 1:
        rows = pl.ds(pl.multiple_of(index * height, height), height)
        pltpu.make_async_copy(tables[0].at[rows], buffer, sem).start()
        return
    per_table = tables[0].shape[0] // height
    rows = pl.ds(pl.multiple_of(lax.rem(index, per_table) * height, height), height)
    turn = lax.rem(lax.div(index, per_table) - place[1] + len(tables), len(tables))
    for number, table in enumerate(tables):

        @pl.when(turn == number)
        def _():
            pltpu.make_async_copy(table.at[rows], buffer, sem).start()


def arrived(tables, buffer, sem):
    pltpu.make_async_copy(tables[0].at[pl.ds(0, buffer.shape[0])], buffer, sem).wait()


def as_row(column):
    size = column.shape[0]
    return jnp.transpose(jnp.broadcast_to(column, (size, size)))[:1]


def as_column(row):
    size = row.shape[1]
    return jnp.transpose(jnp.broadcast_to(row, (size, size)))[:, :1]


def words_of(row, first):
    high = row.astype(bf16).astype(f32)
    middle = (row - high).astype(bf16).astype(f32)
    low = row - high - middle
    line = lax.broadcasted_iota(jnp.int32, (words_height, row.shape[1]), 0)
    block = jnp.where(line == first, high, 0.0)
    block = jnp.where(line == first + 1, middle, block)
    return jnp.where(line == first + 2, low, block)


def picked_rows(wanted, pool, offset):
    number = lax.broadcasted_iota(jnp.int32, (wanted.shape[0], pool.shape[0]), 1) + offset
    chosen = jnp.where(number == wanted, 1.0, 0.0).astype(bf16)
    return jnp.dot(chosen, pool, preferred_element_type=f32)


def inputs_kernel(wanted, pool, inputs):
    column = as_column(wanted[...].astype(f32)).astype(jnp.int32)
    inputs[...] = picked_rows(column, pool[0], 0).astype(bf16)


def head_kernel(place, wanted, inputs, gain, *refs):
    pools, (first, tail) = refs[:-2], refs[-2:]
    rows = inputs.shape[0]
    half = rows // 2
    height = pools[0].shape[0]
    count = height * len(pools)
    column = as_column(wanted[...].astype(f32)).astype(jnp.int32)
    turned = lax.rem(column - place[1] * height + count, count)
    value = sum(picked_rows(turned, pool[...], number * height) for number, pool in enumerate(pools))
    target = (value * gain[...].astype(f32)).astype(bf16)
    first[:rows] = inputs[...]
    first[rows:] = target[:half]
    tail[:half] = target[half:]
    tail[half:] = jnp.zeros((words_height, value.shape[1]), bf16)
    squares = as_row(jnp.sum(value * value, axis=1, keepdims=True))
    tail[half:, :rows] = words_of(squares, 3).astype(bf16)


def pull_all(place, order, tables, buffer, sems):
    for slot, k in enumerate(order):
        pull(place, k, tables, buffer.at[slot], sems.at[slot])


def early_trans_kernel(order, late, place, *refs):
    pieces, refs = refs[: len(order)], refs[len(order) :]
    weight, result, late_weight, buffer, sems, late_sems = refs
    rows = result.shape[0]
    pull_all(place, order, [weight], buffer, sems)
    pull_all(place, late, [weight], late_weight, late_sems)
    for slot in range(len(order)):
        arrived([weight], buffer.at[slot], sems.at[slot])
        part = jnp.dot(pieces[slot][:rows], buffer[slot], preferred_element_type=f32)
        if slot:
            result[...] += part
        else:
            result[...] = part
    for slot in range(len(late)):
        arrived([weight], late_weight.at[slot], late_sems.at[slot])


def late_trans_kernel(count, *refs):
    pieces, refs = refs[:count], refs[count:]
    weight, so_far, own, bias, gain, tail, trans, payload = refs
    rows = so_far.shape[0]
    trans[...] = so_far[...] + own[:rows].astype(f32) + bias[...].astype(f32)
    for slot in range(count):
        trans[...] += jnp.dot(pieces[slot][:rows], weight[slot], preferred_element_type=f32)
    value = trans[...]
    payload[:rows] = (value * gain[...].astype(f32)).astype(bf16)
    payload[rows:] = tail[...]
    squares = as_row(jnp.sum(value * value, axis=1, keepdims=True))
    start = payload.shape[0] - words_height
    payload[start:, :rows] = (
        words_of(squares, 0) + tail[-words_height:, :rows].astype(f32)
    ).astype(bf16)


def target_kernel(order, lines, table_count, place, *refs):
    pieces, refs = refs[: len(order)], refs[len(order) :]
    tables, refs = refs[:table_count], refs[table_count:]
    result, blocks, sems = refs
    pull_all(place, order, tables, blocks, sems)
    for slot in range(len(order)):
        arrived(tables, blocks.at[slot], sems.at[slot])
        part = jnp.dot(pieces[slot][lines[0] : lines[1]], blocks[slot], preferred_element_type=f32)
        if slot:
            result[...] += part
        else:
            result[...] = part


def early_logits_kernel(count, *refs):
    pieces, (blocks, result, word_sum) = refs[:count], refs[count:]
    for slot in range(count):
        part = jnp.dot(pieces[slot][...], blocks[slot], preferred_element_type=f32)
        if slot:
            result[...] += part
        else:
            result[...] = part
    word_sum[...] = sum(piece[-words_height:].astype(f32) for piece in pieces)


def late_logits_kernel(first, count, width, *refs):
    pieces, refs = refs[:count], refs[count:]
    blocks, so_far, early_words, target_half, logits, target_logits, stats, scale, acc = refs
    rows = logits.shape[0]
    half = target_half.shape[0]
    acc[...] = so_far[...]
    for slot in range(count):
        acc[...] += jnp.dot(pieces[slot][...], blocks[first + slot], preferred_element_type=f32)
    words = early_words[...] + sum(piece[-words_height:].astype(f32) for piece in pieces)
    words = words[:, :rows]
    trans_scale = lax.rsqrt((words[0:1] + words[1:2] + words[2:3]) / width + epsilon)
    final_scale = lax.rsqrt((words[3:4] + words[4:5] + words[5:6]) / width + epsilon)
    scale[...] = jnp.broadcast_to(trans_scale, scale.shape)
    trans_column, final_column = as_column(trans_scale), as_column(final_scale)
    trans_logits = acc[:rows] * trans_column
    logits[...] = trans_logits
    target_logits[:half] = target_half[...] * final_column[:half]
    target_logits[half:] = acc[rows : rows + rows - half] * final_column[half:]
    target = target_logits[...]
    trans_max = jnp.max(trans_logits, axis=1, keepdims=True)
    target_max = jnp.max(target, axis=1, keepdims=True)
    shifted = trans_logits - trans_max
    trans_exp = jnp.exp(shifted)
    target_exp = jnp.exp(target - target_max)
    columns = (
        trans_max,
        jnp.sum(trans_exp, axis=1, keepdims=True),
        jnp.sum(trans_exp * shifted, axis=1, keepdims=True),
        target_max,
        jnp.sum(target_exp, axis=1, keepdims=True),
        jnp.sum(target_exp * (target - trans_logits), axis=1, keepdims=True),
        jnp.sum(target_exp * shifted, axis=1, keepdims=True),
    )
    lane = lax.broadcasted_iota(jnp.int32, (rows, rows), 1)
    packed = jnp.zeros((rows, rows), f32)
    for number, column in enumerate(columns):
        packed = jnp.where(lane == number, column, packed)
    stats[...] = jnp.transpose(packed)[: stats.shape[0]]


def backward_block(dlogits, block):
    return lax.dot_general(
        dlogits, block, (((1,), (1,)), ((), ())), preferred_element_type=f32
    ).astype(bf16)


def first_backward_kernel(order, blocks, logits, target_logits, *refs):
    stats, (dlogits, info, *outs) = refs[:4], refs[4:]
    every = [part[i] for part in stats for i in range(part.shape[0])]
    top = functools.reduce(jnp.maximum, [s[0:1] for s in every])
    target_top = functools.reduce(jnp.maximum, [s[3:4] for s in every])
    trans_sum = target_sum = kl_sum = trans_dot = target_dot = 0.0
    for s in every:
        drop = s[0:1] - top
        factor = jnp.exp(drop)
        target_factor = jnp.exp(s[3:4] - target_top)
        trans_sum += factor * s[1:2]
        target_sum += target_factor * s[4:5]
        kl_sum += target_factor * s[5:6]
        trans_dot += factor * (s[2:3] + s[1:2] * drop)
        target_dot += target_factor * (s[6:7] + s[4:5] * drop)
    log_sum = top + jnp.log(trans_sum)
    target_log_sum = target_top + jnp.log(target_sum)
    value = (
        jnp.exp(logits[...] - as_column(log_sum))
        - jnp.exp(target_logits[...] - as_column(target_log_sum))
    ).astype(bf16)
    dlogits[...] = value
    line = lax.broadcasted_iota(jnp.int32, info.shape, 0)
    kl_rows = kl_sum / target_sum - (target_log_sum - log_sum)
    info[...] = jnp.where(line == 0, kl_rows, trans_dot / trans_sum - target_dot / target_sum)
    for k, out in zip(order, outs):
        out[...] = backward_block(value, blocks[k])


def later_backward_kernel(order, blocks, dlogits, *outs):
    value = dlogits[...]
    for k, out in zip(order, outs):
        out[...] = backward_block(value, blocks[k])


def weight_kernel(count, term_count, width, place, *refs):
    pieces, refs = refs[:count], refs[count:]
    terms, refs = refs[:term_count], refs[term_count:]
    trans, gain, scale, info, grad_weight, grad_bias, kl, buffer, sems = refs
    rows = trans.shape[0]
    height = buffer.shape[1]
    dnormed = functools.reduce(lambda a, b: a + b, [term[...].astype(f32) for term in terms])
    scale_row = scale[0:1]
    weight_row = scale_row * scale_row * info[1:2] / (width * scale_row)
    dtrans = as_column(scale_row) * (dnormed * gain[...].astype(f32) - trans[...] * as_column(weight_row))
    grad_bias[...] = jnp.sum(dtrans, axis=0, keepdims=True)
    kl[...] = jnp.broadcast_to(jnp.sum(info[0:1], axis=1, keepdims=True) / rows, kl.shape)
    rounded = dtrans.astype(bf16)
    copies = []
    for k in range(count):
        buffer[k] = lax.dot_general(
            pieces[k][:rows], rounded, (((0,), (0,)), ((), ())), preferred_element_type=f32
        ).astype(bf16)
        start = pl.multiple_of((place[0] ^ k) * height, height)
        copies.append(pltpu.make_async_copy(buffer.at[k], grad_weight.at[0, pl.ds(start, height)], sems.at[k]))
        copies[-1].start()
    for copy in copies:
        copy.wait()


def per_device(hidden, final_hidden, row_pick, trans_weight, trans_bias, norm_gain, unembed):
    count = lax.axis_size("vocab")
    sections = lax.axis_size("section")
    me = lax.axis_index("vocab")
    section = lax.axis_index("section")
    place = jnp.stack([me, section]).astype(jnp.int32)
    width, cols = trans_weight.shape[1:]
    rows = row_pick.shape[1]
    half = rows // 2
    weight = trans_weight[0]
    gain = norm_gain[None]
    shape = jax.ShapeDtypeStruct
    entries = unembed.shape[1]
    weight_block = 2 * cols * cols
    table_block = 2 * cols * entries

    def table_scratch(number, columns):
        return [pltpu.VMEM((number, cols, columns), bf16), pltpu.SemaphoreType.DMA((number,))]

    def from_others(value):
        return [
            lax.ppermute(value, "section", [((i + k) % sections, i) for i in range(sections)])
            for k in range(1, sections)
        ]

    final_pools = [final_hidden] + from_others(final_hidden)
    inputs = kernel_call(
        inputs_kernel,
        "inputs",
        [vmem] * 2,
        shape((rows, cols), bf16),
        vmem,
        [],
        0,
        hidden.shape[1] * cols * 2,
    )(row_pick, in_main_memory(hidden))
    first_own, tail = kernel_call(
        head_kernel,
        "head",
        [smem] + [vmem] * (3 + sections),
        (shape((rows + half, cols), bf16), shape((rows - half + words_height, cols), bf16)),
        (vmem, vmem),
        [],
        0,
        6 * rows * cols,
    )(place, row_pick, inputs, gain, *map(in_main_memory, final_pools))
    tables = [unembed] + from_others(after(unembed, first_own))
    first = gather_pieces(first_own, count, tables[1:])

    early = list(range(count // 2))
    late = list(range(count // 2, count))
    every = early + late
    side = len(early)
    so_far, late_weight = kernel_call(
        functools.partial(early_trans_kernel, early, late),
        "trans_early",
        [smem] + [vmem] * side + [main_memory],
        (shape((rows, cols), f32), shape((side, cols, cols), bf16)),
        (vmem, vmem),
        table_scratch(side, cols) + [pltpu.SemaphoreType.DMA((side,))],
        side * rows * weight_block,
        2 * side * weight_block,
    )(place, *[first[k] for k in early], in_main_memory(weight))
    payload_shape = shape((first_own.shape[0] + words_height, cols), bf16)
    trans, second_own = kernel_call(
        functools.partial(late_trans_kernel, side),
        "trans_late",
        [vmem] * (side + 6),
        (shape((rows, cols), f32), payload_shape),
        (vmem, vmem),
        [],
        side * rows * weight_block,
        side * weight_block,
    )(*[first[k] for k in late], late_weight, so_far, first_own, trans_bias, gain, tail)
    second = gather_pieces(second_own, count)

    target_half, blocks_in_order = kernel_call(
        functools.partial(target_kernel, every, (rows, rows + half), sections),
        "target_half",
        [smem] + [vmem] * count + [main_memory] * sections,
        (shape((half, entries), f32), shape((count, cols, entries), bf16)),
        (vmem, vmem),
        [pltpu.SemaphoreType.DMA((count,))],
        count * half * table_block,
        count * table_block,
    )(place, *[first[k] for k in every], *map(in_main_memory, tables))
    height = payload_shape.shape[0]
    so_far, words = kernel_call(
        functools.partial(early_logits_kernel, side),
        "logits_early",
        [vmem] * (side + 1),
        (shape((height, entries), f32), shape((words_height, cols), f32)),
        (vmem, vmem),
        [],
        side * height * table_block,
        side * table_block,
    )(*[second[k] for k in early], blocks_in_order)
    logits, target_logits, stats, scale = kernel_call(
        functools.partial(late_logits_kernel, side, side, width),
        "logits_late",
        [vmem] * (side + 4),
        (shape((rows, entries), f32), shape((rows, entries), f32), shape((8, rows), f32), shape((8, rows), f32)),
        (vmem,) * 4,
        [pltpu.VMEM((height, entries), f32)],
        side * height * table_block,
        side * table_block,
    )(*[second[k] for k in late], blocks_in_order, so_far, words, target_half)

    line_stats = jnp.stack([stats] + [swap(stats, k, count) for k in range(4, count, 4)])
    all_stats = [line_stats] + [swap(line_stats, k, count) for k in (1, 2, 3)]

    blocks = {}
    far = [base + 3 for base in range(0, count, 4)][::-1]
    piece = shape((rows, cols), bf16)
    dlogits, info, *made = kernel_call(
        functools.partial(first_backward_kernel, far),
        "backward_far",
        [vmem] * 7,
        (shape((rows, entries), bf16), shape((8, rows), f32), *[piece] * len(far)),
        (vmem,) * (2 + len(far)),
        [],
        len(far) * rows * table_block,
        len(far) * table_block,
    )(blocks_in_order, logits, target_logits, *all_stats)
    blocks.update(zip(far, made))
    bases = list(range(0, count, 4))[::-1]
    for number, part in enumerate((bases[: len(bases) // 2], bases[len(bases) // 2 :])):
        rest = [base + k for base in part for k in (1, 2, 0)]
        made = kernel_call(
            functools.partial(later_backward_kernel, rest),
            "backward_near_%d" % number,
            [vmem] * 2,
            tuple([piece] * len(rest)),
            (vmem,) * len(rest),
            [],
            len(rest) * rows * table_block,
            len(rest) * table_block,
        )(blocks_in_order, dlogits)
        blocks.update(zip(rest, made))
    terms = scatter_sums(blocks, count)

    grad_weight, grad_bias, kl = kernel_call(
        functools.partial(weight_kernel, count, len(terms), width),
        "grad_weight",
        [smem] + [vmem] * (count + len(terms) + 4),
        (shape((1, width, cols), bf16), shape((1, cols), f32), shape((1, rows), f32)),
        (main_memory, vmem, vmem),
        table_scratch(count, cols),
        count * rows * weight_block,
        count * weight_block,
    )(place, *[first[k] for k in range(count)], *terms, trans, gain, scale, info)
    return grad_weight, grad_bias, kl[0, :1]


def solution(mesh):
    placed = (
        P("section", None, "vocab"),
        P("section", "vocab"),
        P("section", None),
        P("section", None, "vocab"),
        P("section", "vocab"),
        P("vocab"),
        P("section", "vocab"),
    )
    return jax.shard_map(
        per_device,
        mesh=mesh,
        in_specs=placed,
        out_specs=(P("section", None, "vocab"), P("section", "vocab"), P("section")),
        check_vma=False,
    )
```

time: 171 us -> 144 us (0.84)
  starting transfers between devices: 67.8 us -> 59.7 us
  local copies, waits for them, and re-layouts: 8.47 us -> 2.05 us
  Pallas kernels: 29 us -> 22.8 us
  blocking collectives: 5.17 us -> 0 us
  other arithmetic: 2.43 us -> 0.38 us
    ppermute x51, starting transfers between devices: 67.3 us -> 59.1 us  [swap(): return lax.ppermute(value, 'vocab', [(i, i ^ offset) for i in range(count)])]
    pallas_call x8 -> x10, Pallas kernels: 23.5 us -> 17.7 us  [the longest x1 4.3 us: per_device(): kernel_call(functools.partial(target_kernel, every, (rows, rows + half),...]
    unnamed x12 -> x8, local copies, waits for them, and re-layouts: 6.78 us -> 1.37 us
    all_gather x1 -> x0, blocking collectives: 5.17 us -> none  [per_device(): final_all = lax.all_gather(final_hidden, 'section', axis=0, tiled=True)]
  transfers between devices with their start and end apart: 52 -> 53, of which waited for: 22 -> 23; matrix products, arithmetic and copies ran while one was open for 2% -> 1% of each run, Pallas kernels for 10% -> 9%
where the time goes in v3:
time: 144 us; the launch traced here: 143 us
  starting transfers between devices  59.7 us (41%)
  waiting for transfers between devices  57.7 us (40%)
  Pallas kernels  22.8 us (16%)
  local copies, waits for them, and re-layouts  2.05 us (1%)
    ppermute x51, starting transfers between devices, swap(): return lax.ppermute(value, 'vocab', [(i, i ^ offset) for i in range(count)])  59.1 us
    ppermute x51, waiting for transfers between devices, swap(): return lax.ppermute(value, 'vocab', [(i, i ^ offset) for i in range(count)])  57.7 us
    pallas_call x1, Pallas kernels, per_device(): kernel_call(functools.partial(weight_kernel, count, len(terms), width), '...  5.02 us
    pallas_call x1, Pallas kernels, per_device(): kernel_call(functools.partial(target_kernel, every, (rows, rows + half),...  4.3 us
    pallas_call x1, Pallas kernels, per_device(): kernel_call(functools.partial(early_trans_kernel, early, late), 'trans_ea...  4.16 us
  transfers between devices with their start and end apart: 53, of which 23 were waited for; matrix products, arithmetic and copies ran while one was open for 1% of the time, Pallas kernels for 9%

profile of v3, /device:TPU:0, one launch (start us, length us, event | category | flops | bytes accessed | tf_op | source)
XLA Modules:
  0.0 143.4 jit_solution(5719443669583656448)
XLA Ops:
  6.3 3.0 %collective-permute-start.4 = (bf16[192,512]{1,0:T(8,128)(2,1)S(1)}, bf16[192,512]{1,0:T(8,128)(2,1)S(1)}, u32[]{:S(2)}, u32[]{:S(2)}) collective-permute-start(bf16[192,512]{1,0:T(8,128)(2,1)S(1)} %get-tuple-element.50.refs_0_.refs_10_), channel_id=1, source_target_pairs={{0,4},{1,5},{2,6},{3,7},{4,0},{5,1},{6,2},{7,3},{8,12},{9,13},{10,... | collective-permute-start | bytes 589832 | tf_op jit(solution)/shard_map/ppermute | solution.py:37
  10.8 2.5 %collective-permute-start.13 = (bf16[192,512]{1,0:T(8,128)(2,1)S(1)}, bf16[192,512]{1,0:T(8,128)(2,1)S(1)}, u32[]{:S(2)}, u32[]{:S(2)}) collective-permute-start(bf16[192,512]{1,0:T(8,128)(2,1)S(1)} %get-tuple-element.50.refs_0_.refs_10_), channel_id=1, source_target_pairs={{0,12},{1,13},{2,14},{3,15},{4,8},{5,9},{6,10},{7,11},{8,4},{9,5},... | collective-permute-start | bytes 589832 | tf_op jit(solution)/shard_map/ppermute | solution.py:37
  14.4 1.7 %collective-permute-start.2 = (bf16[192,512]{1,0:T(8,128)(2,1)S(1)}, bf16[192,512]{1,0:T(8,128)(2,1)S(1)}, u32[]{:S(2)}, u32[]{:S(2)}) collective-permute-start(bf16[192,512]{1,0:T(8,128)(2,1)S(1)} %get-tuple-element.50.refs_0_.refs_10_), channel_id=1, source_target_pairs={{0,2},{1,3},{2,0},{3,1},{4,6},{5,7},{6,4},{7,5},{8,10},{9,11},{10,... | collective-permute-start | bytes 589832 | tf_op jit(solution)/shard_map/ppermute | solution.py:37
  16.5 1.7 %collective-permute-start.3 = (bf16[192,512]{1,0:T(8,128)(2,1)S(1)}, bf16[192,512]{1,0:T(8,128)(2,1)S(1)}, u32[]{:S(2)}, u32[]{:S(2)}) collective-permute-start(bf16[192,512]{1,0:T(8,128)(2,1)S(1)} %collective-permute-done.1.refs_1_), channel_id=1, source_target_pairs={{0,2},{1,3},{2,0},{3,1},{4,6},{5,7},{6,4},{7,5},{8,10},{9,11},{10,... | collective-permute-start | bytes 589832 | tf_op jit(solution)/shard_map/ppermute | solution.py:37
  18.2 3.7 %collective-permute-done.13.refs_12_.refs_4_ = bf16[192,512]{1,0:T(8,128)(2,1)S(1)} collective-permute-done((bf16[192,512]{1,0:T(8,128)(2,1)S(1)}, bf16[192,512]{1,0:T(8,128)(2,1)S(1)}, u32[]{:S(2)}, u32[]{:S(2)}) %collective-permute-start.13) | collective-permute-done | bytes 196640 | tf_op jit(solution)/shard_map/ppermute | solution.py:37
  23.3 7.3 %collective-permute-done.9.refs_8_.refs_0_ = bf16[192,512]{1,0:T(8,128)(2,1)S(1)} collective-permute-done((bf16[192,512]{1,0:T(8,128)(2,1)S(1)}, bf16[192,512]{1,0:T(8,128)(2,1)S(1)}, u32[]{:S(2)}, u32[]{:S(2)}) %collective-permute-start.9) | collective-permute-done | bytes 196640 | tf_op jit(solution)/shard_map/ppermute | solution.py:37
  31.1 1.5 %collective-permute-start.15 = (bf16[192,512]{1,0:T(8,128)(2,1)S(1)}, bf16[192,512]{1,0:T(8,128)(2,1)S(1)}, u32[]{:S(2)}, u32[]{:S(2)}) collective-permute-start(bf16[192,512]{1,0:T(8,128)(2,1)S(1)} %collective-permute-done.13.refs_12_.refs_4_), channel_id=1, source_target_pairs={{0,2},{1,3},{2,0},{3,1},{4,6},{5,7},{6,4},{7,5},{8,10},{9,11},{10,... | collective-permute-start | bytes 589832 | tf_op jit(solution)/shard_map/ppermute | solution.py:37
  35.2 3.2 %collective-permute-done.10.refs_9_.refs_1_ = bf16[192,512]{1,0:T(8,128)(2,1)S(1)} collective-permute-done((bf16[192,512]{1,0:T(8,128)(2,1)S(1)}, bf16[192,512]{1,0:T(8,128)(2,1)S(1)}, u32[]{:S(2)}, u32[]{:S(2)}) %collective-permute-start.10) | collective-permute-done | bytes 196640 | tf_op jit(solution)/shard_map/ppermute | solution.py:37
  40.5 2.1 %collective-permute-done.8.refs_7_ = bf16[192,512]{1,0:T(8,128)(2,1)S(1)} collective-permute-done((bf16[192,512]{1,0:T(8,128)(2,1)S(1)}, bf16[192,512]{1,0:T(8,128)(2,1)S(1)}, u32[]{:S(2)}, u32[]{:S(2)}) %collective-permute-start.8) | collective-permute-done | bytes 196640 | tf_op jit(solution)/shard_map/ppermute | solution.py:37
  42.6 4.2 %trans_early.1 = (f32[128,512]{1,0:T(8,128)S(1)}, bf16[8,512,512]{2,1,0:T(8,128)(2,1)S(1)}) custom-call(s32[2]{0:T(128)S(1)} %pad_add_fusion.place, bf16[192,512]{1,0:T(8,128)(2,1)S(1)} %get-tuple-element.50.refs_0_.refs_10_, bf16[192,512]{1,0:T(8,128)(2,1)S(1)} %collective-permute-done.1.refs_1_, bf16[192,512]{1,0:T(8,128)(2,1)S(1)} %collective-permute-done.2.refs_2_, ...), custom_call_target="tpu_custom_call" | custom-call | flops 536870912 | bytes 8388608 | tf_op jit(solution)/shard_map/trans_early/pallas_call | solution.py:381
  46.9 2.1 %collective-permute-done.16.refs_15_.refs_7_ = bf16[192,512]{1,0:T(8,128)(2,1)S(1)} collective-permute-done((bf16[192,512]{1,0:T(8,128)(2,1)S(1)}, bf16[192,512]{1,0:T(8,128)(2,1)S(1)}, u32[]{:S(2)}, u32[]{:S(2)}) %collective-permute-start.16) | collective-permute-done | bytes 196640 | tf_op jit(solution)/shard_map/ppermute | solution.py:37
  49.8 1.7 %collective-permute-start.28 = (bf16[208,512]{1,0:T(8,128)(2,1)S(1)}, bf16[208,512]{1,0:T(8,128)(2,1)S(1)}, u32[]{:S(2)}, u32[]{:S(2)}) collective-permute-start(bf16[208,512]{1,0:T(8,128)(2,1)S(1)} %get-tuple-element.59.refs_0_), channel_id=1, source_target_pairs={{0,4},{1,5},{2,6},{3,7},{4,0},{5,1},{6,2},{7,3},{8,12},{9,13},{10,... | collective-permute-start | bytes 638984 | tf_op jit(solution)/shard_map/ppermute | solution.py:37
  55.4 3.3 %collective-permute-done.28.refs_4_ = bf16[208,512]{1,0:T(8,128)(2,1)S(1)} collective-permute-done((bf16[208,512]{1,0:T(8,128)(2,1)S(1)}, bf16[208,512]{1,0:T(8,128)(2,1)S(1)}, u32[]{:S(2)}, u32[]{:S(2)}) %collective-permute-start.28) | collective-permute-done | bytes 213024 | tf_op jit(solution)/shard_map/ppermute | solution.py:37
  58.7 1.8 %collective-permute-start.30 = (bf16[208,512]{1,0:T(8,128)(2,1)S(1)}, bf16[208,512]{1,0:T(8,128)(2,1)S(1)}, u32[]{:S(2)}, u32[]{:S(2)}) collective-permute-start(bf16[208,512]{1,0:T(8,128)(2,1)S(1)} %collective-permute-done.28.refs_4_), channel_id=1, source_target_pairs={{0,2},{1,3},{2,0},{3,1},{4,6},{5,7},{6,4},{7,5},{8,10},{9,11},{10,... | collective-permute-start | bytes 638984 | tf_op jit(solution)/shard_map/ppermute | solution.py:37
  60.5 2.5 %collective-permute-done.21.refs_4_ = bf16[208,512]{1,0:T(8,128)(2,1)S(1)} collective-permute-done((bf16[208,512]{1,0:T(8,128)(2,1)S(1)}, bf16[208,512]{1,0:T(8,128)(2,1)S(1)}, u32[]{:S(2)}, u32[]{:S(2)}) %collective-permute-start.21) | collective-permute-done | bytes 213024 | tf_op jit(solution)/shard_map/ppermute | solution.py:37
  64.5 5.9 %collective-permute-done.17.refs_0_ = bf16[208,512]{1,0:T(8,128)(2,1)S(1)} collective-permute-done((bf16[208,512]{1,0:T(8,128)(2,1)S(1)}, bf16[208,512]{1,0:T(8,128)(2,1)S(1)}, u32[]{:S(2)}, u32[]{:S(2)}) %collective-permute-start.17) | collective-permute-done | bytes 213024 | tf_op jit(solution)/shard_map/ppermute | solution.py:37
  71.7 1.7 %collective-permute-start.18 = (bf16[208,512]{1,0:T(8,128)(2,1)S(1)}, bf16[208,512]{1,0:T(8,128)(2,1)S(1)}, u32[]{:S(2)}, u32[]{:S(2)}) collective-permute-start(bf16[208,512]{1,0:T(8,128)(2,1)S(1)} %collective-permute-done.17.refs_0_), channel_id=1, source_target_pairs={{0,1},{1,0},{2,3},{3,2},{4,5},{5,4},{6,7},{7,6},{8,9},{9,8},{10,11... | collective-permute-start | bytes 638984 | tf_op jit(solution)/shard_map/ppermute | solution.py:37
  73.8 1.7 %collective-permute-start.22 = (bf16[208,512]{1,0:T(8,128)(2,1)S(1)}, bf16[208,512]{1,0:T(8,128)(2,1)S(1)}, u32[]{:S(2)}, u32[]{:S(2)}) collective-permute-start(bf16[208,512]{1,0:T(8,128)(2,1)S(1)} %collective-permute-done.21.refs_4_), channel_id=1, source_target_pairs={{0,1},{1,0},{2,3},{3,2},{4,5},{5,4},{6,7},{7,6},{8,9},{9,8},{10,11... | collective-permute-start | bytes 638984 | tf_op jit(solution)/shard_map/ppermute | solution.py:37
  75.9 2.5 %collective-permute-done.23.refs_6_ = bf16[208,512]{1,0:T(8,128)(2,1)S(1)} collective-permute-done((bf16[208,512]{1,0:T(8,128)(2,1)S(1)}, bf16[208,512]{1,0:T(8,128)(2,1)S(1)}, u32[]{:S(2)}, u32[]{:S(2)}) %collective-permute-start.23) | collective-permute-done | bytes 213024 | tf_op jit(solution)/shard_map/ppermute | solution.py:37
  80.0 1.6 %collective-permute-start.20 = (bf16[208,512]{1,0:T(8,128)(2,1)S(1)}, bf16[208,512]{1,0:T(8,128)(2,1)S(1)}, u32[]{:S(2)}, u32[]{:S(2)}) collective-permute-start(bf16[208,512]{1,0:T(8,128)(2,1)S(1)} %collective-permute-done.18.refs_1_), channel_id=1, source_target_pairs={{0,2},{1,3},{2,0},{3,1},{4,6},{5,7},{6,4},{7,5},{8,10},{9,11},{10,... | collective-permute-start | bytes 638984 | tf_op jit(solution)/shard_map/ppermute | solution.py:37
  81.5 4.3 %target_half.1 = (f32[64,512]{1,0:T(8,128)S(1)}, bf16[16,512,512]{2,1,0:T(8,128)(2,1)S(1)}) custom-call(s32[2]{0:T(128)S(1)} %pad_add_fusion.place, bf16[192,512]{1,0:T(8,128)(2,1)S(1)} %get-tuple-element.50.refs_0_.refs_10_, bf16[192,512]{1,0:T(8,128)(2,1)S(1)} %collective-permute-done.1.refs_1_, bf16[192,512]{1,0:T(8,128)(2,1)S(1)} %collective-permute-done.2.refs_2_, ...), custom_call_target="tpu_custom_call" | custom-call | flops 536870912 | bytes 8388608 | tf_op jit(solution)/shard_map/target_half/pallas_call | solution.py:404
  87.4 2.3 %collective-permute-done.24.refs_7_ = bf16[208,512]{1,0:T(8,128)(2,1)S(1)} collective-permute-done((bf16[208,512]{1,0:T(8,128)(2,1)S(1)}, bf16[208,512]{1,0:T(8,128)(2,1)S(1)}, u32[]{:S(2)}, u32[]{:S(2)}) %collective-permute-start.24) | collective-permute-done | bytes 213024 | tf_op jit(solution)/shard_map/ppermute | solution.py:37
  91.0 3.2 %collective-permute-start.34 = (f32[8,128]{1,0:T(8,128)S(1)}, f32[8,128]{1,0:T(8,128)S(1)}, u32[]{:S(2)}, u32[]{:S(2)}) collective-permute-start(f32[8,128]{1,0:T(8,128)S(1)} %get-tuple-element.65), channel_id=1, source_target_pairs={{0,12},{1,13},{2,14},{3,15},{4,8},{5,9},{6,10},{7,11},{8,4},{9,5},... | collective-permute-start | bytes 12296 | tf_op jit(solution)/shard_map/ppermute | solution.py:37
  96.4 2.3 %collective-permute-done.33 = f32[8,128]{1,0:T(8,128)S(1)} collective-permute-done((f32[8,128]{1,0:T(8,128)S(1)}, f32[8,128]{1,0:T(8,128)S(1)}, u32[]{:S(2)}, u32[]{:S(2)}) %collective-permute-start.33) | collective-permute-done | bytes 4128 | tf_op jit(solution)/shard_map/ppermute | solution.py:37
  98.7 1.7 %collective-permute-start.37 = (f32[4,8,128]{2,1,0:T(8,128)S(1)}, f32[4,8,128]{2,1,0:T(8,128)S(1)}, u32[]{:S(2)}, u32[]{:S(2)}) collective-permute-start(f32[4,8,128]{2,1,0:T(8,128)S(1)} %pad_maximum_fusion.refs_0_), channel_id=1, source_target_pairs={{0,3},{1,2},{2,1},{3,0},{4,7},{5,6},{6,5},{7,4},{8,11},{9,10},{10,... | collective-permute-start | bytes 49160 | tf_op jit(solution)/shard_map/ppermute | solution.py:37
  104.2 1.7 %collective-permute-done.35.refs_1_ = f32[4,8,128]{2,1,0:T(8,128)S(1)} collective-permute-done((f32[4,8,128]{2,1,0:T(8,128)S(1)}, f32[4,8,128]{2,1,0:T(8,128)S(1)}, u32[]{:S(2)}, u32[]{:S(2)}) %collective-permute-start.35) | collective-permute-done | bytes 16416 | tf_op jit(solution)/shard_map/ppermute | solution.py:37
  107.6 1.8 %collective-permute-start.46 = (bf16[128,512]{1,0:T(8,128)(2,1)S(1)}, bf16[128,512]{1,0:T(8,128)(2,1)S(1)}, u32[]{:S(2)}, u32[]{:S(2)}) collective-permute-start(bf16[128,512]{1,0:T(8,128)(2,1)S(1)} %get-tuple-element.81), channel_id=1, source_target_pairs={{0,1},{1,0},{2,3},{3,2},{4,5},{5,4},{6,7},{7,6},{8,9},{9,8},{10,11... | collective-permute-start | bytes 393224 | tf_op jit(solution)/shard_map/ppermute | solution.py:37
  119.0 3.5 %collective-permute-done.44 = bf16[128,512]{1,0:T(8,128)(2,1)S(1)} collective-permute-done((bf16[128,512]{1,0:T(8,128)(2,1)S(1)}, bf16[128,512]{1,0:T(8,128)(2,1)S(1)}, u32[]{:S(2)}, u32[]{:S(2)}) %collective-permute-start.44) | collective-permute-done | bytes 131104 | tf_op jit(solution)/shard_map/ppermute | solution.py:37
  123.9 2.0 %collective-permute-start.45 = (bf16[128,512]{1,0:T(8,128)(2,1)S(1)}, bf16[128,512]{1,0:T(8,128)(2,1)S(1)}, u32[]{:S(2)}, u32[]{:S(2)}) collective-permute-start(bf16[128,512]{1,0:T(8,128)(2,1)S(1)} %add_convert_fusion.3), channel_id=1, source_target_pairs={{0,8},{1,9},{2,10},{3,11},{4,12},{5,13},{6,14},{7,15},{8,0},{9,1},... | collective-permute-start | bytes 393224 | tf_op jit(solution)/shard_map/ppermute | solution.py:37
  128.5 2.4 %collective-permute-done.47 = bf16[128,512]{1,0:T(8,128)(2,1)S(1)} collective-permute-done((bf16[128,512]{1,0:T(8,128)(2,1)S(1)}, bf16[128,512]{1,0:T(8,128)(2,1)S(1)}, u32[]{:S(2)}, u32[]{:S(2)}) %collective-permute-start.47) | collective-permute-done | bytes 131104 | tf_op jit(solution)/shard_map/ppermute | solution.py:37
  132.6 5.2 %collective-permute-done.41.refs_16_ = bf16[128,512]{1,0:T(8,128)(2,1)S(1)} collective-permute-done((bf16[128,512]{1,0:T(8,128)(2,1)S(1)}, bf16[128,512]{1,0:T(8,128)(2,1)S(1)}, u32[]{:S(2)}, u32[]{:S(2)}) %collective-permute-start.41) | collective-permute-done | bytes 131104 | tf_op jit(solution)/shard_map/ppermute | solution.py:37
  138.4 5.0 %grad_weight.1 = (bf16[1,8192,512]{2,1,0:T(8,128)(2,1)}, f32[1,512]{1,0:T(1,128)}, f32[1,128]{1,0:T(1,128)}) custom-call(s32[2]{0:T(128)S(1)} %pad_add_fusion.place, bf16[192,512]{1,0:T(8,128)(2,1)S(1)} %get-tuple-element.50.refs_0_.refs_10_, bf16[192,512]{1,0:T(8,128)(2,1)S(1)} %collective-permute-done.1.refs_1_, ...), custom_call_target="tpu_custom_call" | custom-call | flops 1073741824 | bytes 8388608 | tf_op jit(solution)/shard_map/grad_weight/pallas_call | solution.py:469
  (103 shorter events, 51.7 us)
Async XLA Ops:
  6.2 9.9 %collective-permute-start.5 = (bf16[4096,512]{1,0:T(8,128)(2,1)}, bf16[4096,512]{1,0:T(8,128)(2,1)S(1)}, u32[]{:S(2)}, u32[]{:S(2)}) collective-permute-start(bf16[4096,512]{1,0:T(8,128)(2,1)} %refs_16_.1), channel_id=1, source_target_pairs={{16,0},{0,16},{17,1},{1,17},{18,2},{2,18},{19,3},{3,19},{20,4},{4,... | collective-permute-start | bytes 12582920 | tf_op jit(solution)/shard_map/ppermute | solution.py:349
  10.8 11.0 %collective-permute-start.13 = (bf16[192,512]{1,0:T(8,128)(2,1)S(1)}, bf16[192,512]{1,0:T(8,128)(2,1)S(1)}, u32[]{:S(2)}, u32[]{:S(2)}) collective-permute-start(bf16[192,512]{1,0:T(8,128)(2,1)S(1)} %get-tuple-element.50.refs_0_.refs_10_), channel_id=1, source_target_pairs={{0,12},{1,13},{2,14},{3,15},{4,8},{5,9},{6,10},{7,11},{8,4},{9,5},... | collective-permute-start | bytes 589832 | tf_op jit(solution)/shard_map/ppermute | solution.py:37
  13.3 17.3 %collective-permute-start.9 = (bf16[192,512]{1,0:T(8,128)(2,1)S(1)}, bf16[192,512]{1,0:T(8,128)(2,1)S(1)}, u32[]{:S(2)}, u32[]{:S(2)}) collective-permute-start(bf16[192,512]{1,0:T(8,128)(2,1)S(1)} %get-tuple-element.50.refs_0_.refs_10_), channel_id=1, source_target_pairs={{0,8},{1,9},{2,10},{3,11},{4,12},{5,13},{6,14},{7,15},{8,0},{9,1},... | collective-permute-start | bytes 589832 | tf_op jit(solution)/shard_map/ppermute | solution.py:37
  14.4 16.7 %collective-permute-start.2 = (bf16[192,512]{1,0:T(8,128)(2,1)S(1)}, bf16[192,512]{1,0:T(8,128)(2,1)S(1)}, u32[]{:S(2)}, u32[]{:S(2)}) collective-permute-start(bf16[192,512]{1,0:T(8,128)(2,1)S(1)} %get-tuple-element.50.refs_0_.refs_10_), channel_id=1, source_target_pairs={{0,2},{1,3},{2,0},{3,1},{4,6},{5,7},{6,4},{7,5},{8,10},{9,11},{10,... | collective-permute-start | bytes 589832 | tf_op jit(solution)/shard_map/ppermute | solution.py:37
  16.1 16.5 %collective-permute-start.7 = (bf16[192,512]{1,0:T(8,128)(2,1)S(1)}, bf16[192,512]{1,0:T(8,128)(2,1)S(1)}, u32[]{:S(2)}, u32[]{:S(2)}) collective-permute-start(bf16[192,512]{1,0:T(8,128)(2,1)S(1)} %collective-permute-done.4.refs_4_), channel_id=1, source_target_pairs={{0,2},{1,3},{2,0},{3,1},{4,6},{5,7},{6,4},{7,5},{8,10},{9,11},{10,... | collective-permute-start | bytes 589832 | tf_op jit(solution)/shard_map/ppermute | solution.py:37
  16.5 17.7 %collective-permute-start.3 = (bf16[192,512]{1,0:T(8,128)(2,1)S(1)}, bf16[192,512]{1,0:T(8,128)(2,1)S(1)}, u32[]{:S(2)}, u32[]{:S(2)}) collective-permute-start(bf16[192,512]{1,0:T(8,128)(2,1)S(1)} %collective-permute-done.1.refs_1_), channel_id=1, source_target_pairs={{0,2},{1,3},{2,0},{3,1},{4,6},{5,7},{6,4},{7,5},{8,10},{9,11},{10,... | collective-permute-start | bytes 589832 | tf_op jit(solution)/shard_map/ppermute | solution.py:37
  21.8 12.8 %collective-permute-start.6 = (bf16[192,512]{1,0:T(8,128)(2,1)S(1)}, bf16[192,512]{1,0:T(8,128)(2,1)S(1)}, u32[]{:S(2)}, u32[]{:S(2)}) collective-permute-start(bf16[192,512]{1,0:T(8,128)(2,1)S(1)} %collective-permute-done.4.refs_4_), channel_id=1, source_target_pairs={{0,1},{1,0},{2,3},{3,2},{4,5},{5,4},{6,7},{7,6},{8,9},{9,8},{10,11... | collective-permute-start | bytes 589832 | tf_op jit(solution)/shard_map/ppermute | solution.py:37
  31.1 8.8 %collective-permute-start.15 = (bf16[192,512]{1,0:T(8,128)(2,1)S(1)}, bf16[192,512]{1,0:T(8,128)(2,1)S(1)}, u32[]{:S(2)}, u32[]{:S(2)}) collective-permute-start(bf16[192,512]{1,0:T(8,128)(2,1)S(1)} %collective-permute-done.13.refs_12_.refs_4_), channel_id=1, source_target_pairs={{0,2},{1,3},{2,0},{3,1},{4,6},{5,7},{6,4},{7,5},{8,10},{9,11},{10,... | collective-permute-start | bytes 589832 | tf_op jit(solution)/shard_map/ppermute | solution.py:37
  32.7 10.0 %collective-permute-start.8 = (bf16[192,512]{1,0:T(8,128)(2,1)S(1)}, bf16[192,512]{1,0:T(8,128)(2,1)S(1)}, u32[]{:S(2)}, u32[]{:S(2)}) collective-permute-start(bf16[192,512]{1,0:T(8,128)(2,1)S(1)} %collective-permute-done.7.refs_6_), channel_id=1, source_target_pairs={{0,1},{1,0},{2,3},{3,2},{4,5},{5,4},{6,7},{7,6},{8,9},{9,8},{10,11... | collective-permute-start | bytes 589832 | tf_op jit(solution)/shard_map/ppermute | solution.py:37
  34.2 12.7 %collective-permute-start.11 = (bf16[192,512]{1,0:T(8,128)(2,1)S(1)}, bf16[192,512]{1,0:T(8,128)(2,1)S(1)}, u32[]{:S(2)}, u32[]{:S(2)}) collective-permute-start(bf16[192,512]{1,0:T(8,128)(2,1)S(1)} %collective-permute-done.9.refs_8_.refs_0_), channel_id=1, source_target_pairs={{0,2},{1,3},{2,0},{3,1},{4,6},{5,7},{6,4},{7,5},{8,10},{9,11},{10,... | collective-permute-start | bytes 589832 | tf_op jit(solution)/shard_map/ppermute | solution.py:37
  34.7 12.2 %collective-permute-start.14 = (bf16[192,512]{1,0:T(8,128)(2,1)S(1)}, bf16[192,512]{1,0:T(8,128)(2,1)S(1)}, u32[]{:S(2)}, u32[]{:S(2)}) collective-permute-start(bf16[192,512]{1,0:T(8,128)(2,1)S(1)} %collective-permute-done.13.refs_12_.refs_4_), channel_id=1, source_target_pairs={{0,1},{1,0},{2,3},{3,2},{4,5},{5,4},{6,7},{7,6},{8,9},{9,8},{10,11... | collective-permute-start | bytes 589832 | tf_op jit(solution)/shard_map/ppermute | solution.py:37
  38.4 8.4 %collective-permute-start.12 = (bf16[192,512]{1,0:T(8,128)(2,1)S(1)}, bf16[192,512]{1,0:T(8,128)(2,1)S(1)}, u32[]{:S(2)}, u32[]{:S(2)}) collective-permute-start(bf16[192,512]{1,0:T(8,128)(2,1)S(1)} %collective-permute-done.10.refs_9_.refs_1_), channel_id=1, source_target_pairs={{0,2},{1,3},{2,0},{3,1},{4,6},{5,7},{6,4},{7,5},{8,10},{9,11},{10,... | collective-permute-start | bytes 589832 | tf_op jit(solution)/shard_map/ppermute | solution.py:37
  40.0 9.0 %collective-permute-start.16 = (bf16[192,512]{1,0:T(8,128)(2,1)S(1)}, bf16[192,512]{1,0:T(8,128)(2,1)S(1)}, u32[]{:S(2)}, u32[]{:S(2)}) collective-permute-start(bf16[192,512]{1,0:T(8,128)(2,1)S(1)} %collective-permute-done.15.refs_14_.refs_6_), channel_id=1, source_target_pairs={{0,1},{1,0},{2,3},{3,2},{4,5},{5,4},{6,7},{7,6},{8,9},{9,8},{10,11... | collective-permute-start | bytes 589832 | tf_op jit(solution)/shard_map/ppermute | solution.py:37
  49.8 8.9 %collective-permute-start.28 = (bf16[208,512]{1,0:T(8,128)(2,1)S(1)}, bf16[208,512]{1,0:T(8,128)(2,1)S(1)}, u32[]{:S(2)}, u32[]{:S(2)}) collective-permute-start(bf16[208,512]{1,0:T(8,128)(2,1)S(1)} %get-tuple-element.59.refs_0_), channel_id=1, source_target_pairs={{0,4},{1,5},{2,6},{3,7},{4,0},{5,1},{6,2},{7,3},{8,12},{9,13},{10,... | collective-permute-start | bytes 638984 | tf_op jit(solution)/shard_map/ppermute | solution.py:37
  51.5 9.0 %collective-permute-start.25 = (bf16[208,512]{1,0:T(8,128)(2,1)S(1)}, bf16[208,512]{1,0:T(8,128)(2,1)S(1)}, u32[]{:S(2)}, u32[]{:S(2)}) collective-permute-start(bf16[208,512]{1,0:T(8,128)(2,1)S(1)} %get-tuple-element.59.refs_0_), channel_id=1, source_target_pairs={{0,1},{1,0},{2,3},{3,2},{4,5},{5,4},{6,7},{7,6},{8,9},{9,8},{10,11... | collective-permute-start | bytes 638984 | tf_op jit(solution)/shard_map/ppermute | solution.py:37
  52.0 11.0 %collective-permute-start.21 = (bf16[208,512]{1,0:T(8,128)(2,1)S(1)}, bf16[208,512]{1,0:T(8,128)(2,1)S(1)}, u32[]{:S(2)}, u32[]{:S(2)}) collective-permute-start(bf16[208,512]{1,0:T(8,128)(2,1)S(1)} %get-tuple-element.59.refs_0_), channel_id=1, source_target_pairs={{0,12},{1,13},{2,14},{3,15},{4,8},{5,9},{6,10},{7,11},{8,4},{9,5},... | collective-permute-start | bytes 638984 | tf_op jit(solution)/shard_map/ppermute | solution.py:37
  53.5 16.9 %collective-permute-start.17 = (bf16[208,512]{1,0:T(8,128)(2,1)S(1)}, bf16[208,512]{1,0:T(8,128)(2,1)S(1)}, u32[]{:S(2)}, u32[]{:S(2)}) collective-permute-start(bf16[208,512]{1,0:T(8,128)(2,1)S(1)} %get-tuple-element.59.refs_0_), channel_id=1, source_target_pairs={{0,8},{1,9},{2,10},{3,11},{4,12},{5,13},{6,14},{7,15},{8,0},{9,1},... | collective-permute-start | bytes 638984 | tf_op jit(solution)/shard_map/ppermute | solution.py:37
  53.9 17.9 %collective-permute-start.26 = (bf16[208,512]{1,0:T(8,128)(2,1)S(1)}, bf16[208,512]{1,0:T(8,128)(2,1)S(1)}, u32[]{:S(2)}, u32[]{:S(2)}) collective-permute-start(bf16[208,512]{1,0:T(8,128)(2,1)S(1)} %get-tuple-element.59.refs_0_), channel_id=1, source_target_pairs={{0,2},{1,3},{2,0},{3,1},{4,6},{5,7},{6,4},{7,5},{8,10},{9,11},{10,... | collective-permute-start | bytes 638984 | tf_op jit(solution)/shard_map/ppermute | solution.py:37
  58.7 14.7 %collective-permute-start.30 = (bf16[208,512]{1,0:T(8,128)(2,1)S(1)}, bf16[208,512]{1,0:T(8,128)(2,1)S(1)}, u32[]{:S(2)}, u32[]{:S(2)}) collective-permute-start(bf16[208,512]{1,0:T(8,128)(2,1)S(1)} %collective-permute-done.28.refs_4_), channel_id=1, source_target_pairs={{0,2},{1,3},{2,0},{3,1},{4,6},{5,7},{6,4},{7,5},{8,10},{9,11},{10,... | collective-permute-start | bytes 638984 | tf_op jit(solution)/shard_map/ppermute | solution.py:37
  60.5 13.2 %collective-permute-start.29 = (bf16[208,512]{1,0:T(8,128)(2,1)S(1)}, bf16[208,512]{1,0:T(8,128)(2,1)S(1)}, u32[]{:S(2)}, u32[]{:S(2)}) collective-permute-start(bf16[208,512]{1,0:T(8,128)(2,1)S(1)} %collective-permute-done.28.refs_4_), channel_id=1, source_target_pairs={{0,1},{1,0},{2,3},{3,2},{4,5},{5,4},{6,7},{7,6},{8,9},{9,8},{10,11... | collective-permute-start | bytes 638984 | tf_op jit(solution)/shard_map/ppermute | solution.py:37
  63.0 12.4 %collective-permute-start.27 = (bf16[208,512]{1,0:T(8,128)(2,1)S(1)}, bf16[208,512]{1,0:T(8,128)(2,1)S(1)}, u32[]{:S(2)}, u32[]{:S(2)}) collective-permute-start(bf16[208,512]{1,0:T(8,128)(2,1)S(1)} %collective-permute-done.25.refs_1_), channel_id=1, source_target_pairs={{0,2},{1,3},{2,0},{3,1},{4,6},{5,7},{6,4},{7,5},{8,10},{9,11},{10,... | collective-permute-start | bytes 638984 | tf_op jit(solution)/shard_map/ppermute | solution.py:37
  73.4 12.4 %collective-permute-start.31 = (bf16[208,512]{1,0:T(8,128)(2,1)S(1)}, bf16[208,512]{1,0:T(8,128)(2,1)S(1)}, u32[]{:S(2)}, u32[]{:S(2)}) collective-permute-start(bf16[208,512]{1,0:T(8,128)(2,1)S(1)} %collective-permute-done.30.refs_6_), channel_id=1, source_target_pairs={{0,1},{1,0},{2,3},{3,2},{4,5},{5,4},{6,7},{7,6},{8,9},{9,8},{10,11... | collective-permute-start | bytes 638984 | tf_op jit(solution)/shard_map/ppermute | solution.py:37
  73.8 13.6 %collective-permute-start.22 = (bf16[208,512]{1,0:T(8,128)(2,1)S(1)}, bf16[208,512]{1,0:T(8,128)(2,1)S(1)}, u32[]{:S(2)}, u32[]{:S(2)}) collective-permute-start(bf16[208,512]{1,0:T(8,128)(2,1)S(1)} %collective-permute-done.21.refs_4_), channel_id=1, source_target_pairs={{0,1},{1,0},{2,3},{3,2},{4,5},{5,4},{6,7},{7,6},{8,9},{9,8},{10,11... | collective-permute-start | bytes 638984 | tf_op jit(solution)/shard_map/ppermute | solution.py:37
  75.4 12.0 %collective-permute-start.19 = (bf16[208,512]{1,0:T(8,128)(2,1)S(1)}, bf16[208,512]{1,0:T(8,128)(2,1)S(1)}, u32[]{:S(2)}, u32[]{:S(2)}) collective-permute-start(bf16[208,512]{1,0:T(8,128)(2,1)S(1)} %collective-permute-done.17.refs_0_), channel_id=1, source_target_pairs={{0,2},{1,3},{2,0},{3,1},{4,6},{5,7},{6,4},{7,5},{8,10},{9,11},{10,... | collective-permute-start | bytes 638984 | tf_op jit(solution)/shard_map/ppermute | solution.py:37
  78.4 11.2 %collective-permute-start.24 = (bf16[208,512]{1,0:T(8,128)(2,1)S(1)}, bf16[208,512]{1,0:T(8,128)(2,1)S(1)}, u32[]{:S(2)}, u32[]{:S(2)}) collective-permute-start(bf16[208,512]{1,0:T(8,128)(2,1)S(1)} %collective-permute-done.23.refs_6_), channel_id=1, source_target_pairs={{0,1},{1,0},{2,3},{3,2},{4,5},{5,4},{6,7},{7,6},{8,9},{9,8},{10,11... | collective-permute-start | bytes 638984 | tf_op jit(solution)/shard_map/ppermute | solution.py:37
  80.0 9.7 %collective-permute-start.20 = (bf16[208,512]{1,0:T(8,128)(2,1)S(1)}, bf16[208,512]{1,0:T(8,128)(2,1)S(1)}, u32[]{:S(2)}, u32[]{:S(2)}) collective-permute-start(bf16[208,512]{1,0:T(8,128)(2,1)S(1)} %collective-permute-done.18.refs_1_), channel_id=1, source_target_pairs={{0,2},{1,3},{2,0},{3,1},{4,6},{5,7},{6,4},{7,5},{8,10},{9,11},{10,... | collective-permute-start | bytes 638984 | tf_op jit(solution)/shard_map/ppermute | solution.py:37
  107.6 9.2 %collective-permute-start.46 = (bf16[128,512]{1,0:T(8,128)(2,1)S(1)}, bf16[128,512]{1,0:T(8,128)(2,1)S(1)}, u32[]{:S(2)}, u32[]{:S(2)}) collective-permute-start(bf16[128,512]{1,0:T(8,128)(2,1)S(1)} %get-tuple-element.81), channel_id=1, source_target_pairs={{0,1},{1,0},{2,3},{3,2},{4,5},{5,4},{6,7},{7,6},{8,9},{9,8},{10,11... | collective-permute-start | bytes 393224 | tf_op jit(solution)/shard_map/ppermute | solution.py:37
  114.8 11.1 %collective-permute-start.40 = (bf16[128,512]{1,0:T(8,128)(2,1)S(1)}, bf16[128,512]{1,0:T(8,128)(2,1)S(1)}, u32[]{:S(2)}, u32[]{:S(2)}) collective-permute-start(bf16[128,512]{1,0:T(8,128)(2,1)S(1)} %add_convert_fusion.6), channel_id=1, source_target_pairs={{0,2},{1,3},{2,0},{3,1},{4,6},{5,7},{6,4},{7,5},{8,10},{9,11},{10,... | collective-permute-start | bytes 393224 | tf_op jit(solution)/shard_map/ppermute | solution.py:37
  116.8 9.1 %collective-permute-start.39 = (bf16[128,512]{1,0:T(8,128)(2,1)S(1)}, bf16[128,512]{1,0:T(8,128)(2,1)S(1)}, u32[]{:S(2)}, u32[]{:S(2)}) collective-permute-start(bf16[128,512]{1,0:T(8,128)(2,1)S(1)} %get-tuple-element.70), channel_id=1, source_target_pairs={{0,1},{1,0},{2,3},{3,2},{4,5},{5,4},{6,7},{7,6},{8,9},{9,8},{10,11... | collective-permute-start | bytes 393224 | tf_op jit(solution)/shard_map/ppermute | solution.py:37
  122.5 10.0 %collective-permute-start.51 = (bf16[128,512]{1,0:T(8,128)(2,1)S(1)}, bf16[128,512]{1,0:T(8,128)(2,1)S(1)}, u32[]{:S(2)}, u32[]{:S(2)}) collective-permute-start(bf16[128,512]{1,0:T(8,128)(2,1)S(1)} %add_convert_fusion), channel_id=1, source_target_pairs={{0,1},{1,0},{2,3},{3,2},{4,5},{5,4},{6,7},{7,6},{8,9},{9,8},{10,11... | collective-permute-start | bytes 393224 | tf_op jit(solution)/shard_map/ppermute | solution.py:37
  123.3 9.3 %collective-permute-start.52 = (bf16[128,512]{1,0:T(8,128)(2,1)S(1)}, bf16[128,512]{1,0:T(8,128)(2,1)S(1)}, u32[]{:S(2)}, u32[]{:S(2)}) collective-permute-start(bf16[128,512]{1,0:T(8,128)(2,1)S(1)} %get-tuple-element.90), channel_id=1, source_target_pairs={{0,2},{1,3},{2,0},{3,1},{4,6},{5,7},{6,4},{7,5},{8,10},{9,11},{10,... | collective-permute-start | bytes 393224 | tf_op jit(solution)/shard_map/ppermute | solution.py:37
  123.9 8.7 %collective-permute-start.45 = (bf16[128,512]{1,0:T(8,128)(2,1)S(1)}, bf16[128,512]{1,0:T(8,128)(2,1)S(1)}, u32[]{:S(2)}, u32[]{:S(2)}) collective-permute-start(bf16[128,512]{1,0:T(8,128)(2,1)S(1)} %add_convert_fusion.3), channel_id=1, source_target_pairs={{0,8},{1,9},{2,10},{3,11},{4,12},{5,13},{6,14},{7,15},{8,0},{9,1},... | collective-permute-start | bytes 393224 | tf_op jit(solution)/shard_map/ppermute | solution.py:37
  (25 other events, 241.7 us)

commit v4 on v3

--- a/solution.py
+++ b/solution.py
@@ -13,6 +13,7 @@
 words_height = 16
 vmem = pl.BlockSpec(memory_space=pltpu.VMEM)
 smem = pl.BlockSpec(memory_space=pltpu.SMEM)
+anywhere = pl.BlockSpec(memory_space=pl.ANY)
 main_memory = pl.BlockSpec(memory_space=pltpu.HBM)
 
 
@@ -41,19 +42,25 @@
     return lax.optimization_barrier((value, *earlier))[0]
 
 
-def gather_pieces(own, count, also=()):
+def gather_pieces(own, count, before_last, make):
     pieces = {0: own}
-    for k in range(4, count, 4):
+    line = list(range(4, count, 4))
+    for k in line[:-1]:
         pieces[k] = swap(own, k, count)
-    for number, base in enumerate(range(0, count, 4)):
-        source = after(pieces[base], *also) if base else pieces[base]
-        pieces[base + 1] = swap(source, 1, count)
+    pieces[line[-1]] = swap(after(own, *before_last) if before_last else own, line[-1], count)
+    made = None
+    for base in [0] + line:
+        pieces[base + 1] = swap(pieces[base], 1, count)
+        source = pieces[base]
+        if make and base == line[len(line) // 2]:
+            made = make()
+            source = after(source, made)
         pieces[base + 2] = swap(source, 2, count)
-        if number % 2:
+        if (base // 4) % 2:
             pieces[base + 3] = swap(pieces[base + 2], 1, count)
         else:
             pieces[base + 3] = swap(pieces[base + 1], 2, count)
-    return pieces
+    return pieces, made
 
 
 def total(*parts):
@@ -65,19 +72,23 @@
 
 def scatter_sums(blocks, count):
     bases = list(range(0, count, 4))[::-1]
-    far = {base: swap(blocks[base + 3], 1 if (base // 4) % 2 else 2, count) for base in bases}
-    terms, near = [], {}
+    far, near, terms = {}, {}, []
+    for base in bases:
+        offset = 3 if base == bases[0] else 1 if (base // 4) % 2 else 2
+        far[base] = swap(blocks[base + 3], offset, count)
     for base in bases:
         x_part, y_part = blocks[base + 1], blocks[base + 2]
-        if (base // 4) % 2:
-            y_part = total(y_part, far[base]).astype(bf16)
+        if base == bases[0]:
+            near[base] = [far[base], swap(x_part, 1, count), swap(y_part, 2, count)]
         else:
-            x_part = total(x_part, far[base]).astype(bf16)
-        earlier = [far[base]] + near.get(base + 8, [])
-        near[base] = [
-            swap(after(x_part, *earlier), 1, count),
-            swap(after(y_part, *earlier), 2, count),
-        ]
+            if (base // 4) % 2:
+                y_part = total(y_part, far[base]).astype(bf16)
+            else:
+                x_part = total(x_part, far[base]).astype(bf16)
+            earlier = near.get(base + 8, [])
+            if earlier:
+                x_part, y_part = after(x_part, *earlier), after(y_part, *earlier)
+            near[base] = [swap(x_part, 1, count), swap(y_part, 2, count)]
         if base:
             terms.append(swap(total(blocks[base], *near[base]).astype(bf16), base, count))
         else:
@@ -137,22 +148,18 @@
     inputs[...] = picked_rows(column, pool[0], 0).astype(bf16)
 
 
-def head_kernel(place, wanted, inputs, gain, *refs):
-    pools, (first, tail) = refs[:-2], refs[-2:]
-    rows = inputs.shape[0]
-    half = rows // 2
+def target_kernel(place, wanted, gain, *refs):
+    pools, tail = refs[:-1], refs[-1]
     height = pools[0].shape[0]
     count = height * len(pools)
     column = as_column(wanted[...].astype(f32)).astype(jnp.int32)
+    rows = column.shape[0]
     turned = lax.rem(column - place[1] * height + count, count)
     value = sum(picked_rows(turned, pool[...], number * height) for number, pool in enumerate(pools))
-    target = (value * gain[...].astype(f32)).astype(bf16)
-    first[:rows] = inputs[...]
-    first[rows:] = target[:half]
-    tail[:half] = target[half:]
-    tail[half:] = jnp.zeros((words_height, value.shape[1]), bf16)
+    tail[:rows] = (value * gain[...].astype(f32).reshape(1, -1)).astype(bf16)
+    tail[rows:] = jnp.zeros((words_height, value.shape[1]), bf16)
     squares = as_row(jnp.sum(value * value, axis=1, keepdims=True))
-    tail[half:, :rows] = words_of(squares, 3).astype(bf16)
+    tail[rows:, :rows] = words_of(squares, 3).astype(bf16)
 
 
 def pull_all(place, order, tables, buffer, sems):
@@ -160,32 +167,34 @@
         pull(place, k, tables, buffer.at[slot], sems.at[slot])
 
 
-def early_trans_kernel(order, late, place, *refs):
-    pieces, refs = refs[: len(order)], refs[len(order) :]
-    weight, result, late_weight, buffer, sems, late_sems = refs
+def fetch_kernel(order, table_count, place, *refs):
+    tables, (blocks, sems) = refs[:table_count], refs[table_count:]
+    pull_all(place, order, tables, blocks, sems)
+    for slot in range(len(order)):
+        arrived(tables, blocks.at[slot], sems.at[slot])
+
+
+def add_products(result, pieces, lines, blocks, first):
+    for slot, piece in enumerate(pieces):
+        part = jnp.dot(piece[lines[0] : lines[1]], blocks[first + slot], preferred_element_type=f32)
+        result[...] += part
+
+
+def early_trans_kernel(count, *refs):
+    pieces, (weight, own, bias, result) = refs[:count], refs[count:]
     rows = result.shape[0]
-    pull_all(place, order, [weight], buffer, sems)
-    pull_all(place, late, [weight], late_weight, late_sems)
-    for slot in range(len(order)):
-        arrived([weight], buffer.at[slot], sems.at[slot])
-        part = jnp.dot(pieces[slot][:rows], buffer[slot], preferred_element_type=f32)
-        if slot:
-            result[...] += part
-        else:
-            result[...] = part
-    for slot in range(len(late)):
-        arrived([weight], late_weight.at[slot], late_sems.at[slot])
+    result[...] = own[:rows].astype(f32) + bias[...].astype(f32)
+    add_products(result, pieces, (0, rows), weight, 0)
 
 
 def late_trans_kernel(count, *refs):
     pieces, refs = refs[:count], refs[count:]
-    weight, so_far, own, bias, gain, tail, trans, payload = refs
+    weight, so_far, gain, tail, trans, payload = refs
     rows = so_far.shape[0]
-    trans[...] = so_far[...] + own[:rows].astype(f32) + bias[...].astype(f32)
-    for slot in range(count):
-        trans[...] += jnp.dot(pieces[slot][:rows], weight[slot], preferred_element_type=f32)
+    trans[...] = so_far[...]
+    add_products(trans, pieces, (0, rows), weight, count)
     value = trans[...]
-    payload[:rows] = (value * gain[...].astype(f32)).astype(bf16)
+    payload[:rows] = (value * gain[...].astype(f32).reshape(1, -1)).astype(bf16)
     payload[rows:] = tail[...]
     squares = as_row(jnp.sum(value * value, axis=1, keepdims=True))
     start = payload.shape[0] - words_height
@@ -194,39 +203,19 @@
     ).astype(bf16)
 
 
-def target_kernel(order, lines, table_count, place, *refs):
-    pieces, refs = refs[: len(order)], refs[len(order) :]
-    tables, refs = refs[:table_count], refs[table_count:]
-    result, blocks, sems = refs
-    pull_all(place, order, tables, blocks, sems)
-    for slot in range(len(order)):
-        arrived(tables, blocks.at[slot], sems.at[slot])
-        part = jnp.dot(pieces[slot][lines[0] : lines[1]], blocks[slot], preferred_element_type=f32)
-        if slot:
-            result[...] += part
-        else:
-            result[...] = part
-
-
 def early_logits_kernel(count, *refs):
     pieces, (blocks, result, word_sum) = refs[:count], refs[count:]
-    for slot in range(count):
-        part = jnp.dot(pieces[slot][...], blocks[slot], preferred_element_type=f32)
-        if slot:
-            result[...] += part
-        else:
-            result[...] = part
+    result[...] = jnp.zeros(result.shape, f32)
+    add_products(result, pieces, (0, result.shape[0]), blocks, 0)
     word_sum[...] = sum(piece[-words_height:].astype(f32) for piece in pieces)
 
 
 def late_logits_kernel(first, count, width, *refs):
     pieces, refs = refs[:count], refs[count:]
-    blocks, so_far, early_words, target_half, logits, target_logits, stats, scale, acc = refs
+    blocks, so_far, early_words, logits, target_logits, stats, scale, acc = refs
     rows = logits.shape[0]
-    half = target_half.shape[0]
     acc[...] = so_far[...]
-    for slot in range(count):
-        acc[...] += jnp.dot(pieces[slot][...], blocks[first + slot], preferred_element_type=f32)
+    add_products(acc, pieces, (0, acc.shape[0]), blocks, first)
     words = early_words[...] + sum(piece[-words_height:].astype(f32) for piece in pieces)
     words = words[:, :rows]
     trans_scale = lax.rsqrt((words[0:1] + words[1:2] + words[2:3]) / width + epsilon)
@@ -235,9 +224,8 @@
     trans_column, final_column = as_column(trans_scale), as_column(final_scale)
     trans_logits = acc[:rows] * trans_column
     logits[...] = trans_logits
-    target_logits[:half] = target_half[...] * final_column[:half]
-    target_logits[half:] = acc[rows : rows + rows - half] * final_column[half:]
-    target = target_logits[...]
+    target = acc[rows : 2 * rows] * final_column
+    target_logits[...] = target
     trans_max = jnp.max(trans_logits, axis=1, keepdims=True)
     target_max = jnp.max(target, axis=1, keepdims=True)
     shifted = trans_logits - trans_max
@@ -309,7 +297,7 @@
     dnormed = functools.reduce(lambda a, b: a + b, [term[...].astype(f32) for term in terms])
     scale_row = scale[0:1]
     weight_row = scale_row * scale_row * info[1:2] / (width * scale_row)
-    dtrans = as_column(scale_row) * (dnormed * gain[...].astype(f32) - trans[...] * as_column(weight_row))
+    dtrans = as_column(scale_row) * (dnormed * gain[...].astype(f32).reshape(1, -1) - trans[...] * as_column(weight_row))
     grad_bias[...] = jnp.sum(dtrans, axis=0, keepdims=True)
     kl[...] = jnp.broadcast_to(jnp.sum(info[0:1], axis=1, keepdims=True) / rows, kl.shape)
     rounded = dtrans.astype(bf16)
@@ -333,9 +321,8 @@
     place = jnp.stack([me, section]).astype(jnp.int32)
     width, cols = trans_weight.shape[1:]
     rows = row_pick.shape[1]
-    half = rows // 2
     weight = trans_weight[0]
-    gain = norm_gain[None]
+    gain = norm_gain
     shape = jax.ShapeDtypeStruct
     entries = unembed.shape[1]
     weight_block = 2 * cols * cols
@@ -351,66 +338,71 @@
         ]
 
     final_pools = [final_hidden] + from_others(final_hidden)
-    inputs = kernel_call(
+    first_own = kernel_call(
         inputs_kernel,
-        "inputs",
+        "head",
         [vmem] * 2,
         shape((rows, cols), bf16),
         vmem,
         [],
         0,
         hidden.shape[1] * cols * 2,
-    )(row_pick, in_main_memory(hidden))
-    first_own, tail = kernel_call(
-        head_kernel,
-        "head",
-        [smem] + [vmem] * (3 + sections),
-        (shape((rows + half, cols), bf16), shape((rows - half + words_height, cols), bf16)),
-        (vmem, vmem),
+    )(in_main_memory(row_pick), in_main_memory(hidden))
+    tail = kernel_call(
+        target_kernel,
+        "target",
+        [smem] + [vmem] * (2 + sections),
+        shape((rows + words_height, cols), bf16),
+        vmem,
         [],
         0,
         6 * rows * cols,
-    )(place, row_pick, inputs, gain, *map(in_main_memory, final_pools))
-    tables = [unembed] + from_others(after(unembed, first_own))
-    first = gather_pieces(first_own, count, tables[1:])
-
-    early = list(range(count // 2))
-    late = list(range(count // 2, count))
-    every = early + late
+    )(place, in_main_memory(row_pick), gain, in_main_memory(final_hidden), *final_pools[1:])
+
+    every = list(range(count))
+    early, late = every[: count // 2], every[count // 2 :]
     side = len(early)
-    so_far, late_weight = kernel_call(
-        functools.partial(early_trans_kernel, early, late),
+
+    def fetch(name, where, number_of_columns, *sources):
+        return kernel_call(
+            functools.partial(fetch_kernel, every, len(sources)),
+            name,
+            [smem, main_memory] + [anywhere] * (len(sources) - 1),
+            shape((count, cols, number_of_columns), bf16),
+            vmem,
+            [pltpu.SemaphoreType.DMA((count,))],
+            0,
+            4 * count * cols * number_of_columns,
+        )(where, in_main_memory(sources[0]), *sources[1:])
+
+    tables = [unembed] + from_others(after(unembed, *final_pools[1:]))
+    weight_blocks = fetch("weight_blocks", after(place, first_own), cols, weight)
+    first, _ = gather_pieces(first_own, count, tables[1:], None)
+    so_far = kernel_call(
+        functools.partial(early_trans_kernel, side),
         "trans_early",
-        [smem] + [vmem] * side + [main_memory],
-        (shape((rows, cols), f32), shape((side, cols, cols), bf16)),
-        (vmem, vmem),
-        table_scratch(side, cols) + [pltpu.SemaphoreType.DMA((side,))],
+        [vmem] * (side + 3),
+        shape((rows, cols), f32),
+        vmem,
+        [],
         side * rows * weight_block,
-        2 * side * weight_block,
-    )(place, *[first[k] for k in early], in_main_memory(weight))
-    payload_shape = shape((first_own.shape[0] + words_height, cols), bf16)
+        side * weight_block,
+    )(*[first[k] for k in early], weight_blocks, first_own, trans_bias)
+    payload_shape = shape((rows + tail.shape[0], cols), bf16)
     trans, second_own = kernel_call(
         functools.partial(late_trans_kernel, side),
         "trans_late",
-        [vmem] * (side + 6),
+        [vmem] * (side + 4),
         (shape((rows, cols), f32), payload_shape),
         (vmem, vmem),
         [],
         side * rows * weight_block,
         side * weight_block,
-    )(*[first[k] for k in late], late_weight, so_far, first_own, trans_bias, gain, tail)
-    second = gather_pieces(second_own, count)
-
-    target_half, blocks_in_order = kernel_call(
-        functools.partial(target_kernel, every, (rows, rows + half), sections),
-        "target_half",
-        [smem] + [vmem] * count + [main_memory] * sections,
-        (shape((half, entries), f32), shape((count, cols, entries), bf16)),
-        (vmem, vmem),
-        [pltpu.SemaphoreType.DMA((count,))],
-        count * half * table_block,
-        count * table_block,
-    )(place, *[first[k] for k in every], *map(in_main_memory, tables))
+    )(*[first[k] for k in late], weight_blocks, so_far, gain, tail)
+    second, blocks_in_order = gather_pieces(
+        second_own, count, (), lambda: fetch("unembed_blocks", after(place, second_own), entries, *tables)
+    )
+
     height = payload_shape.shape[0]
     so_far, words = kernel_call(
         functools.partial(early_logits_kernel, side),
@@ -425,19 +417,20 @@
     logits, target_logits, stats, scale = kernel_call(
         functools.partial(late_logits_kernel, side, side, width),
         "logits_late",
-        [vmem] * (side + 4),
+        [vmem] * (side + 3),
         (shape((rows, entries), f32), shape((rows, entries), f32), shape((8, rows), f32), shape((8, rows), f32)),
         (vmem,) * 4,
         [pltpu.VMEM((height, entries), f32)],
         side * height * table_block,
         side * table_block,
-    )(*[second[k] for k in late], blocks_in_order, so_far, words, target_half)
+    )(*[second[k] for k in late], blocks_in_order, so_far, words)
 
     line_stats = jnp.stack([stats] + [swap(stats, k, count) for k in range(4, count, 4)])
     all_stats = [line_stats] + [swap(line_stats, k, count) for k in (1, 2, 3)]
 
     blocks = {}
-    far = [base + 3 for base in range(0, count, 4)][::-1]
+    last = count - 4
+    far = [last + 3, last + 1, last + 2] + [base + 3 for base in range(0, last, 4)][::-1]
     piece = shape((rows, cols), bf16)
     dlogits, info, *made = kernel_call(
         functools.partial(first_backward_kernel, far),
@@ -452,7 +445,7 @@
     blocks.update(zip(far, made))
     bases = list(range(0, count, 4))[::-1]
     for number, part in enumerate((bases[: len(bases) // 2], bases[len(bases) // 2 :])):
-        rest = [base + k for base in part for k in (1, 2, 0)]
+        rest = [base + k for base in part for k in (1, 2, 0) if base + k not in far]
         made = kernel_call(
             functools.partial(later_backward_kernel, rest),
             "backward_near_%d" % number,

time: 144 us -> 133 us (0.924)
  waiting for transfers between devices: 57.7 us -> 42.6 us
  starting transfers between devices: 59.7 us -> 64.2 us
    ppermute x51, waiting for transfers between devices: 57.7 us -> 41.3 us  [swap(): return lax.ppermute(value, 'vocab', [(i, i ^ offset) for i in range(count)])]
    ppermute x51, starting transfers between devices: 59.1 us -> 63.3 us  [swap(): return lax.ppermute(value, 'vocab', [(i, i ^ offset) for i in range(count)])]
    pallas_call x4 -> x5, Pallas kernels: 11.3 us -> 10.5 us  [the longest x2 6.94 us: fetch(): kernel_call(functools.partial(fetch_kernel, every, len(sources)), name, [...]
  transfers between devices with their start and end apart: 53 -> 53, of which waited for: 23 -> 22; matrix products, arithmetic and copies ran while one was open for 1% -> 0% of each run, Pallas kernels for 9% -> 10%
where the time goes in v4:
time: 133 us
  starting transfers between devices  64.2 us (48%)
  waiting for transfers between devices  42.6 us (32%)
  Pallas kernels  22.5 us (17%)
  local copies, waits for them, and re-layouts  2.02 us (2%)
    ppermute x51, starting transfers between devices, swap(): return lax.ppermute(value, 'vocab', [(i, i ^ offset) for i in range(count)])  63.3 us
    ppermute x51, waiting for transfers between devices, swap(): return lax.ppermute(value, 'vocab', [(i, i ^ offset) for i in range(count)])  41.3 us
    pallas_call x2, Pallas kernels, fetch(): kernel_call(functools.partial(fetch_kernel, every, len(sources)), name, [...  6.94 us
    pallas_call x1, Pallas kernels, per_device(): kernel_call(functools.partial(weight_kernel, count, len(terms), width), '...  5.02 us
  transfers between devices with their start and end apart: 53, of which 22 were waited for; matrix products, arithmetic and copies ran while one was open for 0% of the time, Pallas kernels for 10%

profile of v4, /device:TPU:0, one launch (start us, length us, event | category | flops | bytes accessed | tf_op | source)
XLA Modules:
  0.0 132.7 jit_solution(2851722435084219790)
XLA Ops:
  4.3 2.8 %collective-permute-start.3 = (bf16[128,512]{1,0:T(8,128)(2,1)S(1)}, bf16[128,512]{1,0:T(8,128)(2,1)S(1)}, u32[]{:S(2)}, u32[]{:S(2)}) collective-permute-start(bf16[128,512]{1,0:T(8,128)(2,1)S(1)} %head.1.refs_0_.refs_9_), channel_id=1, source_target_pairs={{0,4},{1,5},{2,6},{3,7},{4,0},{5,1},{6,2},{7,3},{8,12},{9,13},{10,... | collective-permute-start | bytes 393224 | tf_op jit(solution)/shard_map/ppermute | solution.py:38
  8.6 1.5 %collective-permute-start.1 = (bf16[128,512]{1,0:T(8,128)(2,1)S(1)}, bf16[128,512]{1,0:T(8,128)(2,1)S(1)}, u32[]{:S(2)}, u32[]{:S(2)}) collective-permute-start(bf16[128,512]{1,0:T(8,128)(2,1)S(1)} %head.1.refs_0_.refs_9_), channel_id=1, source_target_pairs={{0,2},{1,3},{2,0},{3,1},{4,6},{5,7},{6,4},{7,5},{8,10},{9,11},{10,... | collective-permute-start | bytes 393224 | tf_op jit(solution)/shard_map/ppermute | solution.py:38
  10.1 2.6 %collective-permute-start.7 = (bf16[128,512]{1,0:T(8,128)(2,1)S(1)}, bf16[128,512]{1,0:T(8,128)(2,1)S(1)}, u32[]{:S(2)}, u32[]{:S(2)}) collective-permute-start(bf16[128,512]{1,0:T(8,128)(2,1)S(1)} %head.1.refs_0_.refs_9_), channel_id=1, source_target_pairs={{0,8},{1,9},{2,10},{3,11},{4,12},{5,13},{6,14},{7,15},{8,0},{9,1},... | collective-permute-start | bytes 393224 | tf_op jit(solution)/shard_map/ppermute | solution.py:38
  12.7 2.0 %copy-done = bf16[4096,512]{1,0:T(8,128)(2,1)} copy-done((bf16[4096,512]{1,0:T(8,128)(2,1)}, bf16[4096,512]{1,0:T(8,128)(2,1)S(1)}, u32[]{:S(2)}) %copy-start) | copy-done | bytes 4194328
  14.7 2.2 %collective-permute-start.13 = (bf16[128,512]{1,0:T(8,128)(2,1)S(1)}, bf16[128,512]{1,0:T(8,128)(2,1)S(1)}, u32[]{:S(2)}, u32[]{:S(2)}) collective-permute-start(bf16[128,512]{1,0:T(8,128)(2,1)S(1)} %head.1.refs_0_.refs_9_), channel_id=1, source_target_pairs={{0,12},{1,13},{2,14},{3,15},{4,8},{5,9},{6,10},{7,11},{8,4},{9,5},... | collective-permute-start | bytes 393224 | tf_op jit(solution)/shard_map/ppermute | solution.py:38
  16.9 1.5 %collective-permute-start.5 = (bf16[128,512]{1,0:T(8,128)(2,1)S(1)}, bf16[128,512]{1,0:T(8,128)(2,1)S(1)}, u32[]{:S(2)}, u32[]{:S(2)}) collective-permute-start(bf16[128,512]{1,0:T(8,128)(2,1)S(1)} %collective-permute-done.3.refs_4_), channel_id=1, source_target_pairs={{0,2},{1,3},{2,0},{3,1},{4,6},{5,7},{6,4},{7,5},{8,10},{9,11},{10,... | collective-permute-start | bytes 393224 | tf_op jit(solution)/shard_map/ppermute | solution.py:38
  19.9 1.9 %collective-permute-done.7.refs_0_.refs_8_ = bf16[128,512]{1,0:T(8,128)(2,1)S(1)} collective-permute-done((bf16[128,512]{1,0:T(8,128)(2,1)S(1)}, bf16[128,512]{1,0:T(8,128)(2,1)S(1)}, u32[]{:S(2)}, u32[]{:S(2)}) %collective-permute-start.7) | collective-permute-done | bytes 131104 | tf_op jit(solution)/shard_map/ppermute | solution.py:38
  22.8 2.0 %collective-permute-start.15 = (bf16[128,512]{1,0:T(8,128)(2,1)S(1)}, bf16[128,512]{1,0:T(8,128)(2,1)S(1)}, u32[]{:S(2)}, u32[]{:S(2)}) collective-permute-start(bf16[128,512]{1,0:T(8,128)(2,1)S(1)} %collective-permute-done.13.refs_4_.refs_12_), channel_id=1, source_target_pairs={{0,2},{1,3},{2,0},{3,1},{4,6},{5,7},{6,4},{7,5},{8,10},{9,11},{10,... | collective-permute-start | bytes 393224 | tf_op jit(solution)/shard_map/ppermute | solution.py:38
  32.1 4.1 %weight_blocks.1.refs_8_ = bf16[16,512,512]{2,1,0:T(8,128)(2,1)S(1)} custom-call(s32[2]{0:T(128)S(1)} %pad_add_fusion.place, bf16[8192,512]{1,0:T(8,128)(2,1)} %bitcast.10), custom_call_target="tpu_custom_call" | custom-call | bytes 16777216 | tf_op jit(solution)/shard_map/weight_blocks/pallas_call | solution.py:367
  41.4 2.9 %collective-permute-start.17 = (bf16[272,512]{1,0:T(8,128)(2,1)S(1)}, bf16[272,512]{1,0:T(8,128)(2,1)S(1)}, u32[]{:S(2)}, u32[]{:S(2)}) collective-permute-start(bf16[272,512]{1,0:T(8,128)(2,1)S(1)} %get-tuple-element.44.refs_0_), channel_id=1, source_target_pairs={{0,8},{1,9},{2,10},{3,11},{4,12},{5,13},{6,14},{7,15},{8,0},{9,1},... | collective-permute-start | bytes 835592 | tf_op jit(solution)/shard_map/ppermute | solution.py:38
  45.7 6.0 %collective-permute-done.28.refs_4_ = bf16[272,512]{1,0:T(8,128)(2,1)S(1)} collective-permute-done((bf16[272,512]{1,0:T(8,128)(2,1)S(1)}, bf16[272,512]{1,0:T(8,128)(2,1)S(1)}, u32[]{:S(2)}, u32[]{:S(2)}) %collective-permute-start.28) | collective-permute-done | bytes 278560 | tf_op jit(solution)/shard_map/ppermute | solution.py:38
  51.7 1.6 %collective-permute-start.30 = (bf16[272,512]{1,0:T(8,128)(2,1)S(1)}, bf16[272,512]{1,0:T(8,128)(2,1)S(1)}, u32[]{:S(2)}, u32[]{:S(2)}) collective-permute-start(bf16[272,512]{1,0:T(8,128)(2,1)S(1)} %collective-permute-done.28.refs_4_), channel_id=1, source_target_pairs={{0,2},{1,3},{2,0},{3,1},{4,6},{5,7},{6,4},{7,5},{8,10},{9,11},{10,... | collective-permute-start | bytes 835592 | tf_op jit(solution)/shard_map/ppermute | solution.py:38
  54.5 6.4 %collective-permute-done.17.refs_0_ = bf16[272,512]{1,0:T(8,128)(2,1)S(1)} collective-permute-done((bf16[272,512]{1,0:T(8,128)(2,1)S(1)}, bf16[272,512]{1,0:T(8,128)(2,1)S(1)}, u32[]{:S(2)}, u32[]{:S(2)}) %collective-permute-start.17) | collective-permute-done | bytes 278560 | tf_op jit(solution)/shard_map/ppermute | solution.py:38
  62.0 1.8 %collective-permute-start.23 = (bf16[272,512]{1,0:T(8,128)(2,1)S(1)}, bf16[272,512]{1,0:T(8,128)(2,1)S(1)}, u32[]{:S(2)}, u32[]{:S(2)}) collective-permute-start(bf16[272,512]{1,0:T(8,128)(2,1)S(1)} %collective-permute-done.21.refs_4_), channel_id=1, source_target_pairs={{0,2},{1,3},{2,0},{3,1},{4,6},{5,7},{6,4},{7,5},{8,10},{9,11},{10,... | collective-permute-start | bytes 835592 | tf_op jit(solution)/shard_map/ppermute | solution.py:38
  64.3 2.9 %unembed_blocks.1.refs_8_.blocks = bf16[16,512,512]{2,1,0:T(8,128)(2,1)S(1)} custom-call(s32[2]{0:T(128)S(1)} %pad_add_fusion.place, bf16[4096,512]{1,0:T(8,128)(2,1)} %refs_0_.3, bf16[4096,512]{1,0:T(8,128)(2,1)S(1)} %copy-done.1), custom_call_target="tpu_custom_call" | custom-call | bytes 16777216 | tf_op jit(solution)/shard_map/unembed_blocks/pallas_call | solution.py:367
  73.4 3.0 %collective-permute-done.31.refs_7_ = bf16[272,512]{1,0:T(8,128)(2,1)S(1)} collective-permute-done((bf16[272,512]{1,0:T(8,128)(2,1)S(1)}, bf16[272,512]{1,0:T(8,128)(2,1)S(1)}, u32[]{:S(2)}, u32[]{:S(2)}) %collective-permute-start.31) | collective-permute-done | bytes 278560 | tf_op jit(solution)/shard_map/ppermute | solution.py:38
  77.8 3.5 %collective-permute-done.22.refs_5_ = bf16[272,512]{1,0:T(8,128)(2,1)S(1)} collective-permute-done((bf16[272,512]{1,0:T(8,128)(2,1)S(1)}, bf16[272,512]{1,0:T(8,128)(2,1)S(1)}, u32[]{:S(2)}, u32[]{:S(2)}) %collective-permute-start.22) | collective-permute-done | bytes 278560 | tf_op jit(solution)/shard_map/ppermute | solution.py:38
  81.2 3.0 %collective-permute-done.24.refs_7_ = bf16[272,512]{1,0:T(8,128)(2,1)S(1)} collective-permute-done((bf16[272,512]{1,0:T(8,128)(2,1)S(1)}, bf16[272,512]{1,0:T(8,128)(2,1)S(1)}, u32[]{:S(2)}, u32[]{:S(2)}) %collective-permute-start.24) | collective-permute-done | bytes 278560 | tf_op jit(solution)/shard_map/ppermute | solution.py:38
  84.2 1.6 %logits_late.1 = (f32[128,512]{1,0:T(8,128)S(1)}, f32[128,512]{1,0:T(8,128)S(1)}, f32[8,128]{1,0:T(8,128)S(1)}, f32[8,128]{1,0:T(8,128)S(1)}) custom-call(bf16[272,512]{1,0:T(8,128)(2,1)S(1)} %collective-permute-done.17.refs_0_, bf16[272,512]{1,0:T(8,128)(2,1)S(1)} %collective-permute-done.18.refs_1_, bf16[272,512]{1,0:T(8,128)(2,1)S(1)} %collective-permute-done.19.refs_2_, ...), custom_call_target="tpu_custom_call" | custom-call | flops 1140850688 | bytes 4194304 | tf_op jit(solution)/shard_map/logits_late/pallas_call | solution.py:417
  85.8 2.0 %collective-permute-start.32 = (f32[8,128]{1,0:T(8,128)S(1)}, f32[8,128]{1,0:T(8,128)S(1)}, u32[]{:S(2)}, u32[]{:S(2)}) collective-permute-start(f32[8,128]{1,0:T(8,128)S(1)} %get-tuple-element.51), channel_id=1, source_target_pairs={{0,4},{1,5},{2,6},{3,7},{4,0},{5,1},{6,2},{7,3},{8,12},{9,13},{10,... | collective-permute-start | bytes 12296 | tf_op jit(solution)/shard_map/ppermute | solution.py:38
  87.8 2.4 %collective-permute-start.34 = (f32[8,128]{1,0:T(8,128)S(1)}, f32[8,128]{1,0:T(8,128)S(1)}, u32[]{:S(2)}, u32[]{:S(2)}) collective-permute-start(f32[8,128]{1,0:T(8,128)S(1)} %get-tuple-element.51), channel_id=1, source_target_pairs={{0,12},{1,13},{2,14},{3,15},{4,8},{5,9},{6,10},{7,11},{8,4},{9,5},... | collective-permute-start | bytes 12296 | tf_op jit(solution)/shard_map/ppermute | solution.py:38
  90.2 2.1 %collective-permute-done.33 = f32[8,128]{1,0:T(8,128)S(1)} collective-permute-done((f32[8,128]{1,0:T(8,128)S(1)}, f32[8,128]{1,0:T(8,128)S(1)}, u32[]{:S(2)}, u32[]{:S(2)}) %collective-permute-start.33) | collective-permute-done | bytes 4128 | tf_op jit(solution)/shard_map/ppermute | solution.py:38
  93.7 1.6 %collective-permute-start.36 = (f32[4,8,128]{2,1,0:T(8,128)S(1)}, f32[4,8,128]{2,1,0:T(8,128)S(1)}, u32[]{:S(2)}, u32[]{:S(2)}) collective-permute-start(f32[4,8,128]{2,1,0:T(8,128)S(1)} %pad_maximum_fusion.refs_0_), channel_id=1, source_target_pairs={{0,2},{1,3},{2,0},{3,1},{4,6},{5,7},{6,4},{7,5},{8,10},{9,11},{10,... | collective-permute-start | bytes 49160 | tf_op jit(solution)/shard_map/ppermute | solution.py:38
  97.4 2.6 %collective-permute-done.37.refs_3_ = f32[4,8,128]{2,1,0:T(8,128)S(1)} collective-permute-done((f32[4,8,128]{2,1,0:T(8,128)S(1)}, f32[4,8,128]{2,1,0:T(8,128)S(1)}, u32[]{:S(2)}, u32[]{:S(2)}) %collective-permute-start.37) | collective-permute-done | bytes 16416 | tf_op jit(solution)/shard_map/ppermute | solution.py:38
  102.6 1.7 %collective-permute-start.44 = (bf16[128,512]{1,0:T(8,128)(2,1)S(1)}, bf16[128,512]{1,0:T(8,128)(2,1)S(1)}, u32[]{:S(2)}, u32[]{:S(2)}) collective-permute-start(bf16[128,512]{1,0:T(8,128)(2,1)S(1)} %get-tuple-element.60), channel_id=1, source_target_pairs={{0,2},{1,3},{2,0},{3,1},{4,6},{5,7},{6,4},{7,5},{8,10},{9,11},{10,... | collective-permute-start | bytes 393224 | tf_op jit(solution)/shard_map/ppermute | solution.py:38
  106.1 1.6 %collective-permute-start.40 = (bf16[128,512]{1,0:T(8,128)(2,1)S(1)}, bf16[128,512]{1,0:T(8,128)(2,1)S(1)}, u32[]{:S(2)}, u32[]{:S(2)}) collective-permute-start(bf16[128,512]{1,0:T(8,128)(2,1)S(1)} %get-tuple-element.56), channel_id=1, source_target_pairs={{0,2},{1,3},{2,0},{3,1},{4,6},{5,7},{6,4},{7,5},{8,10},{9,11},{10,... | collective-permute-start | bytes 393224 | tf_op jit(solution)/shard_map/ppermute | solution.py:38
  109.3 2.2 %collective-permute-done.38 = bf16[128,512]{1,0:T(8,128)(2,1)S(1)} collective-permute-done((bf16[128,512]{1,0:T(8,128)(2,1)S(1)}, bf16[128,512]{1,0:T(8,128)(2,1)S(1)}, u32[]{:S(2)}, u32[]{:S(2)}) %collective-permute-start.38) | collective-permute-done | bytes 131104 | tf_op jit(solution)/shard_map/ppermute | solution.py:38
  114.6 1.7 %collective-permute-start.48 = (bf16[128,512]{1,0:T(8,128)(2,1)S(1)}, bf16[128,512]{1,0:T(8,128)(2,1)S(1)}, u32[]{:S(2)}, u32[]{:S(2)}) collective-permute-start(bf16[128,512]{1,0:T(8,128)(2,1)S(1)} %add_convert_fusion.2), channel_id=1, source_target_pairs={{0,2},{1,3},{2,0},{3,1},{4,6},{5,7},{6,4},{7,5},{8,10},{9,11},{10,... | collective-permute-start | bytes 393224 | tf_op jit(solution)/shard_map/ppermute | solution.py:38
  116.5 2.5 %collective-permute-start.41 = (bf16[128,512]{1,0:T(8,128)(2,1)S(1)}, bf16[128,512]{1,0:T(8,128)(2,1)S(1)}, u32[]{:S(2)}, u32[]{:S(2)}) collective-permute-start(bf16[128,512]{1,0:T(8,128)(2,1)S(1)} %add_convert_fusion.5), channel_id=1, source_target_pairs={{0,12},{1,13},{2,14},{3,15},{4,8},{5,9},{6,10},{7,11},{8,4},{9,5},... | collective-permute-start | bytes 393224 | tf_op jit(solution)/shard_map/ppermute | solution.py:38
  121.3 2.0 %collective-permute-start.45 = (bf16[128,512]{1,0:T(8,128)(2,1)S(1)}, bf16[128,512]{1,0:T(8,128)(2,1)S(1)}, u32[]{:S(2)}, u32[]{:S(2)}) collective-permute-start(bf16[128,512]{1,0:T(8,128)(2,1)S(1)} %add_convert_fusion.3), channel_id=1, source_target_pairs={{0,8},{1,9},{2,10},{3,11},{4,12},{5,13},{6,14},{7,15},{8,0},{9,1},... | collective-permute-start | bytes 393224 | tf_op jit(solution)/shard_map/ppermute | solution.py:38
  125.3 2.3 %collective-permute-done.49.refs_18_ = bf16[128,512]{1,0:T(8,128)(2,1)S(1)} collective-permute-done((bf16[128,512]{1,0:T(8,128)(2,1)S(1)}, bf16[128,512]{1,0:T(8,128)(2,1)S(1)}, u32[]{:S(2)}, u32[]{:S(2)}) %collective-permute-start.49) | collective-permute-done | bytes 131104 | tf_op jit(solution)/shard_map/ppermute | solution.py:38
  127.5 5.0 %grad_weight.1 = (bf16[1,8192,512]{2,1,0:T(8,128)(2,1)}, f32[1,512]{1,0:T(1,128)}, f32[1,128]{1,0:T(1,128)}) custom-call(s32[2]{0:T(128)S(1)} %pad_add_fusion.place, bf16[128,512]{1,0:T(8,128)(2,1)S(1)} %head.1.refs_0_.refs_9_, bf16[128,512]{1,0:T(8,128)(2,1)S(1)} %collective-permute-done.refs_1_, bf16[128,512]{1,0:T(8,128)(2,1)S(1)} %collective-permute-done.1.refs_2_, ...), custom_call_target="tpu_custom_call" | custom-call | flops 1073741824 | bytes 8388608 | tf_op jit(solution)/shard_map/grad_weight/pallas_call | solution.py:462
  (102 shorter events, 48.8 us)
Async XLA Ops:
  2.5 10.2 %collective-permute-start.12 = (bf16[4096,512]{1,0:T(8,128)(2,1)}, bf16[4096,512]{1,0:T(8,128)(2,1)S(1)}, u32[]{:S(2)}, u32[]{:S(2)}) collective-permute-start(bf16[4096,512]{1,0:T(8,128)(2,1)} %refs_0_.3), channel_id=1, source_target_pairs={{16,0},{0,16},{17,1},{1,17},{18,2},{2,18},{19,3},{3,19},{20,4},{4,... | collective-permute-start | bytes 12582920 | tf_op jit(solution)/shard_map/ppermute | solution.py:336
  4.3 12.6 %collective-permute-start.3 = (bf16[128,512]{1,0:T(8,128)(2,1)S(1)}, bf16[128,512]{1,0:T(8,128)(2,1)S(1)}, u32[]{:S(2)}, u32[]{:S(2)}) collective-permute-start(bf16[128,512]{1,0:T(8,128)(2,1)S(1)} %head.1.refs_0_.refs_9_), channel_id=1, source_target_pairs={{0,4},{1,5},{2,6},{3,7},{4,0},{5,1},{6,2},{7,3},{8,12},{9,13},{10,... | collective-permute-start | bytes 393224 | tf_op jit(solution)/shard_map/ppermute | solution.py:38
  7.1 11.3 %collective-permute-start = (bf16[128,512]{1,0:T(8,128)(2,1)S(1)}, bf16[128,512]{1,0:T(8,128)(2,1)S(1)}, u32[]{:S(2)}, u32[]{:S(2)}) collective-permute-start(bf16[128,512]{1,0:T(8,128)(2,1)S(1)} %head.1.refs_0_.refs_9_), channel_id=1, source_target_pairs={{0,1},{1,0},{2,3},{3,2},{4,5},{5,4},{6,7},{7,6},{8,9},{9,8},{10,11... | collective-permute-start | bytes 393224 | tf_op jit(solution)/shard_map/ppermute | solution.py:38
  8.6 14.2 %collective-permute-start.1 = (bf16[128,512]{1,0:T(8,128)(2,1)S(1)}, bf16[128,512]{1,0:T(8,128)(2,1)S(1)}, u32[]{:S(2)}, u32[]{:S(2)}) collective-permute-start(bf16[128,512]{1,0:T(8,128)(2,1)S(1)} %head.1.refs_0_.refs_9_), channel_id=1, source_target_pairs={{0,2},{1,3},{2,0},{3,1},{4,6},{5,7},{6,4},{7,5},{8,10},{9,11},{10,... | collective-permute-start | bytes 393224 | tf_op jit(solution)/shard_map/ppermute | solution.py:38
  10.1 11.7 %collective-permute-start.7 = (bf16[128,512]{1,0:T(8,128)(2,1)S(1)}, bf16[128,512]{1,0:T(8,128)(2,1)S(1)}, u32[]{:S(2)}, u32[]{:S(2)}) collective-permute-start(bf16[128,512]{1,0:T(8,128)(2,1)S(1)} %head.1.refs_0_.refs_9_), channel_id=1, source_target_pairs={{0,8},{1,9},{2,10},{3,11},{4,12},{5,13},{6,14},{7,15},{8,0},{9,1},... | collective-permute-start | bytes 393224 | tf_op jit(solution)/shard_map/ppermute | solution.py:38
  14.7 8.1 %collective-permute-start.13 = (bf16[128,512]{1,0:T(8,128)(2,1)S(1)}, bf16[128,512]{1,0:T(8,128)(2,1)S(1)}, u32[]{:S(2)}, u32[]{:S(2)}) collective-permute-start(bf16[128,512]{1,0:T(8,128)(2,1)S(1)} %head.1.refs_0_.refs_9_), channel_id=1, source_target_pairs={{0,12},{1,13},{2,14},{3,15},{4,8},{5,9},{6,10},{7,11},{8,4},{9,5},... | collective-permute-start | bytes 393224 | tf_op jit(solution)/shard_map/ppermute | solution.py:38
  16.9 7.9 %collective-permute-start.5 = (bf16[128,512]{1,0:T(8,128)(2,1)S(1)}, bf16[128,512]{1,0:T(8,128)(2,1)S(1)}, u32[]{:S(2)}, u32[]{:S(2)}) collective-permute-start(bf16[128,512]{1,0:T(8,128)(2,1)S(1)} %collective-permute-done.3.refs_4_), channel_id=1, source_target_pairs={{0,2},{1,3},{2,0},{3,1},{4,6},{5,7},{6,4},{7,5},{8,10},{9,11},{10,... | collective-permute-start | bytes 393224 | tf_op jit(solution)/shard_map/ppermute | solution.py:38
  18.4 7.5 %collective-permute-start.4 = (bf16[128,512]{1,0:T(8,128)(2,1)S(1)}, bf16[128,512]{1,0:T(8,128)(2,1)S(1)}, u32[]{:S(2)}, u32[]{:S(2)}) collective-permute-start(bf16[128,512]{1,0:T(8,128)(2,1)S(1)} %collective-permute-done.3.refs_4_), channel_id=1, source_target_pairs={{0,1},{1,0},{2,3},{3,2},{4,5},{5,4},{6,7},{7,6},{8,9},{9,8},{10,11... | collective-permute-start | bytes 393224 | tf_op jit(solution)/shard_map/ppermute | solution.py:38
  22.8 8.0 %collective-permute-start.15 = (bf16[128,512]{1,0:T(8,128)(2,1)S(1)}, bf16[128,512]{1,0:T(8,128)(2,1)S(1)}, u32[]{:S(2)}, u32[]{:S(2)}) collective-permute-start(bf16[128,512]{1,0:T(8,128)(2,1)S(1)} %collective-permute-done.13.refs_4_.refs_12_), channel_id=1, source_target_pairs={{0,2},{1,3},{2,0},{3,1},{4,6},{5,7},{6,4},{7,5},{8,10},{9,11},{10,... | collective-permute-start | bytes 393224 | tf_op jit(solution)/shard_map/ppermute | solution.py:38
  24.8 12.9 %collective-permute-start.6 = (bf16[128,512]{1,0:T(8,128)(2,1)S(1)}, bf16[128,512]{1,0:T(8,128)(2,1)S(1)}, u32[]{:S(2)}, u32[]{:S(2)}) collective-permute-start(bf16[128,512]{1,0:T(8,128)(2,1)S(1)} %collective-permute-done.5.refs_6_), channel_id=1, source_target_pairs={{0,1},{1,0},{2,3},{3,2},{4,5},{5,4},{6,7},{7,6},{8,9},{9,8},{10,11... | collective-permute-start | bytes 393224 | tf_op jit(solution)/shard_map/ppermute | solution.py:38
  25.9 12.5 %collective-permute-start.9 = (bf16[128,512]{1,0:T(8,128)(2,1)S(1)}, bf16[128,512]{1,0:T(8,128)(2,1)S(1)}, u32[]{:S(2)}, u32[]{:S(2)}) collective-permute-start(bf16[128,512]{1,0:T(8,128)(2,1)S(1)} %collective-permute-done.7.refs_0_.refs_8_), channel_id=1, source_target_pairs={{0,2},{1,3},{2,0},{3,1},{4,6},{5,7},{6,4},{7,5},{8,10},{9,11},{10,... | collective-permute-start | bytes 393224 | tf_op jit(solution)/shard_map/ppermute | solution.py:38
  27.6 10.8 %collective-permute-start.10 = (bf16[128,512]{1,0:T(8,128)(2,1)S(1)}, bf16[128,512]{1,0:T(8,128)(2,1)S(1)}, u32[]{:S(2)}, u32[]{:S(2)}) collective-permute-start(bf16[128,512]{1,0:T(8,128)(2,1)S(1)} %collective-permute-done.8.refs_1_.refs_9_), channel_id=1, source_target_pairs={{0,2},{1,3},{2,0},{3,1},{4,6},{5,7},{6,4},{7,5},{8,10},{9,11},{10,... | collective-permute-start | bytes 393224 | tf_op jit(solution)/shard_map/ppermute | solution.py:38
  28.4 10.0 %collective-permute-start.14 = (bf16[128,512]{1,0:T(8,128)(2,1)S(1)}, bf16[128,512]{1,0:T(8,128)(2,1)S(1)}, u32[]{:S(2)}, u32[]{:S(2)}) collective-permute-start(bf16[128,512]{1,0:T(8,128)(2,1)S(1)} %collective-permute-done.13.refs_4_.refs_12_), channel_id=1, source_target_pairs={{0,1},{1,0},{2,3},{3,2},{4,5},{5,4},{6,7},{7,6},{8,9},{9,8},{10,11... | collective-permute-start | bytes 393224 | tf_op jit(solution)/shard_map/ppermute | solution.py:38
  30.8 7.7 %collective-permute-start.16 = (bf16[128,512]{1,0:T(8,128)(2,1)S(1)}, bf16[128,512]{1,0:T(8,128)(2,1)S(1)}, u32[]{:S(2)}, u32[]{:S(2)}) collective-permute-start(bf16[128,512]{1,0:T(8,128)(2,1)S(1)} %collective-permute-done.15.refs_6_.refs_14_), channel_id=1, source_target_pairs={{0,1},{1,0},{2,3},{3,2},{4,5},{5,4},{6,7},{7,6},{8,9},{9,8},{10,11... | collective-permute-start | bytes 393224 | tf_op jit(solution)/shard_map/ppermute | solution.py:38
  39.3 12.4 %collective-permute-start.28 = (bf16[272,512]{1,0:T(8,128)(2,1)S(1)}, bf16[272,512]{1,0:T(8,128)(2,1)S(1)}, u32[]{:S(2)}, u32[]{:S(2)}) collective-permute-start(bf16[272,512]{1,0:T(8,128)(2,1)S(1)} %get-tuple-element.44.refs_0_), channel_id=1, source_target_pairs={{0,4},{1,5},{2,6},{3,7},{4,0},{5,1},{6,2},{7,3},{8,12},{9,13},{10,... | collective-permute-start | bytes 835592 | tf_op jit(solution)/shard_map/ppermute | solution.py:38
  40.8 12.5 %collective-permute-start.25 = (bf16[272,512]{1,0:T(8,128)(2,1)S(1)}, bf16[272,512]{1,0:T(8,128)(2,1)S(1)}, u32[]{:S(2)}, u32[]{:S(2)}) collective-permute-start(bf16[272,512]{1,0:T(8,128)(2,1)S(1)} %get-tuple-element.44.refs_0_), channel_id=1, source_target_pairs={{0,1},{1,0},{2,3},{3,2},{4,5},{5,4},{6,7},{7,6},{8,9},{9,8},{10,11... | collective-permute-start | bytes 835592 | tf_op jit(solution)/shard_map/ppermute | solution.py:38
  40.8 13.0 %collective-permute-start.26 = (bf16[272,512]{1,0:T(8,128)(2,1)S(1)}, bf16[272,512]{1,0:T(8,128)(2,1)S(1)}, u32[]{:S(2)}, u32[]{:S(2)}) collective-permute-start(bf16[272,512]{1,0:T(8,128)(2,1)S(1)} %get-tuple-element.44.refs_0_), channel_id=1, source_target_pairs={{0,2},{1,3},{2,0},{3,1},{4,6},{5,7},{6,4},{7,5},{8,10},{9,11},{10,... | collective-permute-start | bytes 835592 | tf_op jit(solution)/shard_map/ppermute | solution.py:38
  41.4 19.5 %collective-permute-start.17 = (bf16[272,512]{1,0:T(8,128)(2,1)S(1)}, bf16[272,512]{1,0:T(8,128)(2,1)S(1)}, u32[]{:S(2)}, u32[]{:S(2)}) collective-permute-start(bf16[272,512]{1,0:T(8,128)(2,1)S(1)} %get-tuple-element.44.refs_0_), channel_id=1, source_target_pairs={{0,8},{1,9},{2,10},{3,11},{4,12},{5,13},{6,14},{7,15},{8,0},{9,1},... | collective-permute-start | bytes 835592 | tf_op jit(solution)/shard_map/ppermute | solution.py:38
  44.2 17.7 %collective-permute-start.21 = (bf16[272,512]{1,0:T(8,128)(2,1)S(1)}, bf16[272,512]{1,0:T(8,128)(2,1)S(1)}, u32[]{:S(2)}, u32[]{:S(2)}) collective-permute-start(bf16[272,512]{1,0:T(8,128)(2,1)S(1)} %get-tuple-element.44.refs_0_), channel_id=1, source_target_pairs={{0,12},{1,13},{2,14},{3,15},{4,8},{5,9},{6,10},{7,11},{8,4},{9,5},... | collective-permute-start | bytes 835592 | tf_op jit(solution)/shard_map/ppermute | solution.py:38
  51.7 12.1 %collective-permute-start.30 = (bf16[272,512]{1,0:T(8,128)(2,1)S(1)}, bf16[272,512]{1,0:T(8,128)(2,1)S(1)}, u32[]{:S(2)}, u32[]{:S(2)}) collective-permute-start(bf16[272,512]{1,0:T(8,128)(2,1)S(1)} %collective-permute-done.28.refs_4_), channel_id=1, source_target_pairs={{0,2},{1,3},{2,0},{3,1},{4,6},{5,7},{6,4},{7,5},{8,10},{9,11},{10,... | collective-permute-start | bytes 835592 | tf_op jit(solution)/shard_map/ppermute | solution.py:38
  53.3 13.9 %collective-permute-start.27 = (bf16[272,512]{1,0:T(8,128)(2,1)S(1)}, bf16[272,512]{1,0:T(8,128)(2,1)S(1)}, u32[]{:S(2)}, u32[]{:S(2)}) collective-permute-start(bf16[272,512]{1,0:T(8,128)(2,1)S(1)} %collective-permute-done.25.refs_1_), channel_id=1, source_target_pairs={{0,2},{1,3},{2,0},{3,1},{4,6},{5,7},{6,4},{7,5},{8,10},{9,11},{10,... | collective-permute-start | bytes 835592 | tf_op jit(solution)/shard_map/ppermute | solution.py:38
  53.7 14.2 %collective-permute-start.29 = (bf16[272,512]{1,0:T(8,128)(2,1)S(1)}, bf16[272,512]{1,0:T(8,128)(2,1)S(1)}, u32[]{:S(2)}, u32[]{:S(2)}) collective-permute-start(bf16[272,512]{1,0:T(8,128)(2,1)S(1)} %collective-permute-done.28.refs_4_), channel_id=1, source_target_pairs={{0,1},{1,0},{2,3},{3,2},{4,5},{5,4},{6,7},{7,6},{8,9},{9,8},{10,11... | collective-permute-start | bytes 835592 | tf_op jit(solution)/shard_map/ppermute | solution.py:38
  60.9 9.6 %collective-permute-start.18 = (bf16[272,512]{1,0:T(8,128)(2,1)S(1)}, bf16[272,512]{1,0:T(8,128)(2,1)S(1)}, u32[]{:S(2)}, u32[]{:S(2)}) collective-permute-start(bf16[272,512]{1,0:T(8,128)(2,1)S(1)} %collective-permute-done.17.refs_0_), channel_id=1, source_target_pairs={{0,1},{1,0},{2,3},{3,2},{4,5},{5,4},{6,7},{7,6},{8,9},{9,8},{10,11... | collective-permute-start | bytes 835592 | tf_op jit(solution)/shard_map/ppermute | solution.py:38
  62.0 9.9 %collective-permute-start.23 = (bf16[272,512]{1,0:T(8,128)(2,1)S(1)}, bf16[272,512]{1,0:T(8,128)(2,1)S(1)}, u32[]{:S(2)}, u32[]{:S(2)}) collective-permute-start(bf16[272,512]{1,0:T(8,128)(2,1)S(1)} %collective-permute-done.21.refs_4_), channel_id=1, source_target_pairs={{0,2},{1,3},{2,0},{3,1},{4,6},{5,7},{6,4},{7,5},{8,10},{9,11},{10,... | collective-permute-start | bytes 835592 | tf_op jit(solution)/shard_map/ppermute | solution.py:38
  63.8 12.6 %collective-permute-start.31 = (bf16[272,512]{1,0:T(8,128)(2,1)S(1)}, bf16[272,512]{1,0:T(8,128)(2,1)S(1)}, u32[]{:S(2)}, u32[]{:S(2)}) collective-permute-start(bf16[272,512]{1,0:T(8,128)(2,1)S(1)} %collective-permute-done.30.refs_6_), channel_id=1, source_target_pairs={{0,1},{1,0},{2,3},{3,2},{4,5},{5,4},{6,7},{7,6},{8,9},{9,8},{10,11... | collective-permute-start | bytes 835592 | tf_op jit(solution)/shard_map/ppermute | solution.py:38
  67.2 10.5 %collective-permute-start.19 = (bf16[272,512]{1,0:T(8,128)(2,1)S(1)}, bf16[272,512]{1,0:T(8,128)(2,1)S(1)}, u32[]{:S(2)}, u32[]{:S(2)}) collective-permute-start(bf16[272,512]{1,0:T(8,128)(2,1)S(1)} %collective-permute-done.17.refs_0_), channel_id=1, source_target_pairs={{0,2},{1,3},{2,0},{3,1},{4,6},{5,7},{6,4},{7,5},{8,10},{9,11},{10,... | collective-permute-start | bytes 835592 | tf_op jit(solution)/shard_map/ppermute | solution.py:38
  67.9 13.3 %collective-permute-start.22 = (bf16[272,512]{1,0:T(8,128)(2,1)S(1)}, bf16[272,512]{1,0:T(8,128)(2,1)S(1)}, u32[]{:S(2)}, u32[]{:S(2)}) collective-permute-start(bf16[272,512]{1,0:T(8,128)(2,1)S(1)} %collective-permute-done.21.refs_4_), channel_id=1, source_target_pairs={{0,1},{1,0},{2,3},{3,2},{4,5},{5,4},{6,7},{7,6},{8,9},{9,8},{10,11... | collective-permute-start | bytes 835592 | tf_op jit(solution)/shard_map/ppermute | solution.py:38
  70.5 10.8 %collective-permute-start.20 = (bf16[272,512]{1,0:T(8,128)(2,1)S(1)}, bf16[272,512]{1,0:T(8,128)(2,1)S(1)}, u32[]{:S(2)}, u32[]{:S(2)}) collective-permute-start(bf16[272,512]{1,0:T(8,128)(2,1)S(1)} %collective-permute-done.18.refs_1_), channel_id=1, source_target_pairs={{0,2},{1,3},{2,0},{3,1},{4,6},{5,7},{6,4},{7,5},{8,10},{9,11},{10,... | collective-permute-start | bytes 835592 | tf_op jit(solution)/shard_map/ppermute | solution.py:38
  71.9 12.3 %collective-permute-start.24 = (bf16[272,512]{1,0:T(8,128)(2,1)S(1)}, bf16[272,512]{1,0:T(8,128)(2,1)S(1)}, u32[]{:S(2)}, u32[]{:S(2)}) collective-permute-start(bf16[272,512]{1,0:T(8,128)(2,1)S(1)} %collective-permute-done.23.refs_6_), channel_id=1, source_target_pairs={{0,1},{1,0},{2,3},{3,2},{4,5},{5,4},{6,7},{7,6},{8,9},{9,8},{10,11... | collective-permute-start | bytes 835592 | tf_op jit(solution)/shard_map/ppermute | solution.py:38
  101.3 7.6 %collective-permute-start.42 = (bf16[128,512]{1,0:T(8,128)(2,1)S(1)}, bf16[128,512]{1,0:T(8,128)(2,1)S(1)}, u32[]{:S(2)}, u32[]{:S(2)}) collective-permute-start(bf16[128,512]{1,0:T(8,128)(2,1)S(1)} %get-tuple-element.59), channel_id=1, source_target_pairs={{0,2},{1,3},{2,0},{3,1},{4,6},{5,7},{6,4},{7,5},{8,10},{9,11},{10,... | collective-permute-start | bytes 393224 | tf_op jit(solution)/shard_map/ppermute | solution.py:38
  102.6 16.4 %collective-permute-start.44 = (bf16[128,512]{1,0:T(8,128)(2,1)S(1)}, bf16[128,512]{1,0:T(8,128)(2,1)S(1)}, u32[]{:S(2)}, u32[]{:S(2)}) collective-permute-start(bf16[128,512]{1,0:T(8,128)(2,1)S(1)} %get-tuple-element.60), channel_id=1, source_target_pairs={{0,2},{1,3},{2,0},{3,1},{4,6},{5,7},{6,4},{7,5},{8,10},{9,11},{10,... | collective-permute-start | bytes 393224 | tf_op jit(solution)/shard_map/ppermute | solution.py:38
  106.1 7.9 %collective-permute-start.40 = (bf16[128,512]{1,0:T(8,128)(2,1)S(1)}, bf16[128,512]{1,0:T(8,128)(2,1)S(1)}, u32[]{:S(2)}, u32[]{:S(2)}) collective-permute-start(bf16[128,512]{1,0:T(8,128)(2,1)S(1)} %get-tuple-element.56), channel_id=1, source_target_pairs={{0,2},{1,3},{2,0},{3,1},{4,6},{5,7},{6,4},{7,5},{8,10},{9,11},{10,... | collective-permute-start | bytes 393224 | tf_op jit(solution)/shard_map/ppermute | solution.py:38
  (25 other events, 152.4 us)

commit v5 on v4

--- a/solution.py
+++ b/solution.py
@@ -10,7 +10,7 @@
 epsilon = 1e-05
 f32 = jnp.float32
 bf16 = jnp.bfloat16
-words_height = 16
+words_height = 8
 vmem = pl.BlockSpec(memory_space=pltpu.VMEM)
 smem = pl.BlockSpec(memory_space=pltpu.SMEM)
 anywhere = pl.BlockSpec(memory_space=pl.ANY)
@@ -288,20 +288,30 @@
         out[...] = backward_block(value, blocks[k])
 
 
-def weight_kernel(count, term_count, width, place, *refs):
+def last_backward_kernel(order, width, blocks, dlogits, trans, gain, scale, info, factor, offset, *outs):
+    later_backward_kernel(order, blocks, dlogits, *outs)
+    scale_row = scale[0:1]
+    factor[...] = as_column(scale_row) * gain[...].astype(f32).reshape(1, -1)
+    offset[...] = trans[...] * as_column(scale_row * scale_row * info[1:2] / width)
+
+
+def weight_kernel(count, term_count, place, *refs):
     pieces, refs = refs[:count], refs[count:]
     terms, refs = refs[:term_count], refs[term_count:]
-    trans, gain, scale, info, grad_weight, grad_bias, kl, buffer, sems = refs
-    rows = trans.shape[0]
+    factor, offset, info, grad_weight, grad_bias, kl, buffer, sems, bias_sum, kl_sum, small_sems = refs
+    rows = factor.shape[0]
     height = buffer.shape[1]
     dnormed = functools.reduce(lambda a, b: a + b, [term[...].astype(f32) for term in terms])
-    scale_row = scale[0:1]
-    weight_row = scale_row * scale_row * info[1:2] / (width * scale_row)
-    dtrans = as_column(scale_row) * (dnormed * gain[...].astype(f32).reshape(1, -1) - trans[...] * as_column(weight_row))
-    grad_bias[...] = jnp.sum(dtrans, axis=0, keepdims=True)
-    kl[...] = jnp.broadcast_to(jnp.sum(info[0:1], axis=1, keepdims=True) / rows, kl.shape)
+    dtrans = dnormed * factor[...] - offset[...]
     rounded = dtrans.astype(bf16)
-    copies = []
+    bias_sum[...] = jnp.sum(dtrans, axis=0, keepdims=True)
+    kl_sum[...] = jnp.broadcast_to(jnp.sum(info[0:1], axis=1, keepdims=True) / rows, kl_sum.shape)
+    copies = [
+        pltpu.make_async_copy(bias_sum, grad_bias, small_sems.at[0]),
+        pltpu.make_async_copy(kl_sum, kl, small_sems.at[1]),
+    ]
+    for copy in copies:
+        copy.start()
     for k in range(count):
         buffer[k] = lax.dot_general(
             pieces[k][:rows], rounded, (((0,), (0,)), ((), ())), preferred_element_type=f32
@@ -348,16 +358,17 @@
         0,
         hidden.shape[1] * cols * 2,
     )(in_main_memory(row_pick), in_main_memory(hidden))
-    tail = kernel_call(
-        target_kernel,
-        "target",
-        [smem] + [vmem] * (2 + sections),
-        shape((rows + words_height, cols), bf16),
-        vmem,
-        [],
-        0,
-        6 * rows * cols,
-    )(place, in_main_memory(row_pick), gain, in_main_memory(final_hidden), *final_pools[1:])
+    def make_tail():
+        return kernel_call(
+            target_kernel,
+            "target",
+            [smem] + [vmem] * (2 + sections),
+            shape((rows + words_height, cols), bf16),
+            vmem,
+            [],
+            0,
+            6 * rows * cols,
+        )(place, in_main_memory(row_pick), gain, in_main_memory(final_hidden), *final_pools[1:])
 
     every = list(range(count))
     early, late = every[: count // 2], every[count // 2 :]
@@ -377,7 +388,7 @@
 
     tables = [unembed] + from_others(after(unembed, *final_pools[1:]))
     weight_blocks = fetch("weight_blocks", after(place, first_own), cols, weight)
-    first, _ = gather_pieces(first_own, count, tables[1:], None)
+    first, tail = gather_pieces(first_own, count, tables[1:], make_tail)
     so_far = kernel_call(
         functools.partial(early_trans_kernel, side),
         "trans_early",
@@ -444,31 +455,43 @@
     )(blocks_in_order, logits, target_logits, *all_stats)
     blocks.update(zip(far, made))
     bases = list(range(0, count, 4))[::-1]
-    for number, part in enumerate((bases[: len(bases) // 2], bases[len(bases) // 2 :])):
-        rest = [base + k for base in part for k in (1, 2, 0) if base + k not in far]
-        made = kernel_call(
-            functools.partial(later_backward_kernel, rest),
-            "backward_near_%d" % number,
-            [vmem] * 2,
-            tuple([piece] * len(rest)),
-            (vmem,) * len(rest),
-            [],
-            len(rest) * rows * table_block,
-            len(rest) * table_block,
-        )(blocks_in_order, dlogits)
-        blocks.update(zip(rest, made))
+    halves = bases[: len(bases) // 2], bases[len(bases) // 2 :]
+    rests = [[base + k for base in part for k in (1, 2, 0) if base + k not in far] for part in halves]
+    made = kernel_call(
+        functools.partial(later_backward_kernel, rests[0]),
+        "backward_near_0",
+        [vmem] * 2,
+        tuple([piece] * len(rests[0])),
+        (vmem,) * len(rests[0]),
+        [],
+        len(rests[0]) * rows * table_block,
+        len(rests[0]) * table_block,
+    )(blocks_in_order, dlogits)
+    blocks.update(zip(rests[0], made))
+    factor, offset, *made = kernel_call(
+        functools.partial(last_backward_kernel, rests[1], width),
+        "backward_near_1",
+        [vmem] * 6,
+        (shape((rows, cols), f32),) * 2 + (piece,) * len(rests[1]),
+        (vmem,) * (2 + len(rests[1])),
+        [],
+        len(rests[1]) * rows * table_block,
+        len(rests[1]) * table_block,
+    )(blocks_in_order, dlogits, trans, gain, scale, info)
+    blocks.update(zip(rests[1], made))
     terms = scatter_sums(blocks, count)
 
     grad_weight, grad_bias, kl = kernel_call(
-        functools.partial(weight_kernel, count, len(terms), width),
+        functools.partial(weight_kernel, count, len(terms)),
         "grad_weight",
-        [smem] + [vmem] * (count + len(terms) + 4),
+        [smem] + [vmem] * (count + len(terms) + 3),
         (shape((1, width, cols), bf16), shape((1, cols), f32), shape((1, rows), f32)),
-        (main_memory, vmem, vmem),
-        table_scratch(count, cols),
+        (main_memory,) * 3,
+        table_scratch(count, cols)
+        + [pltpu.VMEM((1, cols), f32), pltpu.VMEM((1, rows), f32), pltpu.SemaphoreType.DMA((2,))],
         count * rows * weight_block,
         count * weight_block,
-    )(place, *[first[k] for k in range(count)], *terms, trans, gain, scale, info)
+    )(place, *[first[k] for k in range(count)], *terms, factor, offset, info)
     return grad_weight, grad_bias, kl[0, :1]
 
 

time: 133 us -> 131 us (0.985)
    unnamed x8 -> x10, local copies, waits for them, and re-layouts: 2.02 us -> 2.71 us
  transfers between devices with their start and end apart: 53 -> 53, of which waited for: 22 -> 20; matrix products, arithmetic and copies ran while one was open for 0% -> 0% of each run, Pallas kernels for 10% -> 10%
where the time goes in v5:
time: 131 us
  starting transfers between devices  63.5 us (48%)
  waiting for transfers between devices  41.6 us (32%)
  Pallas kernels  21.8 us (17%)
  local copies, waits for them, and re-layouts  2.71 us (2%)
    ppermute x51, starting transfers between devices, swap(): return lax.ppermute(value, 'vocab', [(i, i ^ offset) for i in range(count)])  62.6 us
    ppermute x51, waiting for transfers between devices, swap(): return lax.ppermute(value, 'vocab', [(i, i ^ offset) for i in range(count)])  40.2 us
    pallas_call x2, Pallas kernels, fetch(): kernel_call(functools.partial(fetch_kernel, every, len(sources)), name, [...  6.94 us
    pallas_call x1, Pallas kernels, per_device(): kernel_call(functools.partial(weight_kernel, count, len(terms)), 'grad_we...  4.38 us
    unnamed x10, local copies, waits for them, and re-layouts  2.71 us
  transfers between devices with their start and end apart: 53, of which 20 were waited for; matrix products, arithmetic and copies ran while one was open for 0% of the time, Pallas kernels for 10%

profile of v5, /device:TPU:0, one launch (start us, length us, event | category | flops | bytes accessed | tf_op | source)
XLA Modules:
  0.0 131.0 jit_solution(3724790570535943165)
XLA Ops:
  4.3 2.8 %collective-permute-start.3 = (bf16[128,512]{1,0:T(8,128)(2,1)S(1)}, bf16[128,512]{1,0:T(8,128)(2,1)S(1)}, u32[]{:S(2)}, u32[]{:S(2)}) collective-permute-start(bf16[128,512]{1,0:T(8,128)(2,1)S(1)} %head.1.refs_0_.refs_9_), channel_id=1, source_target_pairs={{0,4},{1,5},{2,6},{3,7},{4,0},{5,1},{6,2},{7,3},{8,12},{9,13},{10,... | collective-permute-start | bytes 393224 | tf_op jit(solution)/shard_map/ppermute | solution.py:38
  7.1 1.5 %collective-permute-start = (bf16[128,512]{1,0:T(8,128)(2,1)S(1)}, bf16[128,512]{1,0:T(8,128)(2,1)S(1)}, u32[]{:S(2)}, u32[]{:S(2)}) collective-permute-start(bf16[128,512]{1,0:T(8,128)(2,1)S(1)} %head.1.refs_0_.refs_9_), channel_id=1, source_target_pairs={{0,1},{1,0},{2,3},{3,2},{4,5},{5,4},{6,7},{7,6},{8,9},{9,8},{10,11... | collective-permute-start | bytes 393224 | tf_op jit(solution)/shard_map/ppermute | solution.py:38
  8.6 1.5 %collective-permute-start.1 = (bf16[128,512]{1,0:T(8,128)(2,1)S(1)}, bf16[128,512]{1,0:T(8,128)(2,1)S(1)}, u32[]{:S(2)}, u32[]{:S(2)}) collective-permute-start(bf16[128,512]{1,0:T(8,128)(2,1)S(1)} %head.1.refs_0_.refs_9_), channel_id=1, source_target_pairs={{0,2},{1,3},{2,0},{3,1},{4,6},{5,7},{6,4},{7,5},{8,10},{9,11},{10,... | collective-permute-start | bytes 393224 | tf_op jit(solution)/shard_map/ppermute | solution.py:38
  10.1 2.6 %collective-permute-start.7 = (bf16[128,512]{1,0:T(8,128)(2,1)S(1)}, bf16[128,512]{1,0:T(8,128)(2,1)S(1)}, u32[]{:S(2)}, u32[]{:S(2)}) collective-permute-start(bf16[128,512]{1,0:T(8,128)(2,1)S(1)} %head.1.refs_0_.refs_9_), channel_id=1, source_target_pairs={{0,8},{1,9},{2,10},{3,11},{4,12},{5,13},{6,14},{7,15},{8,0},{9,1},... | collective-permute-start | bytes 393224 | tf_op jit(solution)/shard_map/ppermute | solution.py:38
  12.7 2.0 %copy-done = bf16[4096,512]{1,0:T(8,128)(2,1)} copy-done((bf16[4096,512]{1,0:T(8,128)(2,1)}, bf16[4096,512]{1,0:T(8,128)(2,1)S(1)}, u32[]{:S(2)}) %copy-start) | copy-done | bytes 4194328
  14.7 2.2 %collective-permute-start.13 = (bf16[128,512]{1,0:T(8,128)(2,1)S(1)}, bf16[128,512]{1,0:T(8,128)(2,1)S(1)}, u32[]{:S(2)}, u32[]{:S(2)}) collective-permute-start(bf16[128,512]{1,0:T(8,128)(2,1)S(1)} %head.1.refs_0_.refs_9_), channel_id=1, source_target_pairs={{0,12},{1,13},{2,14},{3,15},{4,8},{5,9},{6,10},{7,11},{8,4},{9,5},... | collective-permute-start | bytes 393224 | tf_op jit(solution)/shard_map/ppermute | solution.py:38
  16.9 1.5 %collective-permute-start.5 = (bf16[128,512]{1,0:T(8,128)(2,1)S(1)}, bf16[128,512]{1,0:T(8,128)(2,1)S(1)}, u32[]{:S(2)}, u32[]{:S(2)}) collective-permute-start(bf16[128,512]{1,0:T(8,128)(2,1)S(1)} %collective-permute-done.3.refs_4_), channel_id=1, source_target_pairs={{0,2},{1,3},{2,0},{3,1},{4,6},{5,7},{6,4},{7,5},{8,10},{9,11},{10,... | collective-permute-start | bytes 393224 | tf_op jit(solution)/shard_map/ppermute | solution.py:38
  18.4 1.5 %collective-permute-start.4 = (bf16[128,512]{1,0:T(8,128)(2,1)S(1)}, bf16[128,512]{1,0:T(8,128)(2,1)S(1)}, u32[]{:S(2)}, u32[]{:S(2)}) collective-permute-start(bf16[128,512]{1,0:T(8,128)(2,1)S(1)} %collective-permute-done.3.refs_4_), channel_id=1, source_target_pairs={{0,1},{1,0},{2,3},{3,2},{4,5},{5,4},{6,7},{7,6},{8,9},{9,8},{10,11... | collective-permute-start | bytes 393224 | tf_op jit(solution)/shard_map/ppermute | solution.py:38
  19.9 1.9 %collective-permute-done.7.refs_0_.refs_8_ = bf16[128,512]{1,0:T(8,128)(2,1)S(1)} collective-permute-done((bf16[128,512]{1,0:T(8,128)(2,1)S(1)}, bf16[128,512]{1,0:T(8,128)(2,1)S(1)}, u32[]{:S(2)}, u32[]{:S(2)}) %collective-permute-start.7) | collective-permute-done | bytes 131104 | tf_op jit(solution)/shard_map/ppermute | solution.py:38
  22.8 2.0 %collective-permute-start.15 = (bf16[128,512]{1,0:T(8,128)(2,1)S(1)}, bf16[128,512]{1,0:T(8,128)(2,1)S(1)}, u32[]{:S(2)}, u32[]{:S(2)}) collective-permute-start(bf16[128,512]{1,0:T(8,128)(2,1)S(1)} %collective-permute-done.13.refs_4_.refs_12_), channel_id=1, source_target_pairs={{0,2},{1,3},{2,0},{3,1},{4,6},{5,7},{6,4},{7,5},{8,10},{9,11},{10,... | collective-permute-start | bytes 393224 | tf_op jit(solution)/shard_map/ppermute | solution.py:38
  31.1 1.5 %collective-permute-start.16 = (bf16[128,512]{1,0:T(8,128)(2,1)S(1)}, bf16[128,512]{1,0:T(8,128)(2,1)S(1)}, u32[]{:S(2)}, u32[]{:S(2)}) collective-permute-start(bf16[128,512]{1,0:T(8,128)(2,1)S(1)} %collective-permute-done.15.refs_6_.refs_14_), channel_id=1, source_target_pairs={{0,1},{1,0},{2,3},{3,2},{4,5},{5,4},{6,7},{7,6},{8,9},{9,8},{10,11... | collective-permute-start | bytes 393224 | tf_op jit(solution)/shard_map/ppermute | solution.py:38
  32.7 4.1 %weight_blocks.1.refs_8_ = bf16[16,512,512]{2,1,0:T(8,128)(2,1)S(1)} custom-call(s32[2]{0:T(128)S(1)} %pad_add_fusion.place, bf16[8192,512]{1,0:T(8,128)(2,1)} %bitcast.10), custom_call_target="tpu_custom_call" | custom-call | bytes 16777216 | tf_op jit(solution)/shard_map/weight_blocks/pallas_call | solution.py:378
  39.6 1.5 %collective-permute-start.26 = (bf16[264,512]{1,0:T(8,128)(2,1)S(1)}, bf16[264,512]{1,0:T(8,128)(2,1)S(1)}, u32[]{:S(2)}, u32[]{:S(2)}) collective-permute-start(bf16[264,512]{1,0:T(8,128)(2,1)S(1)} %get-tuple-element.48.refs_0_), channel_id=1, source_target_pairs={{0,2},{1,3},{2,0},{3,1},{4,6},{5,7},{6,4},{7,5},{8,10},{9,11},{10,... | collective-permute-start | bytes 811016 | tf_op jit(solution)/shard_map/ppermute | solution.py:38
  43.6 6.1 %collective-permute-done.28.refs_4_ = bf16[264,512]{1,0:T(8,128)(2,1)S(1)} collective-permute-done((bf16[264,512]{1,0:T(8,128)(2,1)S(1)}, bf16[264,512]{1,0:T(8,128)(2,1)S(1)}, u32[]{:S(2)}, u32[]{:S(2)}) %collective-permute-start.28) | collective-permute-done | bytes 270368 | tf_op jit(solution)/shard_map/ppermute | solution.py:38
  49.6 2.0 %collective-permute-start.27 = (bf16[264,512]{1,0:T(8,128)(2,1)S(1)}, bf16[264,512]{1,0:T(8,128)(2,1)S(1)}, u32[]{:S(2)}, u32[]{:S(2)}) collective-permute-start(bf16[264,512]{1,0:T(8,128)(2,1)S(1)} %collective-permute-done.25.refs_1_), channel_id=1, source_target_pairs={{0,2},{1,3},{2,0},{3,1},{4,6},{5,7},{6,4},{7,5},{8,10},{9,11},{10,... | collective-permute-start | bytes 811016 | tf_op jit(solution)/shard_map/ppermute | solution.py:38
  51.6 8.6 %collective-permute-done.17.refs_0_ = bf16[264,512]{1,0:T(8,128)(2,1)S(1)} collective-permute-done((bf16[264,512]{1,0:T(8,128)(2,1)S(1)}, bf16[264,512]{1,0:T(8,128)(2,1)S(1)}, u32[]{:S(2)}, u32[]{:S(2)}) %collective-permute-start.17) | collective-permute-done | bytes 270368 | tf_op jit(solution)/shard_map/ppermute | solution.py:38
  60.3 1.6 %collective-permute-start.18 = (bf16[264,512]{1,0:T(8,128)(2,1)S(1)}, bf16[264,512]{1,0:T(8,128)(2,1)S(1)}, u32[]{:S(2)}, u32[]{:S(2)}) collective-permute-start(bf16[264,512]{1,0:T(8,128)(2,1)S(1)} %collective-permute-done.17.refs_0_), channel_id=1, source_target_pairs={{0,1},{1,0},{2,3},{3,2},{4,5},{5,4},{6,7},{7,6},{8,9},{9,8},{10,11... | collective-permute-start | bytes 811016 | tf_op jit(solution)/shard_map/ppermute | solution.py:38
  63.9 2.9 %unembed_blocks.1.refs_8_.blocks = bf16[16,512,512]{2,1,0:T(8,128)(2,1)S(1)} custom-call(s32[2]{0:T(128)S(1)} %pad_add_fusion.place, bf16[4096,512]{1,0:T(8,128)(2,1)} %refs_0_.3, bf16[4096,512]{1,0:T(8,128)(2,1)S(1)} %copy-done.1), custom_call_target="tpu_custom_call" | custom-call | bytes 16777216 | tf_op jit(solution)/shard_map/unembed_blocks/pallas_call | solution.py:378
  67.3 1.6 %collective-permute-start.22 = (bf16[264,512]{1,0:T(8,128)(2,1)S(1)}, bf16[264,512]{1,0:T(8,128)(2,1)S(1)}, u32[]{:S(2)}, u32[]{:S(2)}) collective-permute-start(bf16[264,512]{1,0:T(8,128)(2,1)S(1)} %collective-permute-done.21.refs_4_), channel_id=1, source_target_pairs={{0,1},{1,0},{2,3},{3,2},{4,5},{5,4},{6,7},{7,6},{8,9},{9,8},{10,11... | collective-permute-start | bytes 811016 | tf_op jit(solution)/shard_map/ppermute | solution.py:38
  72.2 3.3 %collective-permute-done.31.refs_7_ = bf16[264,512]{1,0:T(8,128)(2,1)S(1)} collective-permute-done((bf16[264,512]{1,0:T(8,128)(2,1)S(1)}, bf16[264,512]{1,0:T(8,128)(2,1)S(1)}, u32[]{:S(2)}, u32[]{:S(2)}) %collective-permute-start.31) | collective-permute-done | bytes 270368 | tf_op jit(solution)/shard_map/ppermute | solution.py:38
  77.0 3.8 %collective-permute-done.22.refs_5_ = bf16[264,512]{1,0:T(8,128)(2,1)S(1)} collective-permute-done((bf16[264,512]{1,0:T(8,128)(2,1)S(1)}, bf16[264,512]{1,0:T(8,128)(2,1)S(1)}, u32[]{:S(2)}, u32[]{:S(2)}) %collective-permute-start.22) | collective-permute-done | bytes 270368 | tf_op jit(solution)/shard_map/ppermute | solution.py:38
  80.8 2.9 %collective-permute-done.24.refs_7_ = bf16[264,512]{1,0:T(8,128)(2,1)S(1)} collective-permute-done((bf16[264,512]{1,0:T(8,128)(2,1)S(1)}, bf16[264,512]{1,0:T(8,128)(2,1)S(1)}, u32[]{:S(2)}, u32[]{:S(2)}) %collective-permute-start.24) | collective-permute-done | bytes 270368 | tf_op jit(solution)/shard_map/ppermute | solution.py:38
  83.7 1.5 %logits_late.1 = (f32[128,512]{1,0:T(8,128)S(1)}, f32[128,512]{1,0:T(8,128)S(1)}, f32[8,128]{1,0:T(8,128)S(1)}, f32[8,128]{1,0:T(8,128)S(1)}) custom-call(bf16[264,512]{1,0:T(8,128)(2,1)S(1)} %collective-permute-done.17.refs_0_, bf16[264,512]{1,0:T(8,128)(2,1)S(1)} %collective-permute-done.18.refs_1_, bf16[264,512]{1,0:T(8,128)(2,1)S(1)} %collective-permute-done.19.refs_2_, ...), custom_call_target="tpu_custom_call" | custom-call | flops 1107296256 | bytes 4194304 | tf_op jit(solution)/shard_map/logits_late/pallas_call | solution.py:428
  86.6 3.1 %collective-permute-start.34 = (f32[8,128]{1,0:T(8,128)S(1)}, f32[8,128]{1,0:T(8,128)S(1)}, u32[]{:S(2)}, u32[]{:S(2)}) collective-permute-start(f32[8,128]{1,0:T(8,128)S(1)} %get-tuple-element.55), channel_id=1, source_target_pairs={{0,12},{1,13},{2,14},{3,15},{4,8},{5,9},{6,10},{7,11},{8,4},{9,5},... | collective-permute-start | bytes 12296 | tf_op jit(solution)/shard_map/ppermute | solution.py:38
  90.4 1.6 %collective-permute-done.34 = f32[8,128]{1,0:T(8,128)S(1)} collective-permute-done((f32[8,128]{1,0:T(8,128)S(1)}, f32[8,128]{1,0:T(8,128)S(1)}, u32[]{:S(2)}, u32[]{:S(2)}) %collective-permute-start.34) | collective-permute-done | bytes 4128 | tf_op jit(solution)/shard_map/ppermute | solution.py:38
  93.9 1.6 %collective-permute-start.37 = (f32[4,8,128]{2,1,0:T(8,128)S(1)}, f32[4,8,128]{2,1,0:T(8,128)S(1)}, u32[]{:S(2)}, u32[]{:S(2)}) collective-permute-start(f32[4,8,128]{2,1,0:T(8,128)S(1)} %pad_maximum_fusion.refs_0_), channel_id=1, source_target_pairs={{0,3},{1,2},{2,1},{3,0},{4,7},{5,6},{6,5},{7,4},{8,11},{9,10},{10,... | collective-permute-start | bytes 49160 | tf_op jit(solution)/shard_map/ppermute | solution.py:38
  96.9 1.8 %collective-permute-done.37.refs_3_ = f32[4,8,128]{2,1,0:T(8,128)S(1)} collective-permute-done((f32[4,8,128]{2,1,0:T(8,128)S(1)}, f32[4,8,128]{2,1,0:T(8,128)S(1)}, u32[]{:S(2)}, u32[]{:S(2)}) %collective-permute-start.37) | collective-permute-done | bytes 16416 | tf_op jit(solution)/shard_map/ppermute | solution.py:38
  102.9 1.4 %collective-permute-start.38 = (bf16[128,512]{1,0:T(8,128)(2,1)S(1)}, bf16[128,512]{1,0:T(8,128)(2,1)S(1)}, u32[]{:S(2)}, u32[]{:S(2)}) collective-permute-start(bf16[128,512]{1,0:T(8,128)(2,1)S(1)} %get-tuple-element.58), channel_id=1, source_target_pairs={{0,3},{1,2},{2,1},{3,0},{4,7},{5,6},{6,5},{7,4},{8,11},{9,10},{10,... | collective-permute-start | bytes 393224 | tf_op jit(solution)/shard_map/ppermute | solution.py:38
  115.0 3.2 %collective-permute-start.41 = (bf16[128,512]{1,0:T(8,128)(2,1)S(1)}, bf16[128,512]{1,0:T(8,128)(2,1)S(1)}, u32[]{:S(2)}, u32[]{:S(2)}) collective-permute-start(bf16[128,512]{1,0:T(8,128)(2,1)S(1)} %add_convert_fusion.5), channel_id=1, source_target_pairs={{0,12},{1,13},{2,14},{3,15},{4,8},{5,9},{6,10},{7,11},{8,4},{9,5},... | collective-permute-start | bytes 393224 | tf_op jit(solution)/shard_map/ppermute | solution.py:38
  120.2 2.1 %collective-permute-start.45 = (bf16[128,512]{1,0:T(8,128)(2,1)S(1)}, bf16[128,512]{1,0:T(8,128)(2,1)S(1)}, u32[]{:S(2)}, u32[]{:S(2)}) collective-permute-start(bf16[128,512]{1,0:T(8,128)(2,1)S(1)} %add_convert_fusion.3), channel_id=1, source_target_pairs={{0,8},{1,9},{2,10},{3,11},{4,12},{5,13},{6,14},{7,15},{8,0},{9,1},... | collective-permute-start | bytes 393224 | tf_op jit(solution)/shard_map/ppermute | solution.py:38
  123.7 2.8 %collective-permute-done.49.refs_18_ = bf16[128,512]{1,0:T(8,128)(2,1)S(1)} collective-permute-done((bf16[128,512]{1,0:T(8,128)(2,1)S(1)}, bf16[128,512]{1,0:T(8,128)(2,1)S(1)}, u32[]{:S(2)}, u32[]{:S(2)}) %collective-permute-start.49) | collective-permute-done | bytes 131104 | tf_op jit(solution)/shard_map/ppermute | solution.py:38
  126.5 4.4 %grad_weight.1 = (bf16[1,8192,512]{2,1,0:T(8,128)(2,1)}, f32[1,512]{1,0:T(1,128)}, f32[1,128]{1,0:T(1,128)}) custom-call(s32[2]{0:T(128)S(1)} %pad_add_fusion.place, bf16[128,512]{1,0:T(8,128)(2,1)S(1)} %head.1.refs_0_.refs_9_, bf16[128,512]{1,0:T(8,128)(2,1)S(1)} %collective-permute-done.refs_1_, bf16[128,512]{1,0:T(8,128)(2,1)S(1)} %collective-permute-done.1.refs_2_, ...), custom_call_target="tpu_custom_call" | custom-call | flops 1073741824 | bytes 8388608 | tf_op jit(solution)/shard_map/grad_weight/pallas_call | solution.py:484
  (104 shorter events, 46.9 us)
Async XLA Ops:
  2.5 10.2 %collective-permute-start.12 = (bf16[4096,512]{1,0:T(8,128)(2,1)}, bf16[4096,512]{1,0:T(8,128)(2,1)S(1)}, u32[]{:S(2)}, u32[]{:S(2)}) collective-permute-start(bf16[4096,512]{1,0:T(8,128)(2,1)} %refs_0_.3), channel_id=1, source_target_pairs={{16,0},{0,16},{17,1},{1,17},{18,2},{2,18},{19,3},{3,19},{20,4},{4,... | collective-permute-start | bytes 12582920 | tf_op jit(solution)/shard_map/ppermute | solution.py:346
  4.3 12.6 %collective-permute-start.3 = (bf16[128,512]{1,0:T(8,128)(2,1)S(1)}, bf16[128,512]{1,0:T(8,128)(2,1)S(1)}, u32[]{:S(2)}, u32[]{:S(2)}) collective-permute-start(bf16[128,512]{1,0:T(8,128)(2,1)S(1)} %head.1.refs_0_.refs_9_), channel_id=1, source_target_pairs={{0,4},{1,5},{2,6},{3,7},{4,0},{5,1},{6,2},{7,3},{8,12},{9,13},{10,... | collective-permute-start | bytes 393224 | tf_op jit(solution)/shard_map/ppermute | solution.py:38
  7.1 11.3 %collective-permute-start = (bf16[128,512]{1,0:T(8,128)(2,1)S(1)}, bf16[128,512]{1,0:T(8,128)(2,1)S(1)}, u32[]{:S(2)}, u32[]{:S(2)}) collective-permute-start(bf16[128,512]{1,0:T(8,128)(2,1)S(1)} %head.1.refs_0_.refs_9_), channel_id=1, source_target_pairs={{0,1},{1,0},{2,3},{3,2},{4,5},{5,4},{6,7},{7,6},{8,9},{9,8},{10,11... | collective-permute-start | bytes 393224 | tf_op jit(solution)/shard_map/ppermute | solution.py:38
  8.6 14.2 %collective-permute-start.1 = (bf16[128,512]{1,0:T(8,128)(2,1)S(1)}, bf16[128,512]{1,0:T(8,128)(2,1)S(1)}, u32[]{:S(2)}, u32[]{:S(2)}) collective-permute-start(bf16[128,512]{1,0:T(8,128)(2,1)S(1)} %head.1.refs_0_.refs_9_), channel_id=1, source_target_pairs={{0,2},{1,3},{2,0},{3,1},{4,6},{5,7},{6,4},{7,5},{8,10},{9,11},{10,... | collective-permute-start | bytes 393224 | tf_op jit(solution)/shard_map/ppermute | solution.py:38
  10.1 11.7 %collective-permute-start.7 = (bf16[128,512]{1,0:T(8,128)(2,1)S(1)}, bf16[128,512]{1,0:T(8,128)(2,1)S(1)}, u32[]{:S(2)}, u32[]{:S(2)}) collective-permute-start(bf16[128,512]{1,0:T(8,128)(2,1)S(1)} %head.1.refs_0_.refs_9_), channel_id=1, source_target_pairs={{0,8},{1,9},{2,10},{3,11},{4,12},{5,13},{6,14},{7,15},{8,0},{9,1},... | collective-permute-start | bytes 393224 | tf_op jit(solution)/shard_map/ppermute | solution.py:38
  14.7 8.1 %collective-permute-start.13 = (bf16[128,512]{1,0:T(8,128)(2,1)S(1)}, bf16[128,512]{1,0:T(8,128)(2,1)S(1)}, u32[]{:S(2)}, u32[]{:S(2)}) collective-permute-start(bf16[128,512]{1,0:T(8,128)(2,1)S(1)} %head.1.refs_0_.refs_9_), channel_id=1, source_target_pairs={{0,12},{1,13},{2,14},{3,15},{4,8},{5,9},{6,10},{7,11},{8,4},{9,5},... | collective-permute-start | bytes 393224 | tf_op jit(solution)/shard_map/ppermute | solution.py:38
  16.9 7.9 %collective-permute-start.5 = (bf16[128,512]{1,0:T(8,128)(2,1)S(1)}, bf16[128,512]{1,0:T(8,128)(2,1)S(1)}, u32[]{:S(2)}, u32[]{:S(2)}) collective-permute-start(bf16[128,512]{1,0:T(8,128)(2,1)S(1)} %collective-permute-done.3.refs_4_), channel_id=1, source_target_pairs={{0,2},{1,3},{2,0},{3,1},{4,6},{5,7},{6,4},{7,5},{8,10},{9,11},{10,... | collective-permute-start | bytes 393224 | tf_op jit(solution)/shard_map/ppermute | solution.py:38
  18.4 9.7 %collective-permute-start.4 = (bf16[128,512]{1,0:T(8,128)(2,1)S(1)}, bf16[128,512]{1,0:T(8,128)(2,1)S(1)}, u32[]{:S(2)}, u32[]{:S(2)}) collective-permute-start(bf16[128,512]{1,0:T(8,128)(2,1)S(1)} %collective-permute-done.3.refs_4_), channel_id=1, source_target_pairs={{0,1},{1,0},{2,3},{3,2},{4,5},{5,4},{6,7},{7,6},{8,9},{9,8},{10,11... | collective-permute-start | bytes 393224 | tf_op jit(solution)/shard_map/ppermute | solution.py:38
  22.8 7.4 %collective-permute-start.2 = (bf16[128,512]{1,0:T(8,128)(2,1)S(1)}, bf16[128,512]{1,0:T(8,128)(2,1)S(1)}, u32[]{:S(2)}, u32[]{:S(2)}) collective-permute-start(bf16[128,512]{1,0:T(8,128)(2,1)S(1)} %collective-permute-done.refs_1_), channel_id=1, source_target_pairs={{0,2},{1,3},{2,0},{3,1},{4,6},{5,7},{6,4},{7,5},{8,10},{9,11},{10,... | collective-permute-start | bytes 393224 | tf_op jit(solution)/shard_map/ppermute | solution.py:38
  22.8 8.4 %collective-permute-start.15 = (bf16[128,512]{1,0:T(8,128)(2,1)S(1)}, bf16[128,512]{1,0:T(8,128)(2,1)S(1)}, u32[]{:S(2)}, u32[]{:S(2)}) collective-permute-start(bf16[128,512]{1,0:T(8,128)(2,1)S(1)} %collective-permute-done.13.refs_4_.refs_12_), channel_id=1, source_target_pairs={{0,2},{1,3},{2,0},{3,1},{4,6},{5,7},{6,4},{7,5},{8,10},{9,11},{10,... | collective-permute-start | bytes 393224 | tf_op jit(solution)/shard_map/ppermute | solution.py:38
  24.8 12.0 %collective-permute-start.6 = (bf16[128,512]{1,0:T(8,128)(2,1)S(1)}, bf16[128,512]{1,0:T(8,128)(2,1)S(1)}, u32[]{:S(2)}, u32[]{:S(2)}) collective-permute-start(bf16[128,512]{1,0:T(8,128)(2,1)S(1)} %collective-permute-done.5.refs_6_), channel_id=1, source_target_pairs={{0,1},{1,0},{2,3},{3,2},{4,5},{5,4},{6,7},{7,6},{8,9},{9,8},{10,11... | collective-permute-start | bytes 393224 | tf_op jit(solution)/shard_map/ppermute | solution.py:38
  28.1 9.4 %collective-permute-start.10 = (bf16[128,512]{1,0:T(8,128)(2,1)S(1)}, bf16[128,512]{1,0:T(8,128)(2,1)S(1)}, u32[]{:S(2)}, u32[]{:S(2)}) collective-permute-start(bf16[128,512]{1,0:T(8,128)(2,1)S(1)} %collective-permute-done.7.refs_0_.refs_8_), channel_id=1, source_target_pairs={{0,2},{1,3},{2,0},{3,1},{4,6},{5,7},{6,4},{7,5},{8,10},{9,11},{10,... | collective-permute-start | bytes 393224 | tf_op jit(solution)/shard_map/ppermute | solution.py:38
  29.0 8.5 %collective-permute-start.11 = (bf16[128,512]{1,0:T(8,128)(2,1)S(1)}, bf16[128,512]{1,0:T(8,128)(2,1)S(1)}, u32[]{:S(2)}, u32[]{:S(2)}) collective-permute-start(bf16[128,512]{1,0:T(8,128)(2,1)S(1)} %collective-permute-done.8.refs_1_.refs_9_), channel_id=1, source_target_pairs={{0,2},{1,3},{2,0},{3,1},{4,6},{5,7},{6,4},{7,5},{8,10},{9,11},{10,... | collective-permute-start | bytes 393224 | tf_op jit(solution)/shard_map/ppermute | solution.py:38
  38.4 11.2 %collective-permute-start.28 = (bf16[264,512]{1,0:T(8,128)(2,1)S(1)}, bf16[264,512]{1,0:T(8,128)(2,1)S(1)}, u32[]{:S(2)}, u32[]{:S(2)}) collective-permute-start(bf16[264,512]{1,0:T(8,128)(2,1)S(1)} %get-tuple-element.48.refs_0_), channel_id=1, source_target_pairs={{0,4},{1,5},{2,6},{3,7},{4,0},{5,1},{6,2},{7,3},{8,12},{9,13},{10,... | collective-permute-start | bytes 811016 | tf_op jit(solution)/shard_map/ppermute | solution.py:38
  38.5 11.1 %collective-permute-start.25 = (bf16[264,512]{1,0:T(8,128)(2,1)S(1)}, bf16[264,512]{1,0:T(8,128)(2,1)S(1)}, u32[]{:S(2)}, u32[]{:S(2)}) collective-permute-start(bf16[264,512]{1,0:T(8,128)(2,1)S(1)} %get-tuple-element.48.refs_0_), channel_id=1, source_target_pairs={{0,1},{1,0},{2,3},{3,2},{4,5},{5,4},{6,7},{7,6},{8,9},{9,8},{10,11... | collective-permute-start | bytes 811016 | tf_op jit(solution)/shard_map/ppermute | solution.py:38
  39.6 12.1 %collective-permute-start.26 = (bf16[264,512]{1,0:T(8,128)(2,1)S(1)}, bf16[264,512]{1,0:T(8,128)(2,1)S(1)}, u32[]{:S(2)}, u32[]{:S(2)}) collective-permute-start(bf16[264,512]{1,0:T(8,128)(2,1)S(1)} %get-tuple-element.48.refs_0_), channel_id=1, source_target_pairs={{0,2},{1,3},{2,0},{3,1},{4,6},{5,7},{6,4},{7,5},{8,10},{9,11},{10,... | collective-permute-start | bytes 811016 | tf_op jit(solution)/shard_map/ppermute | solution.py:38
  41.1 19.2 %collective-permute-start.17 = (bf16[264,512]{1,0:T(8,128)(2,1)S(1)}, bf16[264,512]{1,0:T(8,128)(2,1)S(1)}, u32[]{:S(2)}, u32[]{:S(2)}) collective-permute-start(bf16[264,512]{1,0:T(8,128)(2,1)S(1)} %get-tuple-element.48.refs_0_), channel_id=1, source_target_pairs={{0,8},{1,9},{2,10},{3,11},{4,12},{5,13},{6,14},{7,15},{8,0},{9,1},... | collective-permute-start | bytes 811016 | tf_op jit(solution)/shard_map/ppermute | solution.py:38
  42.2 19.7 %collective-permute-start.21 = (bf16[264,512]{1,0:T(8,128)(2,1)S(1)}, bf16[264,512]{1,0:T(8,128)(2,1)S(1)}, u32[]{:S(2)}, u32[]{:S(2)}) collective-permute-start(bf16[264,512]{1,0:T(8,128)(2,1)S(1)} %get-tuple-element.48.refs_0_), channel_id=1, source_target_pairs={{0,12},{1,13},{2,14},{3,15},{4,8},{5,9},{6,10},{7,11},{8,4},{9,5},... | collective-permute-start | bytes 811016 | tf_op jit(solution)/shard_map/ppermute | solution.py:38
  49.6 13.4 %collective-permute-start.30 = (bf16[264,512]{1,0:T(8,128)(2,1)S(1)}, bf16[264,512]{1,0:T(8,128)(2,1)S(1)}, u32[]{:S(2)}, u32[]{:S(2)}) collective-permute-start(bf16[264,512]{1,0:T(8,128)(2,1)S(1)} %collective-permute-done.28.refs_4_), channel_id=1, source_target_pairs={{0,2},{1,3},{2,0},{3,1},{4,6},{5,7},{6,4},{7,5},{8,10},{9,11},{10,... | collective-permute-start | bytes 811016 | tf_op jit(solution)/shard_map/ppermute | solution.py:38
  49.6 17.2 %collective-permute-start.27 = (bf16[264,512]{1,0:T(8,128)(2,1)S(1)}, bf16[264,512]{1,0:T(8,128)(2,1)S(1)}, u32[]{:S(2)}, u32[]{:S(2)}) collective-permute-start(bf16[264,512]{1,0:T(8,128)(2,1)S(1)} %collective-permute-done.25.refs_1_), channel_id=1, source_target_pairs={{0,2},{1,3},{2,0},{3,1},{4,6},{5,7},{6,4},{7,5},{8,10},{9,11},{10,... | collective-permute-start | bytes 811016 | tf_op jit(solution)/shard_map/ppermute | solution.py:38
  51.6 15.7 %collective-permute-start.29 = (bf16[264,512]{1,0:T(8,128)(2,1)S(1)}, bf16[264,512]{1,0:T(8,128)(2,1)S(1)}, u32[]{:S(2)}, u32[]{:S(2)}) collective-permute-start(bf16[264,512]{1,0:T(8,128)(2,1)S(1)} %collective-permute-done.28.refs_4_), channel_id=1, source_target_pairs={{0,1},{1,0},{2,3},{3,2},{4,5},{5,4},{6,7},{7,6},{8,9},{9,8},{10,11... | collective-permute-start | bytes 811016 | tf_op jit(solution)/shard_map/ppermute | solution.py:38
  60.3 9.4 %collective-permute-start.18 = (bf16[264,512]{1,0:T(8,128)(2,1)S(1)}, bf16[264,512]{1,0:T(8,128)(2,1)S(1)}, u32[]{:S(2)}, u32[]{:S(2)}) collective-permute-start(bf16[264,512]{1,0:T(8,128)(2,1)S(1)} %collective-permute-done.17.refs_0_), channel_id=1, source_target_pairs={{0,1},{1,0},{2,3},{3,2},{4,5},{5,4},{6,7},{7,6},{8,9},{9,8},{10,11... | collective-permute-start | bytes 811016 | tf_op jit(solution)/shard_map/ppermute | solution.py:38
  61.9 9.4 %collective-permute-start.23 = (bf16[264,512]{1,0:T(8,128)(2,1)S(1)}, bf16[264,512]{1,0:T(8,128)(2,1)S(1)}, u32[]{:S(2)}, u32[]{:S(2)}) collective-permute-start(bf16[264,512]{1,0:T(8,128)(2,1)S(1)} %collective-permute-done.21.refs_4_), channel_id=1, source_target_pairs={{0,2},{1,3},{2,0},{3,1},{4,6},{5,7},{6,4},{7,5},{8,10},{9,11},{10,... | collective-permute-start | bytes 811016 | tf_op jit(solution)/shard_map/ppermute | solution.py:38
  63.0 12.5 %collective-permute-start.31 = (bf16[264,512]{1,0:T(8,128)(2,1)S(1)}, bf16[264,512]{1,0:T(8,128)(2,1)S(1)}, u32[]{:S(2)}, u32[]{:S(2)}) collective-permute-start(bf16[264,512]{1,0:T(8,128)(2,1)S(1)} %collective-permute-done.30.refs_6_), channel_id=1, source_target_pairs={{0,1},{1,0},{2,3},{3,2},{4,5},{5,4},{6,7},{7,6},{8,9},{9,8},{10,11... | collective-permute-start | bytes 811016 | tf_op jit(solution)/shard_map/ppermute | solution.py:38
  66.8 10.2 %collective-permute-start.19 = (bf16[264,512]{1,0:T(8,128)(2,1)S(1)}, bf16[264,512]{1,0:T(8,128)(2,1)S(1)}, u32[]{:S(2)}, u32[]{:S(2)}) collective-permute-start(bf16[264,512]{1,0:T(8,128)(2,1)S(1)} %collective-permute-done.17.refs_0_), channel_id=1, source_target_pairs={{0,2},{1,3},{2,0},{3,1},{4,6},{5,7},{6,4},{7,5},{8,10},{9,11},{10,... | collective-permute-start | bytes 811016 | tf_op jit(solution)/shard_map/ppermute | solution.py:38
  67.3 13.5 %collective-permute-start.22 = (bf16[264,512]{1,0:T(8,128)(2,1)S(1)}, bf16[264,512]{1,0:T(8,128)(2,1)S(1)}, u32[]{:S(2)}, u32[]{:S(2)}) collective-permute-start(bf16[264,512]{1,0:T(8,128)(2,1)S(1)} %collective-permute-done.21.refs_4_), channel_id=1, source_target_pairs={{0,1},{1,0},{2,3},{3,2},{4,5},{5,4},{6,7},{7,6},{8,9},{9,8},{10,11... | collective-permute-start | bytes 811016 | tf_op jit(solution)/shard_map/ppermute | solution.py:38
  69.7 11.1 %collective-permute-start.20 = (bf16[264,512]{1,0:T(8,128)(2,1)S(1)}, bf16[264,512]{1,0:T(8,128)(2,1)S(1)}, u32[]{:S(2)}, u32[]{:S(2)}) collective-permute-start(bf16[264,512]{1,0:T(8,128)(2,1)S(1)} %collective-permute-done.18.refs_1_), channel_id=1, source_target_pairs={{0,2},{1,3},{2,0},{3,1},{4,6},{5,7},{6,4},{7,5},{8,10},{9,11},{10,... | collective-permute-start | bytes 811016 | tf_op jit(solution)/shard_map/ppermute | solution.py:38
  71.3 12.4 %collective-permute-start.24 = (bf16[264,512]{1,0:T(8,128)(2,1)S(1)}, bf16[264,512]{1,0:T(8,128)(2,1)S(1)}, u32[]{:S(2)}, u32[]{:S(2)}) collective-permute-start(bf16[264,512]{1,0:T(8,128)(2,1)S(1)} %collective-permute-done.23.refs_6_), channel_id=1, source_target_pairs={{0,1},{1,0},{2,3},{3,2},{4,5},{5,4},{6,7},{7,6},{8,9},{9,8},{10,11... | collective-permute-start | bytes 811016 | tf_op jit(solution)/shard_map/ppermute | solution.py:38
  100.0 7.6 %collective-permute-start.42 = (bf16[128,512]{1,0:T(8,128)(2,1)S(1)}, bf16[128,512]{1,0:T(8,128)(2,1)S(1)}, u32[]{:S(2)}, u32[]{:S(2)}) collective-permute-start(bf16[128,512]{1,0:T(8,128)(2,1)S(1)} %get-tuple-element.63), channel_id=1, source_target_pairs={{0,2},{1,3},{2,0},{3,1},{4,6},{5,7},{6,4},{7,5},{8,10},{9,11},{10,... | collective-permute-start | bytes 393224 | tf_op jit(solution)/shard_map/ppermute | solution.py:38
  102.1 16.1 %collective-permute-start.44 = (bf16[128,512]{1,0:T(8,128)(2,1)S(1)}, bf16[128,512]{1,0:T(8,128)(2,1)S(1)}, u32[]{:S(2)}, u32[]{:S(2)}) collective-permute-start(bf16[128,512]{1,0:T(8,128)(2,1)S(1)} %get-tuple-element.64), channel_id=1, source_target_pairs={{0,2},{1,3},{2,0},{3,1},{4,6},{5,7},{6,4},{7,5},{8,10},{9,11},{10,... | collective-permute-start | bytes 393224 | tf_op jit(solution)/shard_map/ppermute | solution.py:38
  110.6 7.6 %collective-permute-start.43 = (bf16[128,512]{1,0:T(8,128)(2,1)S(1)}, bf16[128,512]{1,0:T(8,128)(2,1)S(1)}, u32[]{:S(2)}, u32[]{:S(2)}) collective-permute-start(bf16[128,512]{1,0:T(8,128)(2,1)S(1)} %add_convert_fusion.4), channel_id=1, source_target_pairs={{0,1},{1,0},{2,3},{3,2},{4,5},{5,4},{6,7},{7,6},{8,9},{9,8},{10,11... | collective-permute-start | bytes 393224 | tf_op jit(solution)/shard_map/ppermute | solution.py:38
  112.6 7.4 %collective-permute-start.46 = (bf16[128,512]{1,0:T(8,128)(2,1)S(1)}, bf16[128,512]{1,0:T(8,128)(2,1)S(1)}, u32[]{:S(2)}, u32[]{:S(2)}) collective-permute-start(bf16[128,512]{1,0:T(8,128)(2,1)S(1)} %get-tuple-element.70), channel_id=1, source_target_pairs={{0,1},{1,0},{2,3},{3,2},{4,5},{5,4},{6,7},{7,6},{8,9},{9,8},{10,11... | collective-permute-start | bytes 393224 | tf_op jit(solution)/shard_map/ppermute | solution.py:38
  (26 other events, 151.8 us)
